TPU v7x, 32 devices: a whole 2x2x4 slice. The times are simulated.
32 devices in a mesh: ctx: 8 (over z, x), tp: 4 (over y, core).
Axes of the slice: x: 2, y: 2, z: 4, core: 2. Of those that a mesh axis runs over, the one named last changes fastest.
Arguments:
- query: bfloat16 [4096, 4096], P('ctx', 'tp'), may hold values from -6 to 6
- key_in: bfloat16 [4096, 4096], P('ctx', 'tp'), may hold values from -6 to 6
- value: bfloat16 [4096, 4096], P('ctx', 'tp'), may hold values from -6 to 6
- rates: float32 [256, 16], P('tp'), as said below
- residues: float32 [256, 16], P('tp'), as said below
- skip_gain: float32 [4096], P('tp'), may hold values from 0.5 to 1.5
- out_weight: bfloat16 [4096, 4096], P('tp'), may hold values from -0.09375 to 0.09375
Outputs:
- layer_out: bfloat16 [4096, 4096], P('ctx', 'tp')
Inputs may be any that keep to these rules, and one draw needn't show every extreme that they name: `rates`: positive, at most 0.0625. `residues`: either sign.
All inputs are finite; a program needn't handle non-finite values.
Results may differ from a plain program's by a relative error of at most 0.0095.
Values may be sent and summed in bfloat16 or wider, within the bound.
No kernel may reach another device: no remote copies, remote signals or barrier semaphores. Data moves between devices by JAX's collectives and lax.ppermute only.
A program may use at most 128 MiB of HBM per device.

v0:
```python
import jax
import jax.numpy as jnp
from jax import lax
from jax.sharding import PartitionSpec as P

GROUP = 16
SUB = 128


def shards(query, key_in, value, rates, residues, skip_gain, out_weight):
    tok_rows, channels = query.shape
    groups_here = channels // GROUP
    sub_count = tok_rows // SUB
    product_bf = (key_in.astype(jnp.float32) * value.astype(jnp.float32)).astype(jnp.bfloat16)
    signal = product_bf.astype(jnp.float32).T
    positions = jnp.arange(SUB, dtype=jnp.float32)
    filter_local = jnp.sum(
        residues[:, :, None] * jnp.exp(-rates[:, :, None] * positions[None, None, :]), axis=1
    )
    lag_index = (
        jnp.arange(SUB, dtype=jnp.int32)[:, None] - jnp.arange(SUB, dtype=jnp.int32)[None, :]
    )
    toeplitz = jnp.where(
        lag_index[None] >= 0, jnp.take(filter_local, jnp.clip(lag_index, 0, SUB - 1), axis=1), 0.0
    )
    grouped = (
        signal.reshape(groups_here, GROUP, sub_count, SUB)
        .transpose(0, 3, 1, 2)
        .reshape(groups_here, SUB, GROUP * sub_count)
    )
    local = jnp.einsum("gts,gsn->gtn", toeplitz, grouped, precision=lax.Precision.HIGHEST)
    local = (
        local.reshape(groups_here, SUB, GROUP, sub_count)
        .transpose(0, 2, 3, 1)
        .reshape(channels, tok_rows)
    )
    rate_cols = jnp.repeat(rates, GROUP, axis=0).T
    residue_cols = jnp.repeat(residues, GROUP, axis=0).T
    decay_in = jnp.exp(-rate_cols[:, :, None] * (SUB - 1.0 - positions)[None, None, :])
    sub_sums = jnp.einsum(
        "mcs,cjs->mcj",
        decay_in,
        signal.reshape(channels, sub_count, SUB),
        precision=lax.Precision.HIGHEST,
    )
    sub_decay = jnp.exp(-rate_cols * SUB)
    inner = [jnp.zeros_like(rate_cols)]
    for index_sub in range(sub_count):
        inner.append(sub_decay * inner[-1] + sub_sums[:, :, index_sub])
    summary = inner[sub_count]
    block_index = lax.axis_index("ctx")
    piece = lax.all_gather(summary[None], "ctx", axis=0, tiled=True)
    count = piece.shape[0]
    distance = block_index - 1 - jnp.arange(count, dtype=jnp.int32)
    spans = (tok_rows * jnp.maximum(distance, 0)).astype(jnp.float32)
    weight = jnp.where(
        distance[:, None, None] >= 0, jnp.exp(-rate_cols[None] * spans[:, None, None]), 0.0
    )
    state = jnp.sum(weight * piece, axis=0)
    starts = [
        inner[index_sub] + jnp.exp(-rate_cols * (SUB * index_sub * 1.0)) * state
        for index_sub in range(sub_count)
    ]
    start_states = jnp.stack(starts, axis=2)
    decay_out = residue_cols[:, :, None] * jnp.exp(
        -rate_cols[:, :, None] * (positions + 1.0)[None, None, :]
    )
    past = jnp.einsum(
        "mct,mcj->cjt", decay_out, start_states, precision=lax.Precision.HIGHEST
    ).reshape(channels, tok_rows)
    conv = local + past
    mixed = (query.astype(jnp.float32).T * (conv + skip_gain[:, None] * signal)).astype(
        jnp.bfloat16
    )
    summed = lax.psum_scatter(
        lax.dot_general(
            out_weight, mixed, (((0,), (0,)), ((), ())), preferred_element_type=jnp.float32
        ),
        "tp",
        scatter_dimension=0,
        tiled=True,
    )
    return summed.T.astype(jnp.bfloat16)


def solution(mesh):
    in_specs = (
        P("ctx", "tp"),
        P("ctx", "tp"),
        P("ctx", "tp"),
        P("tp", None),
        P("tp", None),
        P("tp"),
        P("tp", None),
    )
    out_specs = P("ctx", "tp")
    return jax.shard_map(shards, mesh=mesh, in_specs=in_specs, out_specs=out_specs, check_vma=False)
```

profile of v0, /device:TPU:0, one launch (start us, length us, event | category | flops | bytes accessed | tf_op | source)
XLA Modules:
  0.0 233.6 jit_solution(13263783769568831602)
XLA Ops:
  6.5 0.0 copy-start.2
  6.5 0.0 reduce-scatter.2.cloned.1.call-start
  6.6 1.6 copy.92
  8.2 0.0 copy-done.2
  8.2 0.5 copy.93
  8.7 0.3 fusion.25
  9.0 0.0 copy-start.6
  9.0 1.1 reshape.111
  10.2 1.1 reshape.107
  11.4 0.0 copy-done.6
  11.4 0.1 copy.89
  11.5 0.2 broadcast_in_dim.62
  11.7 0.3 neg.22
  11.9 0.2 copy.94
  12.1 0.0 copy-start.3
  12.2 0.8 copy-done.3
  12.9 9.6 %fusion.4 = f32[1024,4,16]{2,1,0:T(4,128)} fusion(bf16[1024,4,128]{2,1,0:T(4,128)(2,1)} %reshape.111, f32[128]{0:T(128)S(1)} %iota_subtract_fusion.1, f32[16,1024]{0,1:T(8,128)S(1)} %copy.94), kind=kOutput, calls=%fused_computation.5 | convolution fusion | flops 102760448 | bytes 1376768 | tf_op jit(solution)/shard_map/mcs,cjs->mcj/dot_general | solution.py:40
  22.5 1.8 copy.95
  24.4 33.2 %all-gather = f32[128,1024]{1,0:T(8,128)S(1)} all-gather(f32[16,1024]{1,0:T(8,128)S(1)} %fusion.28), channel_id=2, replica_groups=mesh['ctx'=8,'tp'=4] {'ctx'}, dimensions={0}, use_global_device_ids=true | all-gather | bytes 589824 | tf_op jit(solution)/shard_map/all_gather | solution.py:52
  57.6 0.0 copy-start.5
  57.6 0.2 multiply_reduce_fusion
  57.8 0.1 add_bitcast_fusion.2
  57.9 1.7 copy.97
  59.6 0.0 copy-done.5
  59.6 0.1 copy.88
  59.7 0.3 multiply_reduce_fusion.1
  60.1 0.1 copy.90
  60.2 54.4 %gather_fusion = f32[16384,64]{1,0:T(8,128)} fusion(f32[64,128]{0,1:T(8,128)S(1)} %copy.90, s32[16384]{0:T(1024)S(1)} %fusion.27), kind=kCustom, calls=%fused_computation | custom fusion | bytes 8454144 | tf_op jit(solution)/shard_map/jit(_take)/gather | solution.py:24
  114.6 7.4 %copy.91 = f32[128,128,64]{1,0,2:T(8,128)} copy(f32[128,128,64]{2,1,0:T(8,128)} %bitcast.109) | data formatting | bytes 8388608 | tf_op jit(solution)/shard_map/jit(_take)/gather | solution.py:24
  121.9 1.5 copy.87
  123.5 0.0 copy-start
  123.5 0.0 copy-start.1
  123.5 12.3 %fusion = f32[1024,4,128]{2,1,0:T(4,128)S(1)} fusion(f32[16,1024,4]{0,2,1:T(4,128)} %copy.97, f32[128]{0:T(128)S(1)} %iota_add_fusion, f32[16,1024]{0,1:T(8,128)S(1)} %bitcast.118, f32[16,1024]{0,1:T(8,128)} %copy-done.3), kind=kOutput, calls=%fused_computation.1 | convolution fusion | flops 104857600 | bytes 2490880 | tf_op jit(solution)/shard_map/mct,mcj->cjt/dot_general | solution.py:68
  135.8 0.0 copy-done
  135.8 0.0 copy-done.1
  135.8 0.0 copy-start.4
  135.9 4.3 %fusion.7 = f32[64,128,64]{1,2,0:T(8,128)S(1)} fusion(bf16[64,128,64]{1,2,0:T(8,128)(2,1)S(1)} %bitcast.111, f32[128,128,64]{1,0,2:T(8,128)S(1)} %copy-done, pred[128,128]{1,0:T(8,128)(4,1)S(1)} %get-tuple-element.9, pred[128,128]{1,0:T(8,128)(4,1)S(1)} %get-tuple-element.10), kind=kOutput, calls=%fused_computation.9 | convolution fusion | flops 807403520 | bytes 7372800 | tf_op jit(solution)/shard_map/gts,gsn->gtn/dot_general | solution.py:31
  140.2 0.0 copy-done.4
  140.2 10.9 %convolution_bitcast_fusion = f32[4096,512]{0,1:T(8,128)} fusion(bf16[1024,4096]{1,0:T(8,128)(2,1)} %param.13, f32[128,8,4,128]{3,2,1,0:T(4,128)S(1)} %bitcast.112, f32[128,8,4,128]{3,2,1,0:T(4,128)S(1)} %bitcast.110, bf16[512,1024]{0,1:T(8,128)(2,1)S(1)} %copy.87, f32[1024]{0:T(1024)S(1)} %copy-done.4, bf16[512,1024]{0,1:T(8,128)(2,1)S(1)} %copy.93, ...), kind=kOutput, calls=%fused_computation.8 | convolution fusion | flops 4300734464 | bytes 24121344 | tf_op jit(solution)/shard_map/dot_general | solution.py:76
  151.1 0.0 reduce-scatter.2.cloned.1.call-update
  151.1 73.0 %reduce-scatter.2.cloned.1.call-done = f32[1024,512]{0,1:T(8,128)} async-done(((f32[4096,512]{0,1:T(8,128)}), f32[1024,512]{0,1:T(8,128)}) %reduce-scatter.2.cloned.1.call-update) | async-done | bytes 2097168 | tf_op jit(solution)/shard_map/reduce_scatter | solution.py:75
  224.1 2.7 %convert_bitcast_fusion = bf16[512,1024]{1,0:T(8,128)(2,1)} fusion(f32[1024,512]{0,1:T(8,128)} %reduce-scatter.2.cloned.1.call-done), kind=kLoop, calls=%fused_computation.27 | loop fusion | flops 524288 | bytes 3145728 | tf_op jit(solution)/shard_map/convert_element_type | solution.py:83
  (10 shorter events, 0.2 us)
Async XLA Ops:
  6.5 1.6 copy-start.2
  6.5 217.5 %reduce-scatter.2.cloned.1.call-start = ((), (), s32[]{:S(2)}) async-start(), calls=%async_computation.1 | async-start | bytes 10485760 | tf_op jit(solution)/shard_map/reduce_scatter | solution.py:75
  9.0 2.3 copy-start.6
  12.1 0.8 copy-start.3
  57.6 2.0 copy-start.5
  123.5 12.3 %copy-start = (f32[128,128,64]{1,0,2:T(8,128)S(1)}, f32[128,128,64]{1,0,2:T(8,128)}, u32[]{:S(2)}) copy-start(f32[128,128,64]{1,0,2:T(8,128)} %copy.91) | copy-start | bytes 12582916
  123.5 12.3 %copy-start.1 = (bf16[64,16,4,128]{3,2,1,0:T(4,128)(2,1)S(1)}, bf16[64,16,4,128]{3,2,1,0:T(4,128)(2,1)}, u32[]{:S(2)}) copy-start(bf16[64,16,4,128]{3,2,1,0:T(4,128)(2,1)} %reshape.107) | copy-start | bytes 3145732
  135.8 4.4 %copy-start.4 = (f32[1024]{0:T(1024)S(1)}, f32[1024]{0:T(1024)}, u32[]{:S(2)}) copy-start(f32[1024]{0:T(1024)} %param.12) | copy-start | bytes 12292
Sparse Core Ops, SparseCore 0:
  151.2 72.8 reduce-scatter.1
where the time goes:
time: 234 us
  waiting for transfers between devices  73 us (31%)
  local copies, waits for them, and re-layouts  72.9 us (31%)
  matrix products  37.1 us (16%)
  blocking collectives  33.2 us (14%)
  between operations  13.6 us (6%)
  other arithmetic  3.79 us (2%)
    reduce_scatter x1, waiting for transfers between devices, shards(): lax.psum_scatter(lax.dot_general(out_weight, mixed, (((0,), (0,)), ((), (...  73 us
    gather x2, local copies, waits for them, and re-layouts, shards(): jnp.take(filter_local, jnp.clip(lag_index, 0, SUB - 1), axis=1)  61.8 us
    all_gather x1, blocking collectives, shards(): piece = lax.all_gather(summary[None], 'ctx', axis=0, tiled=True)  33.2 us
    dot_general x1, matrix products, shards(): jnp.einsum('mct,mcj->cjt', decay_out, start_states, precision=lax.Precisi...  12.3 us
    dot_general x1, matrix products, shards(): lax.dot_general(out_weight, mixed, (((0,), (0,)), ((), ())), preferred_el...  10.9 us
    dot_general x1, matrix products, shards(): jnp.einsum('mcs,cjs->mcj', decay_in, signal.reshape(channels, sub_count,...  9.58 us
  transfers between devices with their start and end apart: 1, of which 1 were waited for; matrix products, arithmetic and copies ran while one was open for 0% of the time, Pallas kernels for 0%

commit v1 on v0

v1 whole, which is shorter than its diff:
```python
import jax
import jax.numpy as jnp
from jax import lax
from jax.experimental import pallas as pl
from jax.experimental.pallas import tpu as pltpu
from jax.sharding import PartitionSpec as P

GROUP = 16
LANES = 128
SUBS = 8
BLK = 256
SEG = 256
CHUNK = 128
F32, BF16 = jnp.float32, jnp.bfloat16


def split_bf16(x, parts):
    pieces = []
    for _ in range(parts):
        piece = x.astype(BF16)
        pieces.append(piece)
        x = x - piece.astype(F32)
    return pieces


def dot(a, b):
    return lax.dot_general(a, b, (((1,), (0,)), ((), ())), preferred_element_type=F32)


def group_mask(groups, modes, channels):
    shape = (groups, modes, channels)
    return lax.broadcasted_iota(jnp.int32, shape, 0) == (
        lax.broadcasted_iota(jnp.int32, shape, 2) // GROUP
    )


def column_of(table, modes):
    groups = table.shape[0]
    rows = groups * modes
    spread = jnp.broadcast_to(table[:, None, :], (groups, modes, modes)).reshape(rows, modes)
    pick = lax.broadcasted_iota(jnp.int32, (rows, modes), 1) == (
        lax.broadcasted_iota(jnp.int32, (rows, modes), 0) % modes
    )
    return jnp.sum(jnp.where(pick, spread, 0.0), axis=1, keepdims=True)


def summary_kernel(k_ref, v_ref, rates_ref, residues_ref, sum_ref, rate_ref, residue_ref, flat_ref):
    groups, modes = rates_ref.shape
    rows = groups * modes
    tokens, channels = k_ref.shape
    rate = column_of(rates_ref[...], modes)
    residue = column_of(residues_ref[...], modes)
    mask = group_mask(groups, modes, channels)

    def compact(dense):
        kept = jnp.where(mask, dense.reshape(groups, modes, channels), 0.0)
        return jnp.sum(kept, axis=0)

    def store(ref, table):
        for tile in range(channels // LANES):
            ref[tile * modes : (tile + 1) * modes, :] = table[:, tile * LANES : (tile + 1) * LANES]

    position = lax.broadcasted_iota(jnp.int32, (rows, SEG), 1).astype(F32)
    decay = split_bf16(jnp.exp(-rate * (SEG - 1.0 - position)), 3)
    carry = jnp.exp(-rate * float(SEG))
    dense = None
    for seg in range(tokens // SEG):
        part = slice(seg * SEG, (seg + 1) * SEG)
        u = (k_ref[part, :].astype(F32) * v_ref[part, :].astype(F32)).astype(BF16)
        here = dot(decay[2], u) + dot(decay[1], u) + dot(decay[0], u)
        dense = here if dense is None else dense * carry + here
    store(sum_ref, compact(dense))
    wide = jnp.broadcast_to(rate, (rows, channels))
    store(rate_ref, compact(wide))
    store(residue_ref, compact(jnp.broadcast_to(residue, (rows, channels))))
    diagonal = lax.broadcasted_iota(jnp.int32, (rows, rows), 0) == lax.broadcasted_iota(
        jnp.int32, (rows, rows), 1
    )
    flat_ref[...] = jnp.sum(
        jnp.where(diagonal, jnp.broadcast_to(rate, (rows, rows)), 0.0), axis=0, keepdims=True
    )


def summary_call(key_in, value, rates, residues):
    tokens, channels = key_in.shape
    modes = rates.shape[1]
    groups = BLK // GROUP
    tiles = BLK // LANES
    table = jax.ShapeDtypeStruct((channels // LANES * modes, LANES), F32)
    table_spec = pl.BlockSpec((tiles * modes, LANES), lambda b: (b, 0))
    return pl.pallas_call(
        summary_kernel,
        grid=(channels // BLK,),
        in_specs=[
            pl.BlockSpec((tokens, BLK), lambda b: (0, b)),
            pl.BlockSpec((tokens, BLK), lambda b: (0, b)),
            pl.BlockSpec((groups, modes), lambda b: (b, 0)),
            pl.BlockSpec((groups, modes), lambda b: (b, 0)),
        ],
        out_specs=[
            table_spec,
            table_spec,
            table_spec,
            pl.BlockSpec((1, groups * modes), lambda b: (0, b)),
        ],
        out_shape=[table, table, table, jax.ShapeDtypeStruct((1, channels // GROUP * modes), F32)],
        compiler_params=pltpu.CompilerParams(vmem_limit_bytes=16 << 20),
        cost_estimate=pl.CostEstimate(
            flops=2 * 3 * tokens * BLK * channels, bytes_accessed=4 * tokens * channels, transcendentals=0
        ),
        name="block_summary",
    )(key_in, value, rates, residues)


def local_kernel(modes, k_ref, v_ref, rate_ref, residue_ref, skip_ref, out_ref, u_ref, state_ref):
    tokens, channels = k_ref.shape
    tiles = channels // LANES

    @pl.when(pl.program_id(0) == 0)
    def _():
        state_ref[...] = jnp.zeros_like(state_ref)

    for tile in range(tiles):
        lanes = slice(tile * LANES, (tile + 1) * LANES)
        u = (k_ref[:, lanes].astype(F32) * v_ref[:, lanes].astype(F32)).astype(BF16)
        u_ref[tile * tokens : (tile + 1) * tokens, :] = u.astype(F32)
    decay = [jnp.exp(-rate_ref[pl.ds(m, tiles, stride=modes), :]) for m in range(modes)]
    residue = [residue_ref[pl.ds(m, tiles, stride=modes), :] for m in range(modes)]
    skip = skip_ref[...]

    def step(t, states):
        u = u_ref[pl.ds(t, tiles, stride=tokens), :]
        states = tuple(d * s + u for d, s in zip(decay, states))
        terms = [skip * u] + [r * s for r, s in zip(residue, states)]
        while len(terms) > 1:
            terms = [a + b for a, b in zip(terms[::2], terms[1::2])] + (
                [terms[-1]] if len(terms) % 2 else []
            )
        out_ref[pl.ds(t, tiles, stride=tokens), :] = terms[0]
        return states

    first = tuple(state_ref[m * tiles : (m + 1) * tiles, :] for m in range(modes))
    last = lax.fori_loop(0, tokens, step, first, unroll=4)
    for m in range(modes):
        state_ref[m * tiles : (m + 1) * tiles, :] = last[m]


def local_call(key_in, value, rate_table, residue_table, skip_tiles, modes):
    tokens, channels = key_in.shape
    tiles = channels // LANES
    whole = lambda j: (0, 0)
    return pl.pallas_call(
        lambda *refs: local_kernel(modes, *refs),
        grid=(tokens // CHUNK,),
        in_specs=[
            pl.BlockSpec((CHUNK, channels), lambda j: (j, 0)),
            pl.BlockSpec((CHUNK, channels), lambda j: (j, 0)),
            pl.BlockSpec(rate_table.shape, whole),
            pl.BlockSpec(residue_table.shape, whole),
            pl.BlockSpec(skip_tiles.shape, whole),
        ],
        out_specs=pl.BlockSpec((tiles * CHUNK, LANES), lambda j: (j, 0)),
        out_shape=jax.ShapeDtypeStruct((tokens * tiles, LANES), F32),
        scratch_shapes=[
            pltpu.VMEM((tiles * CHUNK, LANES), F32),
            pltpu.VMEM((modes * tiles, LANES), F32),
        ],
        compiler_params=pltpu.CompilerParams(vmem_limit_bytes=16 << 20),
        cost_estimate=pl.CostEstimate(
            flops=4 * modes * tokens * channels, bytes_accessed=8 * tokens * channels, transcendentals=0
        ),
        name="local_conv",
    )(key_in, value, rate_table, residue_table, skip_tiles)


def mix_kernel(first, modes, q_ref, local_ref, state_ref, residue_ref, flat_ref, out_ref):
    tokens, channels = q_ref.shape
    tiles = channels // LANES
    groups = channels // GROUP
    rows = groups * modes
    weighted = state_ref[...] * residue_ref[...]
    weighted = jnp.concatenate([weighted[i * modes : (i + 1) * modes] for i in range(tiles)], axis=1)
    spread = jnp.broadcast_to(weighted[None], (groups, modes, channels))
    spread = jnp.where(group_mask(groups, modes, channels), spread, 0.0).reshape(rows, channels)
    since = lax.broadcasted_iota(jnp.int32, (tokens, rows), 0).astype(F32) + (first + 1.0)
    decay_hi, decay_lo = split_bf16(jnp.exp(-flat_ref[...] * since), 2)
    state_hi, state_lo = split_bf16(spread, 2)
    past = dot(decay_lo, state_hi) + dot(decay_hi, state_lo) + dot(decay_hi, state_hi)
    for tile in range(tiles):
        lanes = slice(tile * LANES, (tile + 1) * LANES)
        conv = local_ref[tile * tokens : (tile + 1) * tokens, :] + past[:, lanes]
        out_ref[:, lanes] = (q_ref[:, lanes].astype(F32) * conv).astype(BF16)


def mix_call(chunk, query, local, state, residue_table, flat_rates, modes):
    channels = query.shape[1]
    blocks = channels // BLK
    tiles = BLK // LANES
    table_spec = pl.BlockSpec((tiles * modes, LANES), lambda b: (b, 0))
    return pl.pallas_call(
        lambda *refs: mix_kernel(chunk * CHUNK, modes, *refs),
        grid=(blocks,),
        in_specs=[
            pl.BlockSpec((CHUNK, BLK), lambda b: (chunk, b)),
            pl.BlockSpec((tiles * CHUNK, LANES), lambda b: (chunk * blocks + b, 0)),
            table_spec,
            table_spec,
            pl.BlockSpec((1, BLK // GROUP * modes), lambda b: (0, b)),
        ],
        out_specs=pl.BlockSpec((CHUNK, BLK), lambda b: (0, b)),
        out_shape=jax.ShapeDtypeStruct((CHUNK, channels), BF16),
        compiler_params=pltpu.CompilerParams(vmem_limit_bytes=16 << 20),
        cost_estimate=pl.CostEstimate(
            flops=2 * 3 * CHUNK * BLK * channels, bytes_accessed=8 * CHUNK * channels, transcendentals=0
        ),
        name="mix",
    )(query, local, state, residue_table, flat_rates)


def project_kernel(at_ref, own_ref, pair_ref, own_w_ref, pair_w_ref, out_ref):
    total = dot(own_ref[...], own_w_ref[...]) + dot(pair_ref[...], pair_w_ref[...])
    out_ref[...] = total.astype(out_ref.dtype)


def project_call(at, mixed, mixed_pair, weight, weight_pair, out_dtype):
    tokens, depth = mixed.shape
    width = weight_pair.shape[1]
    cols = 256
    steps = width // cols
    return pl.pallas_call(
        project_kernel,
        grid_spec=pltpu.PrefetchScalarGridSpec(
            num_scalar_prefetch=1,
            grid=(steps,),
            in_specs=[
                pl.BlockSpec((tokens, depth), lambda n, at: (0, 0)),
                pl.BlockSpec((tokens, depth), lambda n, at: (0, 0)),
                pl.BlockSpec((depth, cols), lambda n, at: (0, at[0] * steps + n)),
                pl.BlockSpec((depth, cols), lambda n, at: (0, n)),
            ],
            out_specs=pl.BlockSpec((tokens, cols), lambda n, at: (0, n)),
        ),
        out_shape=jax.ShapeDtypeStruct((tokens, width), out_dtype),
        compiler_params=pltpu.CompilerParams(vmem_limit_bytes=24 << 20),
        cost_estimate=pl.CostEstimate(
            flops=4 * tokens * depth * width,
            bytes_accessed=4 * depth * width + 4 * tokens * width,
            transcendentals=0,
        ),
        name="project",
    )(at, mixed, mixed_pair, weight, weight_pair)


def start_state(summary, rate_table, block_rows, count):
    radix = 8

    def earlier(x, distance):
        return lax.ppermute(x, "ctx", [(i, i + distance) for i in range(count - distance)])

    def decayed(blocks):
        return jnp.exp(-rate_table * float(block_rows * blocks))

    total = jnp.zeros_like(summary)
    for distance in range(1, min(radix, count - 1) + 1):
        total = total + decayed(distance - 1) * earlier(summary, distance)
    span = radix
    while span < count - 1:
        base = total
        for step in range(1, radix):
            if step * span < count - 1:
                total = total + decayed(step * span) * earlier(base, step * span)
        span *= radix
    return total


def shards(query, key_in, value, rates, residues, skip_gain, out_weight, *, n_ctx, n_tp):
    tokens, channels = query.shape
    modes = rates.shape[1]
    width = out_weight.shape[1] // n_tp
    me = lax.axis_index("tp")

    def swap(x, bit):
        return lax.ppermute(x, "tp", [(i, i ^ bit) for i in range(n_tp)])

    def part_of_weight(at):
        return lax.dynamic_slice(out_weight, (0, at * width), (channels, width))

    summary, rate_table, residue_table, flat_rates = summary_call(key_in, value, rates, residues)
    pair_far = swap(part_of_weight(me ^ 3), 1)
    pair_near = swap(part_of_weight(me ^ 1), 1)
    state = start_state(summary, rate_table, tokens, n_ctx)
    skip_tiles = skip_gain.reshape(channels // LANES, LANES)
    local = local_call(key_in, value, rate_table, residue_table, skip_tiles, modes)

    far = (me ^ 2).reshape(1).astype(jnp.int32)
    near = me.reshape(1).astype(jnp.int32)
    mixed, mixed_pair, arrived = [], [], []
    for chunk in range(tokens // CHUNK):
        own = mix_call(chunk, query, local, state, residue_table, flat_rates, modes)
        other = swap(own, 1)
        partial = project_call(far, own, other, out_weight, pair_far, BF16)
        arrived.append(swap(partial, 2))
        mixed.append(own)
        mixed_pair.append(other)
    own_sum = project_call(
        near,
        jnp.concatenate(mixed, axis=0),
        jnp.concatenate(mixed_pair, axis=0),
        out_weight,
        pair_near,
        F32,
    )
    return (own_sum + jnp.concatenate(arrived, axis=0).astype(F32)).astype(BF16)


def solution(mesh):
    n_ctx, n_tp = mesh.shape["ctx"], mesh.shape["tp"]
    in_specs = (
        P("ctx", "tp"),
        P("ctx", "tp"),
        P("ctx", "tp"),
        P("tp", None),
        P("tp", None),
        P("tp"),
        P("tp", None),
    )

    def body(*args):
        return shards(*args, n_ctx=n_ctx, n_tp=n_tp)

    return jax.shard_map(body, mesh=mesh, in_specs=in_specs, out_specs=P("ctx", "tp"), check_vma=False)
```

time: 234 us -> 86.2 us (0.37)
  waiting for transfers between devices: 73 us -> 4.67 us
  local copies, waits for them, and re-layouts: 72.9 us -> 10.8 us
  matrix products: 37.1 us -> 0 us
  Pallas kernels: 0 us -> 34.2 us
  blocking collectives: 33.2 us -> 0 us
  starting transfers between devices: 0.01 us -> 31.8 us
  between operations: 13.6 us -> 0.31 us
    reduce_scatter x1 -> x0, waiting for transfers between devices: 73 us -> none  [shards(): lax.psum_scatter(lax.dot_general(out_weight, mixed, (((0,), (0,)), ((), (...]
    gather x2 -> x0, local copies, waits for them, and re-layouts: 61.8 us -> none  [shards(): jnp.take(filter_local, jnp.clip(lag_index, 0, SUB - 1), axis=1)]
    dot_general x4 -> x0, matrix products: 37.1 us -> none  [the longest x1 12.3 us: shards(): jnp.einsum('mct,mcj->cjt', decay_out, start_states, precision=lax.Precisi...]
    pallas_call x0 -> x11, Pallas kernels: none -> 34.2 us  [the longest x5 18.5 us: project_call(): pl.pallas_call(project_kernel, grid_spec=pltpu.PrefetchScalarGridSpec(num...]
    all_gather x1 -> x0, blocking collectives: 33.2 us -> none  [shards(): piece = lax.all_gather(summary[None], 'ctx', axis=0, tiled=True)]
    ppermute x0 -> x17, starting transfers between devices: none -> 31.8 us  [the longest x7 25.9 us: earlier(): lax.ppermute(x, 'ctx', [(i, i + distance) for i in range(count - distance)])]
    dynamic_slice x0 -> x1, local copies, waits for them, and re-layouts: none -> 4.79 us  [part_of_weight(): return lax.dynamic_slice(out_weight, (0, at * width), (channels, width))]
    ppermute x0 -> x17, waiting for transfers between devices: none -> 4.67 us  [the longest x10 4.65 us: swap(): return lax.ppermute(x, 'tp', [(i, i ^ bit) for i in range(n_tp)])]
  transfers between devices with their start and end apart: 1 -> 17, of which waited for: 1 -> 1; matrix products, arithmetic and copies ran while one was open for 0% -> 3% of each run, Pallas kernels for 0% -> 40%
where the time goes in v1:
time: 86.2 us; the launch traced here: 85.5 us
  Pallas kernels  34.2 us (40%)
  starting transfers between devices  31.8 us (37%)
  local copies, waits for them, and re-layouts  10.8 us (13%)
  waiting for transfers between devices  4.67 us (5%)
  other arithmetic  3.73 us (4%)
    ppermute x7, starting transfers between devices, earlier(): lax.ppermute(x, 'ctx', [(i, i + distance) for i in range(count - distance)])  25.9 us
    pallas_call x5, Pallas kernels, project_call(): pl.pallas_call(project_kernel, grid_spec=pltpu.PrefetchScalarGridSpec(num...  18.5 us
    pallas_call x1, Pallas kernels, local_call(): pl.pallas_call(lambda *refs: local_kernel(modes, *refs), grid=(tokens //...  7.24 us
    pallas_call x4, Pallas kernels, mix_call(): pl.pallas_call(lambda *refs: mix_kernel(chunk * CHUNK, modes, *refs), gri...  6.2 us
    unnamed x20, local copies, waits for them, and re-layouts  6.01 us
    ppermute x10, starting transfers between devices, swap(): return lax.ppermute(x, 'tp', [(i, i ^ bit) for i in range(n_tp)])  5.96 us
    dynamic_slice x1, local copies, waits for them, and re-layouts, part_of_weight(): return lax.dynamic_slice(out_weight, (0, at * width), (channels, width))  4.79 us
    ppermute x10, waiting for transfers between devices, swap(): return lax.ppermute(x, 'tp', [(i, i ^ bit) for i in range(n_tp)])  4.65 us
  transfers between devices with their start and end apart: 17, of which 1 were waited for; matrix products, arithmetic and copies ran while one was open for 3% of the time, Pallas kernels for 40%

profile of v1, /device:TPU:0, one launch (start us, length us, event | category | flops | bytes accessed | tf_op | source)
XLA Modules:
  0.0 85.5 jit_solution(3938711478810483134)
XLA Ops:
  0.0 0.0 copy-start.7
  0.0 4.8 %constant_dynamic-slice_fusion = (bf16[1024,1024]{1,0:T(8,128)(2,1)}, bf16[1024,1024]{1,0:T(8,128)(2,1)}) fusion(bf16[1024,4096]{1,0:T(8,128)(2,1)} %own_w_ref.9, s32[]{:T(128)S(6)} %select_n.7, s32[]{:T(128)S(6)} %select_n.6), kind=kLoop, calls=%fused_computation.4 | loop fusion | bytes 8388616 | tf_op jit(solution)/shard_map/dynamic_slice | solution.py:286
  4.8 0.5 collective-permute-start.12
  5.3 0.0 collective-permute-start.11
  5.3 0.0 copy-done.7
  5.3 0.1 copy.8.rates_ref
  5.4 0.0 copy-done.8
  5.4 0.1 copy.9.residues_ref
  5.5 0.0 copy-done.2
  5.5 0.0 copy-done.4
  5.5 2.3 %block_summary.1 = (f32[128,128]{1,0:T(8,128)S(1)}, f32[128,128]{1,0:T(8,128)S(1)}, f32[128,128]{1,0:T(8,128)S(1)}, f32[1,1024]{1,0:T(1,128)S(1)}) custom-call(bf16[512,1024]{1,0:T(8,128)(2,1)S(1)} %copy-done.2, bf16[512,1024]{1,0:T(8,128)(2,1)S(1)} %copy-done.4, f32[64,16]{1,0:T(8,128)S(1)} %copy.8.rates_ref, f32[64,16]{1,0:T(8,128)S(1)} %copy.9.residues_ref), custom_call_target="tpu_custom_call" | custom-call | flops 805306368 | bytes 2097152 | tf_op jit(solution)/shard_map/block_summary/pallas_call | solution.py:91
  7.8 4.9 %collective-permute-start = (f32[128,128]{1,0:T(8,128)S(1)}, f32[128,128]{1,0:T(8,128)S(1)}, u32[]{:S(2)}, u32[]{:S(2)}) collective-permute-start(f32[128,128]{1,0:T(8,128)S(1)} %get-tuple-element.11), channel_id=1, source_target_pairs={{0,4},{4,8},{8,12},{12,16},{16,20},{20,24},{24,28},{1,5},{5,9},{9,... | collective-permute-start | bytes 196616 | tf_op jit(solution)/shard_map/ppermute | solution.py:258
  12.7 3.5 %collective-permute-start.1 = (f32[128,128]{1,0:T(8,128)S(1)}, f32[128,128]{1,0:T(8,128)S(1)}, u32[]{:S(2)}, u32[]{:S(2)}) collective-permute-start(f32[128,128]{1,0:T(8,128)S(1)} %get-tuple-element.11), channel_id=1, source_target_pairs={{0,8},{4,12},{8,16},{12,20},{16,24},{20,28},{1,9},{5,13},{9,17},{1... | collective-permute-start | bytes 196616 | tf_op jit(solution)/shard_map/ppermute | solution.py:258
  16.1 4.5 %collective-permute-start.2 = (f32[128,128]{1,0:T(8,128)S(1)}, f32[128,128]{1,0:T(8,128)S(1)}, u32[]{:S(2)}, u32[]{:S(2)}) collective-permute-start(f32[128,128]{1,0:T(8,128)S(1)} %get-tuple-element.11), channel_id=1, source_target_pairs={{0,12},{4,16},{8,20},{12,24},{16,28},{1,13},{5,17},{9,21},{13,25},... | collective-permute-start | bytes 196616 | tf_op jit(solution)/shard_map/ppermute | solution.py:258
  20.6 0.0 collective-permute-done
  20.6 1.9 %collective-permute-start.3 = (f32[128,128]{1,0:T(8,128)S(1)}, f32[128,128]{1,0:T(8,128)S(1)}, u32[]{:S(2)}, u32[]{:S(2)}) collective-permute-start(f32[128,128]{1,0:T(8,128)S(1)} %get-tuple-element.11), channel_id=1, source_target_pairs={{0,16},{4,20},{8,24},{12,28},{1,17},{5,21},{9,25},{13,29},{2,18},{... | collective-permute-start | bytes 196616 | tf_op jit(solution)/shard_map/ppermute | solution.py:258
  22.6 0.0 collective-permute-done.1
  22.6 1.7 %collective-permute-start.4 = (f32[128,128]{1,0:T(8,128)S(1)}, f32[128,128]{1,0:T(8,128)S(1)}, u32[]{:S(2)}, u32[]{:S(2)}) collective-permute-start(f32[128,128]{1,0:T(8,128)S(1)} %get-tuple-element.11), channel_id=1, source_target_pairs={{0,20},{4,24},{8,28},{1,21},{5,25},{9,29},{2,22},{6,26},{10,30},{3... | collective-permute-start | bytes 196616 | tf_op jit(solution)/shard_map/ppermute | solution.py:258
  24.3 0.0 collective-permute-done.2
  24.3 7.3 %collective-permute-start.5 = (f32[128,128]{1,0:T(8,128)S(1)}, f32[128,128]{1,0:T(8,128)S(1)}, u32[]{:S(2)}, u32[]{:S(2)}) collective-permute-start(f32[128,128]{1,0:T(8,128)S(1)} %get-tuple-element.11), channel_id=1, source_target_pairs={{0,24},{4,28},{1,25},{5,29},{2,26},{6,30},{3,27},{7,31}} | collective-permute-start | bytes 196616 | tf_op jit(solution)/shard_map/ppermute | solution.py:258
  31.6 0.0 collective-permute-done.3
  31.6 2.2 %collective-permute-start.6 = (f32[128,128]{1,0:T(8,128)S(1)}, f32[128,128]{1,0:T(8,128)S(1)}, u32[]{:S(2)}, u32[]{:S(2)}) collective-permute-start(f32[128,128]{1,0:T(8,128)S(1)} %get-tuple-element.11), channel_id=1, source_target_pairs={{0,28},{1,29},{2,30},{3,31}} | collective-permute-start | bytes 196616 | tf_op jit(solution)/shard_map/ppermute | solution.py:258
  33.7 0.0 copy-done.6
  33.7 0.0 copy-start.3
  33.8 1.2 %copy-done.3 = bf16[512,1024]{1,0:T(8,128)(2,1)S(1)} copy-done((bf16[512,1024]{1,0:T(8,128)(2,1)S(1)}, bf16[512,1024]{1,0:T(8,128)(2,1)}, u32[]{:S(2)}) %copy-start.3) | copy-done | bytes 1048600
  35.0 1.2 %copy-done.5 = bf16[512,1024]{1,0:T(8,128)(2,1)S(1)} copy-done((bf16[512,1024]{1,0:T(8,128)(2,1)S(1)}, bf16[512,1024]{1,0:T(8,128)(2,1)}, u32[]{:S(2)}) %copy-start.5) | copy-done | bytes 1048600
  36.2 7.2 %local_conv.1.refs_1_ = f32[4096,128]{1,0:T(8,128)S(1)} custom-call(bf16[512,1024]{1,0:T(8,128)(2,1)S(1)} %copy-done.3, bf16[512,1024]{1,0:T(8,128)(2,1)S(1)} %copy-done.5, f32[128,128]{1,0:T(8,128)S(1)} %get-tuple-element.9.refs_2_, f32[128,128]{1,0:T(8,128)S(1)} %get-tuple-element.10.refs_3_, f32[8,128]{1,0:T(8,128)S(1)} %bitcast.3), custom_call_target="tpu_custom_call" | custom-call | flops 33554432 | bytes 4194304 | tf_op jit(solution)/shard_map/local_conv/pallas_call | solution.py:152
  43.5 0.0 collective-permute-done.4
  43.5 0.0 collective-permute-done.5
  43.5 0.0 collective-permute-done.6
  43.5 0.1 multiply_add_fusion.refs_2_
  43.6 0.0 copy-done.1
  43.6 2.0 %mix.4.own_ref = bf16[128,1024]{1,0:T(8,128)(2,1)} custom-call(bf16[512,1024]{1,0:T(8,128)(2,1)S(1)} %copy-done.1, f32[4096,128]{1,0:T(8,128)S(1)} %local_conv.1.refs_1_, f32[128,128]{1,0:T(8,128)S(1)} %multiply_add_fusion.refs_2_, f32[128,128]{1,0:T(8,128)S(1)} %get-tuple-element.10.refs_3_, f32[1,1024]{1,0:T(1,128)S(1)} %get-tuple-element.12.refs_4_), custom_call_target="tpu_custom_call" | custom-call | flops 201326592 | bytes 1048576 | tf_op jit(solution)/shard_map/mix/pallas_call | solution.py:200
  45.6 0.0 collective-permute-start.7
  45.6 2.0 %mix.5.own_ref = bf16[128,1024]{1,0:T(8,128)(2,1)} custom-call(bf16[512,1024]{1,0:T(8,128)(2,1)S(1)} %copy-done.1, f32[4096,128]{1,0:T(8,128)S(1)} %local_conv.1.refs_1_, f32[128,128]{1,0:T(8,128)S(1)} %multiply_add_fusion.refs_2_, f32[128,128]{1,0:T(8,128)S(1)} %get-tuple-element.10.refs_3_, f32[1,1024]{1,0:T(1,128)S(1)} %get-tuple-element.12.refs_4_), custom_call_target="tpu_custom_call" | custom-call | flops 201326592 | bytes 1048576 | tf_op jit(solution)/shard_map/mix/pallas_call | solution.py:200
  47.6 0.5 collective-permute-start.8
  48.2 1.1 %mix.6.own_ref = bf16[128,1024]{1,0:T(8,128)(2,1)S(1)} custom-call(bf16[512,1024]{1,0:T(8,128)(2,1)S(1)} %copy-done.1, f32[4096,128]{1,0:T(8,128)S(1)} %local_conv.1.refs_1_, f32[128,128]{1,0:T(8,128)S(1)} %multiply_add_fusion.refs_2_, f32[128,128]{1,0:T(8,128)S(1)} %get-tuple-element.10.refs_3_, f32[1,1024]{1,0:T(1,128)S(1)} %get-tuple-element.12.refs_4_), custom_call_target="tpu_custom_call" | custom-call | flops 201326592 | bytes 1048576 | tf_op jit(solution)/shard_map/mix/pallas_call | solution.py:200
  49.2 0.1 collective-permute-start.9
  49.3 1.1 %mix.7.own_ref = bf16[128,1024]{1,0:T(8,128)(2,1)S(1)} custom-call(bf16[512,1024]{1,0:T(8,128)(2,1)S(1)} %copy-done.1, f32[4096,128]{1,0:T(8,128)S(1)} %local_conv.1.refs_1_, f32[128,128]{1,0:T(8,128)S(1)} %multiply_add_fusion.refs_2_, f32[128,128]{1,0:T(8,128)S(1)} %get-tuple-element.10.refs_3_, f32[1,1024]{1,0:T(1,128)S(1)} %get-tuple-element.12.refs_4_), custom_call_target="tpu_custom_call" | custom-call | flops 201326592 | bytes 1048576 | tf_op jit(solution)/shard_map/mix/pallas_call | solution.py:200
  50.4 0.0 collective-permute-done.7.pair_ref
  50.4 0.5 collective-permute-start.10
  51.0 1.1 %pad_maximum_fusion.own_ref = bf16[512,1024]{1,0:T(8,128)(2,1)S(1)} fusion(bf16[128,1024]{1,0:T(8,128)(2,1)S(1)} %mix.7.own_ref, bf16[128,1024]{1,0:T(8,128)(2,1)S(1)} %mix.6.own_ref, bf16[128,1024]{1,0:T(8,128)(2,1)} %mix.5.own_ref, bf16[128,1024]{1,0:T(8,128)(2,1)} %mix.4.own_ref), kind=kLoop, calls=%fused_computation.1 | loop fusion | flops 4194304 | bytes 2097152 | tf_op jit(solution)/shard_map/concatenate | solution.py:307
  52.1 0.0 collective-permute-done.12.pair_w_ref
  52.1 0.0 copy-start
  52.1 3.4 %copy-done = bf16[1024,4096]{1,0:T(8,128)(2,1)S(1)} copy-done((bf16[1024,4096]{1,0:T(8,128)(2,1)S(1)}, bf16[1024,4096]{1,0:T(8,128)(2,1)}, u32[]{:S(2)}) %copy-start) | copy-done | bytes 8388632
  55.5 3.5 %project.6 = bf16[128,1024]{1,0:T(8,128)(2,1)S(1)} custom-call(s32[1]{0:T(128)} %bitcast.2.at_ref, bf16[128,1024]{1,0:T(8,128)(2,1)} %mix.4.own_ref, bf16[128,1024]{1,0:T(8,128)(2,1)} %collective-permute-done.7.pair_ref, bf16[1024,4096]{1,0:T(8,128)(2,1)S(1)} %copy-done, bf16[1024,1024]{1,0:T(8,128)(2,1)} %collective-permute-done.12.pair_w_ref), custom_call_target="tpu_custom_call" | custom-call | flops 536870912 | bytes 4718592 | tf_op jit(solution)/shard_map/project/pallas_call | solution.py:230
  59.0 1.6 %collective-permute-start.13 = (bf16[128,1024]{1,0:T(8,128)(2,1)S(1)}, bf16[128,1024]{1,0:T(8,128)(2,1)S(1)}, u32[]{:S(2)}, u32[]{:S(2)}) collective-permute-start(bf16[128,1024]{1,0:T(8,128)(2,1)S(1)} %project.6), channel_id=1, source_target_pairs={{0,2},{1,3},{2,0},{3,1},{4,6},{5,7},{6,4},{7,5},{8,10},{9,11},{10,... | collective-permute-start | bytes 786440 | tf_op jit(solution)/shard_map/ppermute | solution.py:283
  60.6 0.0 collective-permute-done.8.pair_ref
  60.6 3.5 %project.7 = bf16[128,1024]{1,0:T(8,128)(2,1)S(1)} custom-call(s32[1]{0:T(128)} %bitcast.2.at_ref, bf16[128,1024]{1,0:T(8,128)(2,1)} %mix.5.own_ref, bf16[128,1024]{1,0:T(8,128)(2,1)} %collective-permute-done.8.pair_ref, bf16[1024,4096]{1,0:T(8,128)(2,1)S(1)} %copy-done, bf16[1024,1024]{1,0:T(8,128)(2,1)} %collective-permute-done.12.pair_w_ref), custom_call_target="tpu_custom_call" | custom-call | flops 536870912 | bytes 4718592 | tf_op jit(solution)/shard_map/project/pallas_call | solution.py:230
  64.1 0.6 collective-permute-start.14
  64.7 0.0 collective-permute-done.9.pair_ref
  64.7 3.4 %project.8 = bf16[128,1024]{1,0:T(8,128)(2,1)S(1)} custom-call(s32[1]{0:T(128)} %bitcast.2.at_ref, bf16[128,1024]{1,0:T(8,128)(2,1)S(1)} %mix.6.own_ref, bf16[128,1024]{1,0:T(8,128)(2,1)} %collective-permute-done.9.pair_ref, bf16[1024,4096]{1,0:T(8,128)(2,1)S(1)} %copy-done, bf16[1024,1024]{1,0:T(8,128)(2,1)} %collective-permute-done.12.pair_w_ref), custom_call_target="tpu_custom_call" | custom-call | flops 536870912 | bytes 4718592 | tf_op jit(solution)/shard_map/project/pallas_call | solution.py:230
  68.1 1.6 %collective-permute-start.15 = (bf16[128,1024]{1,0:T(8,128)(2,1)S(1)}, bf16[128,1024]{1,0:T(8,128)(2,1)S(1)}, u32[]{:S(2)}, u32[]{:S(2)}) collective-permute-start(bf16[128,1024]{1,0:T(8,128)(2,1)S(1)} %project.8), channel_id=1, source_target_pairs={{0,2},{1,3},{2,0},{3,1},{4,6},{5,7},{6,4},{7,5},{8,10},{9,11},{10,... | collective-permute-start | bytes 786440 | tf_op jit(solution)/shard_map/ppermute | solution.py:283
  69.7 0.0 collective-permute-done.10.pair_ref
  69.7 3.4 %project.9 = bf16[128,1024]{1,0:T(8,128)(2,1)S(1)} custom-call(s32[1]{0:T(128)} %bitcast.2.at_ref, bf16[128,1024]{1,0:T(8,128)(2,1)S(1)} %mix.7.own_ref, bf16[128,1024]{1,0:T(8,128)(2,1)S(1)} %collective-permute-done.10.pair_ref, bf16[1024,4096]{1,0:T(8,128)(2,1)S(1)} %copy-done, bf16[1024,1024]{1,0:T(8,128)(2,1)} %collective-permute-done.12.pair_w_ref), custom_call_target="tpu_custom_call" | custom-call | flops 536870912 | bytes 4718592 | tf_op jit(solution)/shard_map/project/pallas_call | solution.py:230
  73.1 0.6 collective-permute-start.16
  73.7 1.2 %pad_maximum_fusion.1.pair_ref = bf16[512,1024]{1,0:T(8,128)(2,1)S(1)} fusion(bf16[128,1024]{1,0:T(8,128)(2,1)S(1)} %collective-permute-done.10.pair_ref, bf16[128,1024]{1,0:T(8,128)(2,1)} %collective-permute-done.9.pair_ref, bf16[128,1024]{1,0:T(8,128)(2,1)} %collective-permute-done.8.pair_ref, bf16[128,1024]{1,0:T(8,128)(2,1)} %collective-permute-done.7.pair_ref), kind=kLoop, calls=%fused_computation.2 | loop fusion | flops 4194304 | bytes 2097152 | tf_op jit(solution)/shard_map/concatenate | solution.py:308
  74.9 0.0 collective-permute-done.11.pair_w_ref
  74.9 4.6 %project.5 = f32[512,1024]{1,0:T(8,128)S(1)} custom-call(s32[1]{0:T(128)} %bitcast.at_ref, bf16[512,1024]{1,0:T(8,128)(2,1)S(1)} %pad_maximum_fusion.own_ref, bf16[512,1024]{1,0:T(8,128)(2,1)S(1)} %pad_maximum_fusion.1.pair_ref, bf16[1024,4096]{1,0:T(8,128)(2,1)S(1)} %copy-done, bf16[1024,1024]{1,0:T(8,128)(2,1)} %collective-permute-done.11.pair_w_ref), custom_call_target="tpu_custom_call" | custom-call | flops 2147483648 | bytes 6291456 | tf_op jit(solution)/shard_map/project/pallas_call | solution.py:230
  79.5 0.0 collective-permute-done.13
  79.5 0.0 collective-permute-done.14
  79.5 0.0 collective-permute-done.15
  79.5 4.6 %collective-permute-done.16 = bf16[128,1024]{1,0:T(8,128)(2,1)S(1)} collective-permute-done((bf16[128,1024]{1,0:T(8,128)(2,1)S(1)}, bf16[128,1024]{1,0:T(8,128)(2,1)S(1)}, u32[]{:S(2)}, u32[]{:S(2)}) %collective-permute-start.16) | collective-permute-done | bytes 262176 | tf_op jit(solution)/shard_map/ppermute | solution.py:283
  84.2 1.4 %add_convert_fusion = bf16[512,1024]{1,0:T(8,128)(2,1)} fusion(f32[512,1024]{1,0:T(8,128)S(1)} %project.5, bf16[128,1024]{1,0:T(8,128)(2,1)S(1)} %collective-permute-done.16, bf16[128,1024]{1,0:T(8,128)(2,1)S(1)} %collective-permute-done.15, bf16[128,1024]{1,0:T(8,128)(2,1)S(1)} %collective-permute-done.14, bf16[128,1024]{1,0:T(8,128)(2,1)S(1)} %collective-permute-done.13), kind=kLoop, calls=%fused_computation | loop fusion | flops 5242880 | bytes 4194304 | tf_op jit(solution)/shard_map/convert_element_type | solution.py:313
  (6 shorter events, 0.0 us)
Async XLA Ops:
  0.0 5.3 %copy-start.7 = (f32[64,16]{0,1:T(8,128)S(1)}, f32[64,16]{0,1:T(8,128)}, u32[]{:S(2)}) copy-start(f32[64,16]{0,1:T(8,128)} %param.10) | copy-start | bytes 12292
  0.0 5.4 %copy-start.8 = (f32[64,16]{0,1:T(8,128)S(1)}, f32[64,16]{0,1:T(8,128)}, u32[]{:S(2)}) copy-start(f32[64,16]{0,1:T(8,128)} %param.11) | copy-start | bytes 12292
  0.0 5.5 %copy-start.2 = (bf16[512,1024]{1,0:T(8,128)(2,1)S(1)}, bf16[512,1024]{1,0:T(8,128)(2,1)}, u32[]{:S(2)}) copy-start(bf16[512,1024]{1,0:T(8,128)(2,1)} %refs_0_.5) | copy-start | bytes 3145732
  0.0 5.5 %copy-start.4 = (bf16[512,1024]{1,0:T(8,128)(2,1)S(1)}, bf16[512,1024]{1,0:T(8,128)(2,1)}, u32[]{:S(2)}) copy-start(bf16[512,1024]{1,0:T(8,128)(2,1)} %refs_1_.1) | copy-start | bytes 3145732
  4.8 28.9 %copy-start.6 = (f32[1024]{0:T(1024)S(1)}, f32[1024]{0:T(1024)}, u32[]{:S(2)}) copy-start(f32[1024]{0:T(1024)} %param.12) | copy-start | bytes 12292
  4.8 47.3 %collective-permute-start.12 = (bf16[1024,1024]{1,0:T(8,128)(2,1)}, bf16[1024,1024]{1,0:T(8,128)(2,1)}, u32[]{:S(2)}, u32[]{:S(2)}) collective-permute-start(bf16[1024,1024]{1,0:T(8,128)(2,1)} %get-tuple-element.13), channel_id=1, source_target_pairs={{0,1},{1,0},{2,3},{3,2},{4,5},{5,4},{6,7},{7,6},{8,9},{9,8},{10,11... | collective-permute-start | bytes 6291464 | tf_op jit(solution)/shard_map/ppermute | solution.py:283
  5.3 69.6 %collective-permute-start.11 = (bf16[1024,1024]{1,0:T(8,128)(2,1)}, bf16[1024,1024]{1,0:T(8,128)(2,1)}, u32[]{:S(2)}, u32[]{:S(2)}) collective-permute-start(bf16[1024,1024]{1,0:T(8,128)(2,1)} %get-tuple-element.14), channel_id=1, source_target_pairs={{0,1},{1,0},{2,3},{3,2},{4,5},{5,4},{6,7},{7,6},{8,9},{9,8},{10,11... | collective-permute-start | bytes 6291464 | tf_op jit(solution)/shard_map/ppermute | solution.py:283
  7.8 12.8 %collective-permute-start = (f32[128,128]{1,0:T(8,128)S(1)}, f32[128,128]{1,0:T(8,128)S(1)}, u32[]{:S(2)}, u32[]{:S(2)}) collective-permute-start(f32[128,128]{1,0:T(8,128)S(1)} %get-tuple-element.11), channel_id=1, source_target_pairs={{0,4},{4,8},{8,12},{12,16},{16,20},{20,24},{24,28},{1,5},{5,9},{9,... | collective-permute-start | bytes 196616 | tf_op jit(solution)/shard_map/ppermute | solution.py:258
  12.7 9.9 %collective-permute-start.1 = (f32[128,128]{1,0:T(8,128)S(1)}, f32[128,128]{1,0:T(8,128)S(1)}, u32[]{:S(2)}, u32[]{:S(2)}) collective-permute-start(f32[128,128]{1,0:T(8,128)S(1)} %get-tuple-element.11), channel_id=1, source_target_pairs={{0,8},{4,12},{8,16},{12,20},{16,24},{20,28},{1,9},{5,13},{9,17},{1... | collective-permute-start | bytes 196616 | tf_op jit(solution)/shard_map/ppermute | solution.py:258
  16.1 8.1 %collective-permute-start.2 = (f32[128,128]{1,0:T(8,128)S(1)}, f32[128,128]{1,0:T(8,128)S(1)}, u32[]{:S(2)}, u32[]{:S(2)}) collective-permute-start(f32[128,128]{1,0:T(8,128)S(1)} %get-tuple-element.11), channel_id=1, source_target_pairs={{0,12},{4,16},{8,20},{12,24},{16,28},{1,13},{5,17},{9,21},{13,25},... | collective-permute-start | bytes 196616 | tf_op jit(solution)/shard_map/ppermute | solution.py:258
  20.6 10.9 %collective-permute-start.3 = (f32[128,128]{1,0:T(8,128)S(1)}, f32[128,128]{1,0:T(8,128)S(1)}, u32[]{:S(2)}, u32[]{:S(2)}) collective-permute-start(f32[128,128]{1,0:T(8,128)S(1)} %get-tuple-element.11), channel_id=1, source_target_pairs={{0,16},{4,20},{8,24},{12,28},{1,17},{5,21},{9,25},{13,29},{2,18},{... | collective-permute-start | bytes 196616 | tf_op jit(solution)/shard_map/ppermute | solution.py:258
  22.6 20.9 %collective-permute-start.4 = (f32[128,128]{1,0:T(8,128)S(1)}, f32[128,128]{1,0:T(8,128)S(1)}, u32[]{:S(2)}, u32[]{:S(2)}) collective-permute-start(f32[128,128]{1,0:T(8,128)S(1)} %get-tuple-element.11), channel_id=1, source_target_pairs={{0,20},{4,24},{8,28},{1,21},{5,25},{9,29},{2,22},{6,26},{10,30},{3... | collective-permute-start | bytes 196616 | tf_op jit(solution)/shard_map/ppermute | solution.py:258
  24.3 19.2 %collective-permute-start.5 = (f32[128,128]{1,0:T(8,128)S(1)}, f32[128,128]{1,0:T(8,128)S(1)}, u32[]{:S(2)}, u32[]{:S(2)}) collective-permute-start(f32[128,128]{1,0:T(8,128)S(1)} %get-tuple-element.11), channel_id=1, source_target_pairs={{0,24},{4,28},{1,25},{5,29},{2,26},{6,30},{3,27},{7,31}} | collective-permute-start | bytes 196616 | tf_op jit(solution)/shard_map/ppermute | solution.py:258
  31.6 11.9 %collective-permute-start.6 = (f32[128,128]{1,0:T(8,128)S(1)}, f32[128,128]{1,0:T(8,128)S(1)}, u32[]{:S(2)}, u32[]{:S(2)}) collective-permute-start(f32[128,128]{1,0:T(8,128)S(1)} %get-tuple-element.11), channel_id=1, source_target_pairs={{0,28},{1,29},{2,30},{3,31}} | collective-permute-start | bytes 196616 | tf_op jit(solution)/shard_map/ppermute | solution.py:258
  33.7 1.2 %copy-start.3 = (bf16[512,1024]{1,0:T(8,128)(2,1)S(1)}, bf16[512,1024]{1,0:T(8,128)(2,1)}, u32[]{:S(2)}) copy-start(bf16[512,1024]{1,0:T(8,128)(2,1)} %refs_0_.5) | copy-start | bytes 3145732
  35.0 1.2 %copy-start.5 = (bf16[512,1024]{1,0:T(8,128)(2,1)S(1)}, bf16[512,1024]{1,0:T(8,128)(2,1)}, u32[]{:S(2)}) copy-start(bf16[512,1024]{1,0:T(8,128)(2,1)} %refs_1_.1) | copy-start | bytes 3145732
  36.2 7.4 %copy-start.1 = (bf16[512,1024]{1,0:T(8,128)(2,1)S(1)}, bf16[512,1024]{1,0:T(8,128)(2,1)}, u32[]{:S(2)}) copy-start(bf16[512,1024]{1,0:T(8,128)(2,1)} %refs_0_.9) | copy-start | bytes 3145732
  45.6 4.8 %collective-permute-start.7 = (bf16[128,1024]{1,0:T(8,128)(2,1)}, bf16[128,1024]{1,0:T(8,128)(2,1)}, u32[]{:S(2)}, u32[]{:S(2)}) collective-permute-start(bf16[128,1024]{1,0:T(8,128)(2,1)} %mix.4.own_ref), channel_id=1, source_target_pairs={{0,1},{1,0},{2,3},{3,2},{4,5},{5,4},{6,7},{7,6},{8,9},{9,8},{10,11... | collective-permute-start | bytes 786440 | tf_op jit(solution)/shard_map/ppermute | solution.py:283
  47.6 12.9 %collective-permute-start.8 = (bf16[128,1024]{1,0:T(8,128)(2,1)}, bf16[128,1024]{1,0:T(8,128)(2,1)}, u32[]{:S(2)}, u32[]{:S(2)}) collective-permute-start(bf16[128,1024]{1,0:T(8,128)(2,1)} %mix.5.own_ref), channel_id=1, source_target_pairs={{0,1},{1,0},{2,3},{3,2},{4,5},{5,4},{6,7},{7,6},{8,9},{9,8},{10,11... | collective-permute-start | bytes 786440 | tf_op jit(solution)/shard_map/ppermute | solution.py:283
  49.2 15.5 %collective-permute-start.9 = (bf16[128,1024]{1,0:T(8,128)(2,1)S(1)}, bf16[128,1024]{1,0:T(8,128)(2,1)}, u32[]{:S(2)}, u32[]{:S(2)}) collective-permute-start(bf16[128,1024]{1,0:T(8,128)(2,1)S(1)} %mix.6.own_ref), channel_id=1, source_target_pairs={{0,1},{1,0},{2,3},{3,2},{4,5},{5,4},{6,7},{7,6},{8,9},{9,8},{10,11... | collective-permute-start | bytes 786440 | tf_op jit(solution)/shard_map/ppermute | solution.py:283
  50.4 19.3 %collective-permute-start.10 = (bf16[128,1024]{1,0:T(8,128)(2,1)S(1)}, bf16[128,1024]{1,0:T(8,128)(2,1)S(1)}, u32[]{:S(2)}, u32[]{:S(2)}) collective-permute-start(bf16[128,1024]{1,0:T(8,128)(2,1)S(1)} %mix.7.own_ref), channel_id=1, source_target_pairs={{0,1},{1,0},{2,3},{3,2},{4,5},{5,4},{6,7},{7,6},{8,9},{9,8},{10,11... | collective-permute-start | bytes 786440 | tf_op jit(solution)/shard_map/ppermute | solution.py:283
  52.1 3.4 %copy-start = (bf16[1024,4096]{1,0:T(8,128)(2,1)S(1)}, bf16[1024,4096]{1,0:T(8,128)(2,1)}, u32[]{:S(2)}) copy-start(bf16[1024,4096]{1,0:T(8,128)(2,1)} %own_w_ref.9) | copy-start | bytes 25165828
  59.0 20.5 %collective-permute-start.13 = (bf16[128,1024]{1,0:T(8,128)(2,1)S(1)}, bf16[128,1024]{1,0:T(8,128)(2,1)S(1)}, u32[]{:S(2)}, u32[]{:S(2)}) collective-permute-start(bf16[128,1024]{1,0:T(8,128)(2,1)S(1)} %project.6), channel_id=1, source_target_pairs={{0,2},{1,3},{2,0},{3,1},{4,6},{5,7},{6,4},{7,5},{8,10},{9,11},{10,... | collective-permute-start | bytes 786440 | tf_op jit(solution)/shard_map/ppermute | solution.py:283
  64.1 15.4 %collective-permute-start.14 = (bf16[128,1024]{1,0:T(8,128)(2,1)S(1)}, bf16[128,1024]{1,0:T(8,128)(2,1)S(1)}, u32[]{:S(2)}, u32[]{:S(2)}) collective-permute-start(bf16[128,1024]{1,0:T(8,128)(2,1)S(1)} %project.7), channel_id=1, source_target_pairs={{0,2},{1,3},{2,0},{3,1},{4,6},{5,7},{6,4},{7,5},{8,10},{9,11},{10,... | collective-permute-start | bytes 786440 | tf_op jit(solution)/shard_map/ppermute | solution.py:283
  68.1 11.4 %collective-permute-start.15 = (bf16[128,1024]{1,0:T(8,128)(2,1)S(1)}, bf16[128,1024]{1,0:T(8,128)(2,1)S(1)}, u32[]{:S(2)}, u32[]{:S(2)}) collective-permute-start(bf16[128,1024]{1,0:T(8,128)(2,1)S(1)} %project.8), channel_id=1, source_target_pairs={{0,2},{1,3},{2,0},{3,1},{4,6},{5,7},{6,4},{7,5},{8,10},{9,11},{10,... | collective-permute-start | bytes 786440 | tf_op jit(solution)/shard_map/ppermute | solution.py:283
  73.1 11.1 %collective-permute-start.16 = (bf16[128,1024]{1,0:T(8,128)(2,1)S(1)}, bf16[128,1024]{1,0:T(8,128)(2,1)S(1)}, u32[]{:S(2)}, u32[]{:S(2)}) collective-permute-start(bf16[128,1024]{1,0:T(8,128)(2,1)S(1)} %project.9), channel_id=1, source_target_pairs={{0,2},{1,3},{2,0},{3,1},{4,6},{5,7},{6,4},{7,5},{8,10},{9,11},{10,... | collective-permute-start | bytes 786440 | tf_op jit(solution)/shard_map/ppermute | solution.py:283

commit v2 on v1

v2 whole, which is shorter than its diff:
```python
import jax
import jax.numpy as jnp
from jax import lax
from jax.experimental import pallas as pl
from jax.experimental.pallas import tpu as pltpu
from jax.sharding import PartitionSpec as P

GROUP = 16
LANES = 128
SUBS = 8
BLK = 256
SEG = 256
CHUNK = 128
F32, BF16 = jnp.float32, jnp.bfloat16


def split_bf16(x, parts):
    pieces = []
    for _ in range(parts):
        piece = x.astype(BF16)
        pieces.append(piece)
        x = x - piece.astype(F32)
    return pieces


def dot(a, b):
    return lax.dot_general(a, b, (((1,), (0,)), ((), ())), preferred_element_type=F32)


def group_mask(groups, modes, channels):
    shape = (groups, modes, channels)
    return lax.broadcasted_iota(jnp.int32, shape, 0) == (
        lax.broadcasted_iota(jnp.int32, shape, 2) // GROUP
    )


def column_of(table, modes):
    groups = table.shape[0]
    rows = groups * modes
    spread = jnp.broadcast_to(table[:, None, :], (groups, modes, modes)).reshape(rows, modes)
    pick = lax.broadcasted_iota(jnp.int32, (rows, modes), 1) == (
        lax.broadcasted_iota(jnp.int32, (rows, modes), 0) % modes
    )
    return jnp.sum(jnp.where(pick, spread, 0.0), axis=1, keepdims=True)


def summary_block(first, k_ref, v_ref, rates_ref, residues_ref, sum_ref, rate_ref, residue_ref, flat_ref):
    modes = rates_ref.shape[1]
    tokens, channels = k_ref.shape[0], BLK
    groups = channels // GROUP
    rows = groups * modes
    here_lanes = slice(first, first + channels)
    here_groups = slice(first // GROUP, first // GROUP + groups)
    rate = column_of(rates_ref[here_groups, :], modes)
    residue = column_of(residues_ref[here_groups, :], modes)
    mask = group_mask(groups, modes, channels)
    tile0 = first // LANES

    def compact(dense):
        kept = jnp.where(mask, dense.reshape(groups, modes, channels), 0.0)
        return jnp.sum(kept, axis=0)

    def store(ref, table):
        for tile in range(channels // LANES):
            rows_here = slice((tile0 + tile) * modes, (tile0 + tile + 1) * modes)
            ref[rows_here, :] = table[:, tile * LANES : (tile + 1) * LANES]

    position = lax.broadcasted_iota(jnp.int32, (rows, SEG), 1).astype(F32)
    decay = split_bf16(jnp.exp(-rate * (SEG - 1.0 - position)), 3)
    carry = jnp.exp(-rate * float(SEG))
    dense = None
    for seg in range(tokens // SEG):
        part = slice(seg * SEG, (seg + 1) * SEG)
        u = (k_ref[part, here_lanes].astype(F32) * v_ref[part, here_lanes].astype(F32)).astype(BF16)
        here = dot(decay[2], u) + dot(decay[1], u) + dot(decay[0], u)
        dense = here if dense is None else dense * carry + here
    store(sum_ref, compact(dense))
    wide = jnp.broadcast_to(rate, (rows, channels))
    store(rate_ref, compact(wide))
    store(residue_ref, compact(jnp.broadcast_to(residue, (rows, channels))))
    diagonal = lax.broadcasted_iota(jnp.int32, (rows, rows), 0) == lax.broadcasted_iota(
        jnp.int32, (rows, rows), 1
    )
    flat_ref[:, first // GROUP * modes : first // GROUP * modes + rows] = jnp.sum(
        jnp.where(diagonal, jnp.broadcast_to(rate, (rows, rows)), 0.0), axis=0, keepdims=True
    )


def summary_kernel(k_ref, *refs):
    for first in range(0, k_ref.shape[1], BLK):
        summary_block(first, k_ref, *refs)


VMEM_SPEC = pl.BlockSpec(memory_space=pltpu.VMEM)
ANY_SPEC = pl.BlockSpec(memory_space=pl.ANY)
PARAMS = pltpu.CompilerParams(vmem_limit_bytes=24 << 20)


def cost(flops, bytes_accessed):
    return pl.CostEstimate(flops=flops, bytes_accessed=bytes_accessed, transcendentals=0)


def summary_call(key_in, value, rates, residues):
    tokens, channels = key_in.shape
    modes = rates.shape[1]
    table = jax.ShapeDtypeStruct((channels // LANES * modes, LANES), F32)
    return pl.pallas_call(
        summary_kernel,
        in_specs=[VMEM_SPEC] * 4,
        out_specs=[VMEM_SPEC] * 4,
        out_shape=[table, table, table, jax.ShapeDtypeStruct((1, channels // GROUP * modes), F32)],
        compiler_params=PARAMS,
        cost_estimate=cost(2 * 3 * tokens * BLK * channels, 4 * tokens * channels),
        name="block_summary",
    )(key_in, value, rates, residues)


def local_kernel(
    chunk, modes, parts,
    k_ref, v_ref, rate_ref, residue_ref, skip_ref, state_ref, weight_ref,
    out_ref, end_ref, *rest,
):
    part_refs, (u_ref, sems) = rest[: len(parts)], rest[len(parts) :]
    tiles = k_ref.shape[1] // LANES
    rows = slice(chunk * CHUNK, (chunk + 1) * CHUNK)
    copies = []
    if parts:
        me = lax.axis_index("tp")
        width = part_refs[0].shape[1]
        for i, part in enumerate(parts):
            at = pl.multiple_of((me ^ part) * width, width)
            copies.append(
                pltpu.make_async_copy(weight_ref.at[:, pl.ds(at, width)], part_refs[i], sems.at[i])
            )
            copies[-1].start()
    for tile in range(tiles):
        lanes = slice(tile * LANES, (tile + 1) * LANES)
        u = (k_ref[rows, lanes].astype(F32) * v_ref[rows, lanes].astype(F32)).astype(BF16)
        u_ref[tile * CHUNK : (tile + 1) * CHUNK, :] = u.astype(F32)
    decay = [jnp.exp(-rate_ref[pl.ds(m, tiles, stride=modes), :]) for m in range(modes)]
    residue = [residue_ref[pl.ds(m, tiles, stride=modes), :] for m in range(modes)]
    skip = skip_ref[...]

    def step(t, states):
        u = u_ref[pl.ds(t, tiles, stride=CHUNK), :]
        states = tuple(d * s + u for d, s in zip(decay, states))
        terms = [skip * u] + [r * s for r, s in zip(residue, states)]
        while len(terms) > 1:
            terms = [a + b for a, b in zip(terms[::2], terms[1::2])] + (
                [terms[-1]] if len(terms) % 2 else []
            )
        out_ref[pl.ds(t, tiles, stride=CHUNK), :] = terms[0]
        return states

    first = tuple(state_ref[m * tiles : (m + 1) * tiles, :] for m in range(modes))
    last = lax.fori_loop(0, CHUNK, step, first, unroll=4)
    for m in range(modes):
        end_ref[m * tiles : (m + 1) * tiles, :] = last[m]
    for copy in copies:
        copy.wait()


def local_call(chunk, parts, key_in, value, rate_table, residue_table, skip_tiles, state, weight, width):
    channels = key_in.shape[1]
    tiles = channels // LANES
    modes = rate_table.shape[0] // tiles
    part_shape = jax.ShapeDtypeStruct((channels, width), weight.dtype)
    return pl.pallas_call(
        lambda *refs: local_kernel(chunk, modes, parts, *refs),
        in_specs=[VMEM_SPEC] * 6 + [ANY_SPEC],
        out_specs=[VMEM_SPEC] * 2 + [ANY_SPEC] * len(parts),
        out_shape=[
            jax.ShapeDtypeStruct((CHUNK * tiles, LANES), F32),
            jax.ShapeDtypeStruct((modes * tiles, LANES), F32),
        ]
        + [part_shape] * len(parts),
        scratch_shapes=[
            pltpu.VMEM((tiles * CHUNK, LANES), F32),
            pltpu.SemaphoreType.DMA((max(len(parts), 1),)),
        ],
        compiler_params=PARAMS,
        cost_estimate=cost(4 * modes * CHUNK * channels, 8 * CHUNK * channels),
        name="local_conv",
    )(key_in, value, rate_table, residue_table, skip_tiles, state, weight)


def mix_kernel(chunk, modes, q_ref, local_ref, state_ref, residue_ref, flat_ref, out_ref):
    groups = BLK // GROUP
    tiles = BLK // LANES
    rows = groups * modes
    tokens = slice(chunk * CHUNK, (chunk + 1) * CHUNK)
    mask = group_mask(groups, modes, BLK)
    since = lax.broadcasted_iota(jnp.int32, (CHUNK, rows), 0).astype(F32) + (chunk * CHUNK + 1.0)
    for block in range(q_ref.shape[1] // BLK):
        tile0 = block * tiles
        weighted = [
            state_ref[i * modes : (i + 1) * modes, :] * residue_ref[i * modes : (i + 1) * modes, :]
            for i in range(tile0, tile0 + tiles)
        ]
        spread = jnp.broadcast_to(jnp.concatenate(weighted, axis=1)[None], (groups, modes, BLK))
        spread = jnp.where(mask, spread, 0.0).reshape(rows, BLK)
        flat = flat_ref[:, block * rows : (block + 1) * rows]
        decay_hi, decay_lo = split_bf16(jnp.exp(-flat * since), 2)
        state_hi, state_lo = split_bf16(spread, 2)
        past = dot(decay_lo, state_hi) + dot(decay_hi, state_lo) + dot(decay_hi, state_hi)
        for tile in range(tiles):
            lanes = slice((tile0 + tile) * LANES, (tile0 + tile + 1) * LANES)
            conv = local_ref[(tile0 + tile) * CHUNK : (tile0 + tile + 1) * CHUNK, :]
            conv = conv + past[:, tile * LANES : (tile + 1) * LANES]
            out_ref[:, lanes] = (q_ref[tokens, lanes].astype(F32) * conv).astype(BF16)


def mix_call(chunk, query, local, state, residue_table, flat_rates):
    channels = query.shape[1]
    modes = flat_rates.shape[1] * GROUP // channels
    return pl.pallas_call(
        lambda *refs: mix_kernel(chunk, modes, *refs),
        in_specs=[VMEM_SPEC] * 5,
        out_specs=VMEM_SPEC,
        out_shape=jax.ShapeDtypeStruct((CHUNK, channels), BF16),
        compiler_params=PARAMS,
        cost_estimate=cost(2 * 3 * CHUNK * BLK * channels, 8 * CHUNK * channels),
        name="mix",
    )(query, local, state, residue_table, flat_rates)


def project_kernel(own_ref, pair_ref, own_w_ref, pair_w_ref, out_ref):
    cols = 256
    for at in range(0, out_ref.shape[1], cols):
        lanes = slice(at, at + cols)
        total = dot(own_ref[...], own_w_ref[:, lanes]) + dot(pair_ref[...], pair_w_ref[:, lanes])
        out_ref[:, lanes] = total.astype(out_ref.dtype)


def project_call(mixed, mixed_pair, weight, weight_pair, out_dtype):
    tokens, depth = mixed.shape
    width = weight.shape[1]
    return pl.pallas_call(
        project_kernel,
        in_specs=[VMEM_SPEC] * 4,
        out_specs=VMEM_SPEC,
        out_shape=jax.ShapeDtypeStruct((tokens, width), out_dtype),
        compiler_params=PARAMS,
        cost_estimate=cost(4 * tokens * depth * width, 4 * depth * width + 4 * tokens * width),
        name="project",
    )(mixed, mixed_pair, weight, weight_pair)


def add_kernel(near_ref, arrived_ref, *refs):
    refs[-1][...] = (near_ref[...] + arrived_ref[...].astype(F32)).astype(BF16)


def add_call(chunk, near, arrived, out, tokens):
    width = near.shape[1]
    block = pl.BlockSpec((CHUNK, width), lambda i: (0, 0))
    args = [near, arrived] + ([] if out is None else [out])
    return pl.pallas_call(
        add_kernel,
        grid=(1,),
        in_specs=[block, block] + [ANY_SPEC] * (len(args) - 2),
        out_specs=pl.BlockSpec((CHUNK, width), lambda i: (chunk, 0)),
        out_shape=jax.ShapeDtypeStruct((tokens, width), BF16),
        input_output_aliases={} if out is None else {2: 0},
        compiler_params=PARAMS,
        cost_estimate=cost(CHUNK * width, 8 * CHUNK * width),
        name="add_arrived",
    )(*args)


def tie(*arrays):
    return lax.optimization_barrier(arrays)


def shards(query, key_in, value, rates, residues, skip_gain, out_weight, *, n_ctx, n_tp):
    tokens, channels = query.shape
    width = out_weight.shape[1] // n_tp
    tiles = channels // LANES
    chunks = tokens // CHUNK
    block = lax.axis_index("ctx")

    def swap(x, bit):
        return lax.ppermute(x, "tp", [(i, i ^ bit) for i in range(n_tp)])

    total, rate_table, residue_table, flat_rates = summary_call(key_in, value, rates, residues)
    skip_tiles = skip_gain.reshape(tiles, LANES)
    carry = jnp.zeros((tiles * rates.shape[1], LANES), F32)
    out_weight = pltpu.with_memory_space_constraint(out_weight, pltpu.HBM)
    local, parts = [], []

    def next_local():
        chunk = len(local)
        wanted = {0: (2, 3), 1: (0, 1)}.get(chunk, ())
        out, end, *got = local_call(
            chunk, wanted, key_in, value, rate_table, residue_table, skip_tiles, carry, out_weight, width
        )
        local.append(out)
        parts.extend(got)
        return end

    def decayed(blocks):
        return jnp.exp(-rate_table * (blocks * tokens).astype(F32))

    state = jnp.zeros_like(total)
    span = 1
    while span < n_ctx:
        last = 2 * span >= n_ctx
        pairs = [(i, i ^ span) for i in range(n_ctx) if not (last and i & span)]
        other = lax.ppermute(total, "ctx", pairs)
        if len(local) < chunks:
            carry = next_local()
            if last:
                while len(local) < chunks:
                    carry = next_local()
            other, carry = tie(other, carry)
        upper = (block & span) != 0
        state = jnp.where(upper, state + decayed(block & (span - 1)) * other, state)
        over = decayed(jnp.int32(span))
        total = jnp.where(upper, total + over * other, other + over * total)
        if not last:
            total, carry = tie(total, carry)
        span *= 2
    while len(local) < chunks:
        carry = next_local()
    far, far_send, near, near_send = parts
    pair_far = swap(far_send, 1)
    pair_near = swap(near_send, 1)

    mixed = [mix_call(c, query, local[c], state, residue_table, flat_rates) for c in range(chunks)]
    mixed_pair = [swap(m, 1) for m in mixed]
    arrived = [
        swap(project_call(m, p, far, pair_far, BF16), 2) for m, p in zip(mixed, mixed_pair)
    ]
    out = None
    for c in range(chunks):
        here = project_call(mixed[c], mixed_pair[c], near, pair_near, F32)
        out = add_call(c, here, arrived[c], out, tokens)
    return out


def solution(mesh):
    n_ctx, n_tp = mesh.shape["ctx"], mesh.shape["tp"]
    in_specs = (
        P("ctx", "tp"),
        P("ctx", "tp"),
        P("ctx", "tp"),
        P("tp", None),
        P("tp", None),
        P("tp"),
        P("tp", None),
    )

    def body(*args):
        return shards(*args, n_ctx=n_ctx, n_tp=n_tp)

    return jax.shard_map(body, mesh=mesh, in_specs=in_specs, out_specs=P("ctx", "tp"), check_vma=False)
```

time: 86.2 us -> 193 us (2.24)
  Pallas kernels: 34.2 us -> 158 us
  starting transfers between devices: 31.8 us -> 14.7 us
  other arithmetic: 3.73 us -> 0.73 us
  waiting for transfers between devices: 4.67 us -> 7.58 us
    pallas_call x11 -> x21, Pallas kernels: 34.2 us -> 158 us  [the longest x4 134 us: local_call(): pl.pallas_call(lambda *refs: local_kernel(chunk, modes, parts, *refs), in...]
    ppermute x7 -> x3, starting transfers between devices: 25.9 us -> 9.05 us  [shards(): other = lax.ppermute(total, 'ctx', pairs)]
    unnamed x20 -> x28, local copies, waits for them, and re-layouts: 6.01 us -> 11 us
    ppermute x7 -> x3, waiting for transfers between devices: 0.02 us -> 4.87 us  [shards(): other = lax.ppermute(total, 'ctx', pairs)]
    dynamic_slice x1 -> x0, local copies, waits for them, and re-layouts: 4.79 us -> none  [part_of_weight(): return lax.dynamic_slice(out_weight, (0, at * width), (channels, width))]
    concatenate x2 -> x0, other arithmetic: 2.28 us -> none  [the longest x1 1.18 us: shards(): jnp.concatenate(mixed_pair, axis=0)]
    ppermute x10, waiting for transfers between devices: 4.65 us -> 2.71 us  [swap(): return lax.ppermute(x, 'tp', [(i, i ^ bit) for i in range(n_tp)])]
  transfers between devices with their start and end apart: 17 -> 13, of which waited for: 1 -> 3; matrix products, arithmetic and copies ran while one was open for 3% -> 0% of each run, Pallas kernels for 40% -> 81%
where the time goes in v2:
time: 193 us; the launch traced here: 192 us
  Pallas kernels  158 us (82%)
  starting transfers between devices  14.7 us (8%)
  local copies, waits for them, and re-layouts  11 us (6%)
  waiting for transfers between devices  7.58 us (4%)
    pallas_call x4, Pallas kernels, local_call(): pl.pallas_call(lambda *refs: local_kernel(chunk, modes, parts, *refs), in...  134 us
    pallas_call x8, Pallas kernels, project_call(): pl.pallas_call(project_kernel, in_specs=[VMEM_SPEC] * 4, out_specs=VMEM_S...  18.5 us
    unnamed x28, local copies, waits for them, and re-layouts  11 us
    ppermute x3, starting transfers between devices, shards(): other = lax.ppermute(total, 'ctx', pairs)  9.05 us
    ppermute x10, starting transfers between devices, swap(): return lax.ppermute(x, 'tp', [(i, i ^ bit) for i in range(n_tp)])  5.68 us
    ppermute x3, waiting for transfers between devices, shards(): other = lax.ppermute(total, 'ctx', pairs)  4.87 us
  transfers between devices with their start and end apart: 13, of which 3 were waited for; matrix products, arithmetic and copies ran while one was open for 0% of the time, Pallas kernels for 81%

profile of v2, /device:TPU:0, one launch (start us, length us, event | category | flops | bytes accessed | tf_op | source)
XLA Modules:
  0.0 192.5 jit_solution(4232477569897457341)
XLA Ops:
  0.0 0.8 copy.11.refs_1_
  0.8 0.8 copy.12.refs_2_
  1.6 1.2 copy-done.2
  2.8 1.2 copy-done.4
  4.0 1.2 block_summary.1
  5.3 3.0 %collective-permute-start = (f32[128,128]{1,0:T(8,128)S(1)}, f32[128,128]{1,0:T(8,128)S(1)}, u32[]{:S(2)}, u32[]{:S(2)}) collective-permute-start(f32[128,128]{1,0:T(8,128)S(1)} %get-tuple-element.30), channel_id=1, source_target_pairs={{0,4},{4,0},{8,12},{12,8},{16,20},{20,16},{24,28},{28,24},{1,5},{5... | collective-permute-start | bytes 196616 | tf_op jit(solution)/shard_map/ppermute | solution.py:308
  8.3 0.0 copy-start.3
  8.3 64.7 %local_conv.4 = (f32[1024,128]{1,0:T(8,128)S(1)}, f32[128,128]{1,0:T(8,128)S(1)}, bf16[1024,1024]{1,0:T(8,128)(2,1)S(1)}, bf16[1024,1024]{1,0:T(8,128)(2,1)}) custom-call(bf16[512,1024]{1,0:T(8,128)(2,1)S(1)} %copy-done.2, bf16[512,1024]{1,0:T(8,128)(2,1)S(1)} %copy-done.4, f32[128,128]{1,0:T(8,128)S(1)} %get-tuple-element.28.refs_2_, ...), custom_call_target="tpu_custom_call" | custom-call | flops 8388608 | bytes 1048576 | tf_op jit(solution)/shard_map/local_conv/pallas_call | solution.py:168
  73.0 0.8 copy-done.8
  73.8 0.0 collective-permute-start.5
  73.8 0.0 collective-permute-done
  73.8 0.0 copy-start.5
  73.8 1.2 copy-done.5
  75.1 64.6 %local_conv.5 = (f32[1024,128]{1,0:T(8,128)S(1)}, f32[128,128]{1,0:T(8,128)S(1)}, bf16[1024,1024]{1,0:T(8,128)(2,1)S(1)}, bf16[1024,1024]{1,0:T(8,128)(2,1)}) custom-call(bf16[512,1024]{1,0:T(8,128)(2,1)S(1)} %copy-done.3, bf16[512,1024]{1,0:T(8,128)(2,1)S(1)} %copy-done.5, f32[128,128]{1,0:T(8,128)S(1)} %get-tuple-element.28.refs_2_, ...), custom_call_target="tpu_custom_call" | custom-call | flops 8388608 | bytes 1048576 | tf_op jit(solution)/shard_map/local_conv/pallas_call | solution.py:168
  139.7 1.4 copy-done
  141.1 0.8 copy-done.10
  141.9 0.5 collective-permute-start.4
  142.4 1.6 collective-permute-start.1
  143.9 2.7 %collective-permute-done.1 = f32[128,128]{1,0:T(8,128)S(1)} collective-permute-done((f32[128,128]{1,0:T(8,128)S(1)}, f32[128,128]{1,0:T(8,128)S(1)}, u32[]{:S(2)}, u32[]{:S(2)}) %collective-permute-start.1) | collective-permute-done | bytes 65568 | tf_op jit(solution)/shard_map/ppermute | solution.py:308
  146.6 0.7 add_select_fusion.2
  147.3 4.5 %collective-permute-start.2 = (f32[128,128]{1,0:T(8,128)}, f32[128,128]{1,0:T(8,128)S(1)}, u32[]{:S(2)}, u32[]{:S(2)}) collective-permute-start(f32[128,128]{1,0:T(8,128)} %add_select_fusion.2), channel_id=1, source_target_pairs={{0,16},{4,20},{8,24},{12,28},{1,17},{5,21},{9,25},{13,29},{2,18},{... | collective-permute-start | bytes 196616 | tf_op jit(solution)/shard_map/ppermute | solution.py:308
  151.8 0.0 copy-start.6
  151.8 2.2 %collective-permute-done.2 = f32[128,128]{1,0:T(8,128)S(1)} collective-permute-done((f32[128,128]{1,0:T(8,128)}, f32[128,128]{1,0:T(8,128)S(1)}, u32[]{:S(2)}, u32[]{:S(2)}) %collective-permute-start.2) | collective-permute-done | bytes 65568 | tf_op jit(solution)/shard_map/ppermute | solution.py:308
  154.0 0.1 add_select_fusion.refs_2_
  154.0 0.0 copy-start.7
  154.0 1.2 copy-done.7
  155.3 1.0 copy-done.11
  156.3 0.5 mix.6.own_ref
  156.8 0.1 collective-permute-start.9
  156.8 0.5 copy-done.9
  157.3 0.4 mix.7.own_ref
  157.8 0.1 collective-permute-start.11
  157.9 1.8 local_conv.6
  159.7 0.5 mix.5.own_ref
  160.2 0.6 collective-permute-start.7
  160.7 2.5 %local_conv.7 = (f32[1024,128]{1,0:T(8,128)S(1)}, f32[128,128]{1,0:T(8,128)}) custom-call(bf16[512,1024]{1,0:T(8,128)(2,1)S(1)} %copy-done.3, bf16[512,1024]{1,0:T(8,128)(2,1)S(1)} %copy-done.6, f32[128,128]{1,0:T(8,128)S(1)} %get-tuple-element.28.refs_2_, f32[128,128]{1,0:T(8,128)S(1)} %get-tuple-element.29.refs_3_, f32[8,128]{1,0:T(8,128)S(1)} %bitcast.4, ...), custom_call_target="tpu_custom_call" | custom-call | flops 8388608 | bytes 1048576 | tf_op jit(solution)/shard_map/local_conv/pallas_call | solution.py:168
  163.2 0.5 mix.4.own_ref
  163.7 0.0 collective-permute-done.9.pair_ref
  163.7 0.1 collective-permute-start.3
  163.8 0.0 collective-permute-done.5.pair_w_ref
  163.8 2.3 %project.13 = bf16[128,1024]{1,0:T(8,128)(2,1)S(1)} custom-call(bf16[128,1024]{1,0:T(8,128)(2,1)S(1)} %mix.6.own_ref, bf16[128,1024]{1,0:T(8,128)(2,1)S(1)} %collective-permute-done.9.pair_ref, bf16[1024,1024]{1,0:T(8,128)(2,1)S(1)} %get-tuple-element.46.own_w_ref, bf16[1024,1024]{1,0:T(8,128)(2,1)} %collective-permute-done.5.pair_w_ref), custom_call_target="tpu_custom_call" | custom-call | flops 536870912 | bytes 4718592 | tf_op jit(solution)/shard_map/project/pallas_call | solution.py:238
  166.1 1.6 collective-permute-start.10
  167.7 0.0 collective-permute-done.11.pair_ref
  167.7 2.3 %project.15 = bf16[128,1024]{1,0:T(8,128)(2,1)S(1)} custom-call(bf16[128,1024]{1,0:T(8,128)(2,1)S(1)} %mix.7.own_ref, bf16[128,1024]{1,0:T(8,128)(2,1)S(1)} %collective-permute-done.11.pair_ref, bf16[1024,1024]{1,0:T(8,128)(2,1)S(1)} %get-tuple-element.46.own_w_ref, bf16[1024,1024]{1,0:T(8,128)(2,1)} %collective-permute-done.5.pair_w_ref), custom_call_target="tpu_custom_call" | custom-call | flops 536870912 | bytes 4718592 | tf_op jit(solution)/shard_map/project/pallas_call | solution.py:238
  170.0 0.6 collective-permute-start.12
  170.6 0.0 collective-permute-done.7.pair_ref
  170.6 2.3 %project.11 = bf16[128,1024]{1,0:T(8,128)(2,1)S(1)} custom-call(bf16[128,1024]{1,0:T(8,128)(2,1)S(1)} %mix.5.own_ref, bf16[128,1024]{1,0:T(8,128)(2,1)S(1)} %collective-permute-done.7.pair_ref, bf16[1024,1024]{1,0:T(8,128)(2,1)S(1)} %get-tuple-element.46.own_w_ref, bf16[1024,1024]{1,0:T(8,128)(2,1)} %collective-permute-done.5.pair_w_ref), custom_call_target="tpu_custom_call" | custom-call | flops 536870912 | bytes 4718592 | tf_op jit(solution)/shard_map/project/pallas_call | solution.py:238
  172.9 1.6 collective-permute-start.8
  174.5 0.0 collective-permute-done.3.pair_ref
  174.5 2.3 %project.9 = bf16[128,1024]{1,0:T(8,128)(2,1)S(1)} custom-call(bf16[128,1024]{1,0:T(8,128)(2,1)S(1)} %mix.4.own_ref, bf16[128,1024]{1,0:T(8,128)(2,1)S(1)} %collective-permute-done.3.pair_ref, bf16[1024,1024]{1,0:T(8,128)(2,1)S(1)} %get-tuple-element.46.own_w_ref, bf16[1024,1024]{1,0:T(8,128)(2,1)} %collective-permute-done.5.pair_w_ref), custom_call_target="tpu_custom_call" | custom-call | flops 536870912 | bytes 4718592 | tf_op jit(solution)/shard_map/project/pallas_call | solution.py:238
  176.9 0.6 collective-permute-start.6
  177.5 0.0 collective-permute-done.4.pair_w_ref
  177.5 2.3 %project.14.near_ref = f32[128,1024]{1,0:T(8,128)S(1)} custom-call(bf16[128,1024]{1,0:T(8,128)(2,1)S(1)} %mix.7.own_ref, bf16[128,1024]{1,0:T(8,128)(2,1)S(1)} %collective-permute-done.11.pair_ref, bf16[1024,1024]{1,0:T(8,128)(2,1)S(1)} %copy-done.1, bf16[1024,1024]{1,0:T(8,128)(2,1)} %collective-permute-done.4.pair_w_ref), custom_call_target="tpu_custom_call" | custom-call | flops 536870912 | bytes 4718592 | tf_op jit(solution)/shard_map/project/pallas_call | solution.py:238
  179.8 2.3 %project.12.near_ref = f32[128,1024]{1,0:T(8,128)S(1)} custom-call(bf16[128,1024]{1,0:T(8,128)(2,1)S(1)} %mix.6.own_ref, bf16[128,1024]{1,0:T(8,128)(2,1)S(1)} %collective-permute-done.9.pair_ref, bf16[1024,1024]{1,0:T(8,128)(2,1)S(1)} %copy-done.1, bf16[1024,1024]{1,0:T(8,128)(2,1)} %collective-permute-done.4.pair_w_ref), custom_call_target="tpu_custom_call" | custom-call | flops 536870912 | bytes 4718592 | tf_op jit(solution)/shard_map/project/pallas_call | solution.py:238
  182.1 2.3 %project.10.near_ref = f32[128,1024]{1,0:T(8,128)S(1)} custom-call(bf16[128,1024]{1,0:T(8,128)(2,1)S(1)} %mix.5.own_ref, bf16[128,1024]{1,0:T(8,128)(2,1)S(1)} %collective-permute-done.7.pair_ref, bf16[1024,1024]{1,0:T(8,128)(2,1)S(1)} %copy-done.1, bf16[1024,1024]{1,0:T(8,128)(2,1)} %collective-permute-done.4.pair_w_ref), custom_call_target="tpu_custom_call" | custom-call | flops 536870912 | bytes 4718592 | tf_op jit(solution)/shard_map/project/pallas_call | solution.py:238
  184.4 2.3 %project.8.near_ref = f32[128,1024]{1,0:T(8,128)S(1)} custom-call(bf16[128,1024]{1,0:T(8,128)(2,1)S(1)} %mix.4.own_ref, bf16[128,1024]{1,0:T(8,128)(2,1)S(1)} %collective-permute-done.3.pair_ref, bf16[1024,1024]{1,0:T(8,128)(2,1)S(1)} %copy-done.1, bf16[1024,1024]{1,0:T(8,128)(2,1)} %collective-permute-done.4.pair_w_ref), custom_call_target="tpu_custom_call" | custom-call | flops 536870912 | bytes 4718592 | tf_op jit(solution)/shard_map/project/pallas_call | solution.py:238
  186.8 0.0 collective-permute-done.12.arrived_ref
  186.8 0.7 add_arrived.4.refs_0_
  187.5 0.0 collective-permute-done.10.arrived_ref
  187.5 0.7 add_arrived.5.refs_0_
  188.3 0.0 collective-permute-done.8.arrived_ref
  188.3 0.7 add_arrived.6.refs_0_
  189.0 2.7 %collective-permute-done.6.arrived_ref = bf16[128,1024]{1,0:T(8,128)(2,1)S(1)} collective-permute-done((bf16[128,1024]{1,0:T(8,128)(2,1)S(1)}, bf16[128,1024]{1,0:T(8,128)(2,1)S(1)}, u32[]{:S(2)}, u32[]{:S(2)}) %collective-permute-start.6) | collective-permute-done | bytes 262176 | tf_op jit(solution)/shard_map/ppermute | solution.py:282
  191.7 0.7 add_arrived.7
  (15 shorter events, 0.1 us)
Async XLA Ops:
  0.0 8.3 %copy-start.12 = (f32[1024]{0:T(1024)S(1)}, f32[1024]{0:T(1024)}, u32[]{:S(2)}) copy-start(f32[1024]{0:T(1024)} %param.12) | copy-start | bytes 12292
  1.6 1.2 copy-start.2
  2.8 1.2 copy-start.4
  5.3 68.5 %collective-permute-start = (f32[128,128]{1,0:T(8,128)S(1)}, f32[128,128]{1,0:T(8,128)S(1)}, u32[]{:S(2)}, u32[]{:S(2)}) collective-permute-start(f32[128,128]{1,0:T(8,128)S(1)} %get-tuple-element.30), channel_id=1, source_target_pairs={{0,4},{4,0},{8,12},{12,8},{16,20},{20,16},{24,28},{28,24},{1,5},{5... | collective-permute-start | bytes 196616 | tf_op jit(solution)/shard_map/ppermute | solution.py:308
  8.3 65.5 %copy-start.3 = (bf16[512,1024]{1,0:T(8,128)(2,1)S(1)}, bf16[512,1024]{1,0:T(8,128)(2,1)}, u32[]{:S(2)}) copy-start(bf16[512,1024]{1,0:T(8,128)(2,1)} %refs_0_.13) | copy-start | bytes 3145732
  73.0 0.8 copy-start.8
  73.8 90.0 %collective-permute-start.5 = (bf16[1024,1024]{1,0:T(8,128)(2,1)}, bf16[1024,1024]{1,0:T(8,128)(2,1)}, u32[]{:S(2)}, u32[]{:S(2)}) collective-permute-start(bf16[1024,1024]{1,0:T(8,128)(2,1)} %get-tuple-element.47), channel_id=1, source_target_pairs={{0,1},{1,0},{2,3},{3,2},{4,5},{5,4},{6,7},{7,6},{8,9},{9,8},{10,11... | collective-permute-start | bytes 6291464 | tf_op jit(solution)/shard_map/ppermute | solution.py:282
  73.8 1.2 copy-start.5
  139.7 1.4 copy-start
  141.1 0.8 copy-start.10
  141.9 35.6 %collective-permute-start.4 = (bf16[1024,1024]{1,0:T(8,128)(2,1)}, bf16[1024,1024]{1,0:T(8,128)(2,1)}, u32[]{:S(2)}, u32[]{:S(2)}) collective-permute-start(bf16[1024,1024]{1,0:T(8,128)(2,1)} %get-tuple-element.45), channel_id=1, source_target_pairs={{0,1},{1,0},{2,3},{3,2},{4,5},{5,4},{6,7},{7,6},{8,9},{9,8},{10,11... | collective-permute-start | bytes 6291464 | tf_op jit(solution)/shard_map/ppermute | solution.py:282
  142.4 4.3 %collective-permute-start.1 = (f32[128,128]{1,0:T(8,128)S(1)}, f32[128,128]{1,0:T(8,128)S(1)}, u32[]{:S(2)}, u32[]{:S(2)}) collective-permute-start(f32[128,128]{1,0:T(8,128)S(1)} %add_select_fusion.3), channel_id=1, source_target_pairs={{0,8},{4,12},{8,0},{12,4},{16,24},{20,28},{24,16},{28,20},{1,9},{5... | collective-permute-start | bytes 196616 | tf_op jit(solution)/shard_map/ppermute | solution.py:308
  147.3 6.7 %collective-permute-start.2 = (f32[128,128]{1,0:T(8,128)}, f32[128,128]{1,0:T(8,128)S(1)}, u32[]{:S(2)}, u32[]{:S(2)}) collective-permute-start(f32[128,128]{1,0:T(8,128)} %add_select_fusion.2), channel_id=1, source_target_pairs={{0,16},{4,20},{8,24},{12,28},{1,17},{5,21},{9,25},{13,29},{2,18},{... | collective-permute-start | bytes 196616 | tf_op jit(solution)/shard_map/ppermute | solution.py:308
  151.8 6.1 %copy-start.6 = (bf16[512,1024]{1,0:T(8,128)(2,1)S(1)}, bf16[512,1024]{1,0:T(8,128)(2,1)}, u32[]{:S(2)}) copy-start(bf16[512,1024]{1,0:T(8,128)(2,1)} %refs_1_.8) | copy-start | bytes 3145732
  154.0 1.2 copy-start.7
  155.3 1.0 copy-start.11
  156.3 1.0 copy-start.9
  156.8 6.9 %collective-permute-start.9 = (bf16[128,1024]{1,0:T(8,128)(2,1)S(1)}, bf16[128,1024]{1,0:T(8,128)(2,1)S(1)}, u32[]{:S(2)}, u32[]{:S(2)}) collective-permute-start(bf16[128,1024]{1,0:T(8,128)(2,1)S(1)} %mix.6.own_ref), channel_id=1, source_target_pairs={{0,1},{1,0},{2,3},{3,2},{4,5},{5,4},{6,7},{7,6},{8,9},{9,8},{10,11... | collective-permute-start | bytes 786440 | tf_op jit(solution)/shard_map/ppermute | solution.py:282
  157.8 9.9 %collective-permute-start.11 = (bf16[128,1024]{1,0:T(8,128)(2,1)S(1)}, bf16[128,1024]{1,0:T(8,128)(2,1)S(1)}, u32[]{:S(2)}, u32[]{:S(2)}) collective-permute-start(bf16[128,1024]{1,0:T(8,128)(2,1)S(1)} %mix.7.own_ref), channel_id=1, source_target_pairs={{0,1},{1,0},{2,3},{3,2},{4,5},{5,4},{6,7},{7,6},{8,9},{9,8},{10,11... | collective-permute-start | bytes 786440 | tf_op jit(solution)/shard_map/ppermute | solution.py:282
  160.2 10.4 %collective-permute-start.7 = (bf16[128,1024]{1,0:T(8,128)(2,1)S(1)}, bf16[128,1024]{1,0:T(8,128)(2,1)S(1)}, u32[]{:S(2)}, u32[]{:S(2)}) collective-permute-start(bf16[128,1024]{1,0:T(8,128)(2,1)S(1)} %mix.5.own_ref), channel_id=1, source_target_pairs={{0,1},{1,0},{2,3},{3,2},{4,5},{5,4},{6,7},{7,6},{8,9},{9,8},{10,11... | collective-permute-start | bytes 786440 | tf_op jit(solution)/shard_map/ppermute | solution.py:282
  163.7 10.8 %collective-permute-start.3 = (bf16[128,1024]{1,0:T(8,128)(2,1)S(1)}, bf16[128,1024]{1,0:T(8,128)(2,1)S(1)}, u32[]{:S(2)}, u32[]{:S(2)}) collective-permute-start(bf16[128,1024]{1,0:T(8,128)(2,1)S(1)} %mix.4.own_ref), channel_id=1, source_target_pairs={{0,1},{1,0},{2,3},{3,2},{4,5},{5,4},{6,7},{7,6},{8,9},{9,8},{10,11... | collective-permute-start | bytes 786440 | tf_op jit(solution)/shard_map/ppermute | solution.py:282
  166.1 21.4 %collective-permute-start.10 = (bf16[128,1024]{1,0:T(8,128)(2,1)S(1)}, bf16[128,1024]{1,0:T(8,128)(2,1)S(1)}, u32[]{:S(2)}, u32[]{:S(2)}) collective-permute-start(bf16[128,1024]{1,0:T(8,128)(2,1)S(1)} %project.13), channel_id=1, source_target_pairs={{0,2},{1,3},{2,0},{3,1},{4,6},{5,7},{6,4},{7,5},{8,10},{9,11},{10,... | collective-permute-start | bytes 786440 | tf_op jit(solution)/shard_map/ppermute | solution.py:282
  170.0 16.8 %collective-permute-start.12 = (bf16[128,1024]{1,0:T(8,128)(2,1)S(1)}, bf16[128,1024]{1,0:T(8,128)(2,1)S(1)}, u32[]{:S(2)}, u32[]{:S(2)}) collective-permute-start(bf16[128,1024]{1,0:T(8,128)(2,1)S(1)} %project.15), channel_id=1, source_target_pairs={{0,2},{1,3},{2,0},{3,1},{4,6},{5,7},{6,4},{7,5},{8,10},{9,11},{10,... | collective-permute-start | bytes 786440 | tf_op jit(solution)/shard_map/ppermute | solution.py:282
  172.9 4.6 %copy-start.1 = (bf16[1024,1024]{1,0:T(8,128)(2,1)S(1)}, bf16[1024,1024]{1,0:T(8,128)(2,1)}, u32[]{:S(2)}) copy-start(bf16[1024,1024]{1,0:T(8,128)(2,1)} %copy-done) | copy-start | bytes 6291460
  172.9 15.4 %collective-permute-start.8 = (bf16[128,1024]{1,0:T(8,128)(2,1)S(1)}, bf16[128,1024]{1,0:T(8,128)(2,1)S(1)}, u32[]{:S(2)}, u32[]{:S(2)}) collective-permute-start(bf16[128,1024]{1,0:T(8,128)(2,1)S(1)} %project.11), channel_id=1, source_target_pairs={{0,2},{1,3},{2,0},{3,1},{4,6},{5,7},{6,4},{7,5},{8,10},{9,11},{10,... | collective-permute-start | bytes 786440 | tf_op jit(solution)/shard_map/ppermute | solution.py:282
  176.9 14.9 %collective-permute-start.6 = (bf16[128,1024]{1,0:T(8,128)(2,1)S(1)}, bf16[128,1024]{1,0:T(8,128)(2,1)S(1)}, u32[]{:S(2)}, u32[]{:S(2)}) collective-permute-start(bf16[128,1024]{1,0:T(8,128)(2,1)S(1)} %project.9), channel_id=1, source_target_pairs={{0,2},{1,3},{2,0},{3,1},{4,6},{5,7},{6,4},{7,5},{8,10},{9,11},{10,... | collective-permute-start | bytes 786440 | tf_op jit(solution)/shard_map/ppermute | solution.py:282

commit v3 on v2

v3 whole, which is shorter than its diff:
```python
import jax
import jax.numpy as jnp
from jax import lax
from jax.experimental import pallas as pl
from jax.experimental.pallas import tpu as pltpu
from jax.sharding import PartitionSpec as P

GROUP = 16
LANES = 128
BLK = 256
SEG = 256
CHUNK = 128
F32, BF16 = jnp.float32, jnp.bfloat16
VMEM_SPEC = pl.BlockSpec(memory_space=pltpu.VMEM)
HBM_SPEC = pl.BlockSpec(memory_space=pltpu.HBM)
ANY_SPEC = pl.BlockSpec(memory_space=pl.ANY)
PARAMS = pltpu.CompilerParams(vmem_limit_bytes=16 << 20)


COST = pl.CostEstimate(flops=1, bytes_accessed=1, transcendentals=0)


def in_hbm(x):
    return pltpu.with_memory_space_constraint(x, pltpu.HBM)


def shape(dims, dtype=F32):
    return jax.ShapeDtypeStruct(dims, dtype)


def split_bf16(x, parts):
    pieces = []
    for _ in range(parts):
        piece = x.astype(BF16)
        pieces.append(piece)
        x = x - piece.astype(F32)
    return pieces


def dot(a, b):
    return lax.dot_general(a, b, (((1,), (0,)), ((), ())), preferred_element_type=F32)


def group_mask(groups, modes, channels):
    dims = (groups, modes, channels)
    return lax.broadcasted_iota(jnp.int32, dims, 0) == (
        lax.broadcasted_iota(jnp.int32, dims, 2) // GROUP
    )


def column_of(table, first, groups):
    modes, width = table.shape
    rows = groups * modes
    spread = jnp.broadcast_to(table[None], (groups, modes, width)).reshape(rows, width)
    pick = lax.broadcasted_iota(jnp.int32, (rows, width), 1) == (
        lax.broadcasted_iota(jnp.int32, (rows, width), 0) // modes + first
    )
    return jnp.sum(jnp.where(pick, spread, 0.0), axis=1, keepdims=True)


def summary_kernel(
    k_hbm, v_hbm, rates_ref, residues_ref,
    sum_ref, rate_ref, residue_ref, flat_ref, u_ref,
    k_ref, v_ref, sems,
):
    tokens, channels = u_ref.shape
    modes = rates_ref.shape[0]
    groups = BLK // GROUP
    rows = groups * modes
    blocks = channels // BLK
    copies = []
    for block in range(blocks):
        lanes = pl.ds(block * BLK, BLK)
        for i, (src, dst) in enumerate(((k_hbm, k_ref), (v_hbm, v_ref))):
            copies.append(
                pltpu.make_async_copy(src.at[:, lanes], dst.at[:, lanes], sems.at[2 * block + i])
            )
            copies[-1].start()
    mask = group_mask(groups, modes, BLK)
    position = lax.broadcasted_iota(jnp.int32, (rows, SEG), 1).astype(F32)
    diagonal = lax.broadcasted_iota(jnp.int32, (rows, rows), 0) == lax.broadcasted_iota(
        jnp.int32, (rows, rows), 1
    )

    def store(ref, block, dense):
        kept = jnp.where(mask, dense.reshape(groups, modes, BLK), 0.0)
        table = jnp.sum(kept, axis=0)
        for tile in range(BLK // LANES):
            at = (block * (BLK // LANES) + tile) * modes
            ref[at : at + modes, :] = table[:, tile * LANES : (tile + 1) * LANES]

    for block in range(blocks):
        lanes = slice(block * BLK, (block + 1) * BLK)
        rate = column_of(rates_ref[...], block * groups, groups)
        residue = column_of(residues_ref[...], block * groups, groups)
        decay = split_bf16(jnp.exp(-rate * (SEG - 1.0 - position)), 3)
        carry = jnp.exp(-rate * float(SEG))
        store(rate_ref, block, jnp.broadcast_to(rate, (rows, BLK)))
        store(residue_ref, block, jnp.broadcast_to(residue, (rows, BLK)))
        flat_ref[:, block * rows : (block + 1) * rows] = jnp.sum(
            jnp.where(diagonal, jnp.broadcast_to(rate, (rows, rows)), 0.0), axis=0, keepdims=True
        )
        for copy in copies[2 * block : 2 * block + 2]:
            copy.wait()
        dense = None
        for at in range(0, tokens, SEG):
            part = slice(at, at + SEG)
            u = (k_ref[part, lanes].astype(F32) * v_ref[part, lanes].astype(F32)).astype(BF16)
            u_ref[part, lanes] = u
            here = dot(decay[2], u) + dot(decay[1], u) + dot(decay[0], u)
            dense = here if dense is None else dense * carry + here
        store(sum_ref, block, dense)


def summary_call(key_in, value, rates_t, residues_t):
    tokens, channels = key_in.shape
    modes = rates_t.shape[0]
    table = shape((channels // LANES * modes, LANES))
    return pl.pallas_call(
        summary_kernel,
        in_specs=[HBM_SPEC] * 2 + [VMEM_SPEC] * 2,
        out_specs=[VMEM_SPEC] * 5,
        out_shape=[
            table, table, table,
            shape((1, channels // GROUP * modes)),
            shape((tokens, channels), BF16),
        ],
        scratch_shapes=[
            pltpu.VMEM((tokens, channels), BF16),
            pltpu.VMEM((tokens, channels), BF16),
            pltpu.SemaphoreType.DMA((2 * channels // BLK,)),
        ],
        compiler_params=PARAMS,
        cost_estimate=COST,
        name="block_summary",
    )(in_hbm(key_in), in_hbm(value), rates_t, residues_t)


def local_kernel(
    chunk, modes, parts, started,
    u_in, rate_ref, residue_ref, skip_ref, q_hbm, weight_hbm, after_ref, *rest,
):
    carry_ref = rest[0] if started else None
    out_ref, end_ref, q_ref, *rest = rest[started:]
    u_ref, sems = rest[-2:]
    tiles = u_in.shape[1] // LANES
    rows = slice(chunk * CHUNK, (chunk + 1) * CHUNK)
    copies = [pltpu.make_async_copy(q_hbm.at[pl.ds(chunk * CHUNK, CHUNK), :], q_ref, sems.at[0])]
    if parts:
        me = lax.axis_index("tp")
        parts_ref = rest[0]
        depth, width = weight_hbm.shape[0], parts_ref.shape[1]
        for i, part in enumerate(parts):
            src = weight_hbm.at[:, pl.ds(pl.multiple_of((me ^ part) * width, width), width)]
            dst = parts_ref.at[pl.ds(i * depth, depth), :]
            copies.append(pltpu.make_async_copy(src, dst, sems.at[i + 1]))
    for copy in copies:
        copy.start()
    for tile in range(tiles):
        u = u_in[rows, tile * LANES : (tile + 1) * LANES]
        u_ref[tile * CHUNK : (tile + 1) * CHUNK, :] = u.astype(F32)
    decay = [jnp.exp(-rate_ref[pl.ds(m, tiles, stride=modes), :]) for m in range(modes)]
    residue = [residue_ref[pl.ds(m, tiles, stride=modes), :] for m in range(modes)]
    skip = skip_ref[...]

    def step(t, states):
        u = u_ref[pl.ds(t, tiles, stride=CHUNK), :]
        states = tuple(d * s + u for d, s in zip(decay, states))
        terms = [skip * u] + [r * s for r, s in zip(residue, states)]
        while len(terms) > 1:
            terms = [a + b for a, b in zip(terms[::2], terms[1::2])] + (
                [terms[-1]] if len(terms) % 2 else []
            )
        out_ref[pl.ds(t, tiles, stride=CHUNK), :] = terms[0]
        return states

    if started:
        first = tuple(carry_ref[m * tiles : (m + 1) * tiles, :] for m in range(modes))
    else:
        first = (jnp.zeros((tiles, LANES), F32),) * modes
    last = lax.fori_loop(0, CHUNK, step, first, unroll=4)
    for m in range(modes):
        end_ref[m * tiles : (m + 1) * tiles, :] = last[m]
    for copy in copies:
        copy.wait()


def local_call(chunk, parts, u, rate_table, residue_table, skip_tiles, query, weight, after, carry, width):
    channels = u.shape[1]
    tiles = channels // LANES
    modes = rate_table.shape[0] // tiles
    started = carry is not None
    return pl.pallas_call(
        lambda *refs: local_kernel(chunk, modes, parts, started, *refs),
        in_specs=[VMEM_SPEC] * 4 + [HBM_SPEC] * 2 + [ANY_SPEC] + [VMEM_SPEC] * started,
        out_specs=[VMEM_SPEC] * (3 + bool(parts)),
        out_shape=[
            shape((CHUNK * tiles, LANES)),
            shape((modes * tiles, LANES)),
            shape((CHUNK, channels), BF16),
        ]
        + [shape((len(parts) * channels, width), BF16)] * bool(parts),
        scratch_shapes=[
            pltpu.VMEM((tiles * CHUNK, LANES), F32),
            pltpu.SemaphoreType.DMA((1 + len(parts),)),
        ],
        compiler_params=PARAMS,
        cost_estimate=COST,
        name="local_conv",
    )(
        u, rate_table, residue_table, skip_tiles, in_hbm(query), in_hbm(weight), after,
        *([carry] if started else []),
    )


def double(span, tokens, rate, total, state, other):
    block = lax.axis_index("ctx")
    upper = (block & span) != 0
    before = ((block & (span - 1)) * tokens).astype(F32)
    state = jnp.where(upper, state + jnp.exp(-rate * before) * other, state)
    over = jnp.exp(-rate * float(span * tokens))
    total = jnp.where(upper, total + over * other, other + over * total)
    return total, state


def join_kernel(span, tokens, passed_ref, rate_ref, other_ref, total_ref, *refs):
    state = refs[0][...] if len(refs) == 4 else jnp.zeros(rate_ref.shape, F32)
    refs[-2][...], refs[-1][...] = double(
        span, tokens, rate_ref[...], total_ref[...], state, other_ref[...]
    )


def join_call(span, tokens, passed, rate_table, other, total, state):
    args = [passed, rate_table, other, total] + ([] if state is None else [state])
    return pl.pallas_call(
        lambda *refs: join_kernel(span, tokens, *refs),
        in_specs=[ANY_SPEC] + [VMEM_SPEC] * (len(args) - 1),
        out_specs=[ANY_SPEC] + [VMEM_SPEC] * 2,
        out_shape=[shape(passed.shape, passed.dtype)] + [shape(total.shape)] * 2,
        input_output_aliases={0: 0},
        compiler_params=PARAMS,
        cost_estimate=COST,
        name="join_blocks",
    )(*args)


def mix_kernel(chunk, modes, q_ref, local_ref, residue_ref, flat_ref, state_ref, after_ref, out_ref):
    groups = BLK // GROUP
    tiles = BLK // LANES
    rows = groups * modes
    mask = group_mask(groups, modes, BLK)
    since = lax.broadcasted_iota(jnp.int32, (CHUNK, rows), 0).astype(F32) + (chunk * CHUNK + 1.0)
    for block in range(q_ref.shape[1] // BLK):
        tile0 = block * tiles
        weighted = [
            state_ref[i * modes : (i + 1) * modes, :] * residue_ref[i * modes : (i + 1) * modes, :]
            for i in range(tile0, tile0 + tiles)
        ]
        spread = jnp.broadcast_to(jnp.concatenate(weighted, axis=1)[None], (groups, modes, BLK))
        spread = jnp.where(mask, spread, 0.0).reshape(rows, BLK)
        flat = flat_ref[:, block * rows : (block + 1) * rows]
        decay_hi, decay_lo = split_bf16(jnp.exp(-flat * since), 2)
        state_hi, state_lo = split_bf16(spread, 2)
        past = dot(decay_lo, state_hi) + dot(decay_hi, state_lo) + dot(decay_hi, state_hi)
        for tile in range(tiles):
            lanes = slice((tile0 + tile) * LANES, (tile0 + tile + 1) * LANES)
            conv = local_ref[(tile0 + tile) * CHUNK : (tile0 + tile + 1) * CHUNK, :]
            conv = conv + past[:, tile * LANES : (tile + 1) * LANES]
            out_ref[:, lanes] = (q_ref[:, lanes].astype(F32) * conv).astype(BF16)


def mix_call(chunk, query, local, residue_table, flat_rates, state, after):
    channels = query.shape[1]
    modes = flat_rates.shape[1] * GROUP // channels
    return pl.pallas_call(
        lambda *refs: mix_kernel(chunk, modes, *refs),
        in_specs=[VMEM_SPEC] * 5 + [ANY_SPEC],
        out_specs=VMEM_SPEC,
        out_shape=shape((CHUNK, channels), BF16),
        compiler_params=PARAMS,
        cost_estimate=COST,
        name="mix",
    )(query, local, residue_table, flat_rates, state, after)


def project_kernel(row, first, count, own_w_ref, pair_w_ref, *refs):
    cols = 256
    own_refs, pair_refs, out_ref = refs[:count], refs[count : 2 * count], refs[-1]
    rows_w = slice(row, row + own_refs[0].shape[1])
    for at in range(0, out_ref.shape[1], cols):
        lanes = slice(first + at, first + at + cols)
        for i, (own, pair) in enumerate(zip(own_refs, pair_refs)):
            total = dot(own[...], own_w_ref[rows_w, lanes]) + dot(pair[...], pair_w_ref[rows_w, lanes])
            rows = slice(i * CHUNK, (i + 1) * CHUNK)
            out_ref[rows, at : at + cols] = total.astype(out_ref.dtype)


def project_call(row, first, width, mixed, mixed_pair, weight, weight_pair, after, out_dtype):
    count = len(mixed)
    return pl.pallas_call(
        lambda *refs: project_kernel(row, first, count, *refs),
        in_specs=[VMEM_SPEC] * (2 + 2 * count) + [ANY_SPEC] * len(after),
        out_specs=VMEM_SPEC,
        out_shape=shape((CHUNK * count, width), out_dtype),
        compiler_params=PARAMS,
        cost_estimate=COST,
        name="project",
    )(weight, weight_pair, *mixed, *mixed_pair, *after)


def add_kernel(near_ref, *refs):
    out_ref = refs[-1]
    at = 0
    for ref in refs[:-1]:
        if ref.dtype == BF16 and ref.shape[0] == CHUNK:
            lanes = slice(at, at + ref.shape[1])
            out_ref[:, lanes] = (near_ref[:, lanes] + ref[...].astype(F32)).astype(BF16)
            at += ref.shape[1]


def add_call(chunk, near, arrived, out):
    tokens, width = near.shape
    args = [near, *arrived] + ([] if out is None else [out])
    row = lambda i: (chunk, 0)
    return pl.pallas_call(
        add_kernel,
        grid=(1,),
        in_specs=[pl.BlockSpec((CHUNK, width), row)]
        + [pl.BlockSpec(a.shape, lambda i: (0, 0)) for a in arrived]
        + [ANY_SPEC] * (out is not None),
        out_specs=pl.BlockSpec((CHUNK, width), row),
        out_shape=shape((tokens, width), BF16),
        input_output_aliases={} if out is None else {len(args) - 1: 0},
        compiler_params=PARAMS,
        cost_estimate=COST,
        name="add_arrived",
    )(*args)


def shards(query, key_in, value, rates, residues, skip_gain, out_weight, *, n_ctx, n_tp):
    tokens, channels = query.shape
    width = out_weight.shape[1] // n_tp
    chunks = tokens // CHUNK

    def swap(x, bit):
        return lax.ppermute(x, "tp", [(i, i ^ bit) for i in range(n_tp)])

    total, rate_table, residue_table, flat_rates, u = summary_call(
        key_in, value, rates.T, residues.T
    )
    skip_tiles = skip_gain.reshape(channels // LANES, LANES)
    local, q, parts = [], [], []

    def next_local(after, carry):
        chunk = len(local)
        wanted = {0: (3, 1), 1: (2, 0)}.get(chunk, ())
        out, carry, q_rows, *got = local_call(
            chunk, wanted, u, rate_table, residue_table, skip_tiles, query, out_weight, after, carry, width
        )
        local.append(out)
        q.append(q_rows)
        parts.extend(got)
        return carry

    state = carry = weight_pair = None
    span = 1
    while span < n_ctx:
        last = 2 * span >= n_ctx
        pairs = [(i, i ^ span) for i in range(n_ctx) if not (last and i & span)]
        other = lax.ppermute(total, "ctx", pairs)
        while len(local) < chunks:
            carry = next_local(total, carry)
            if not last:
                break
        passed = parts[0] if span == 1 else carry
        passed, total, state = join_call(span, tokens, passed, rate_table, other, total, state)
        if span == 1:
            weight_pair = swap(passed, 1)
        else:
            carry = passed
        span *= 2
    weight = parts[1]

    mixed, mixed_pair, after = [], [], carry
    for c in range(chunks):
        after = mix_call(c, q[c], local[c], residue_table, flat_rates, state, after)
        mixed.append(after)
        mixed_pair.append(swap(after, 1))
    arrived = []
    for c in range(chunks):
        pieces = 2 if c == 0 else 1
        arrived.append([])
        earlier = arrived[0] if c == chunks - 1 else []
        for piece in range(pieces):
            cols = width // pieces
            after = project_call(
                0, piece * cols, cols, mixed[c : c + 1], mixed_pair[c : c + 1], weight, weight_pair, [after, *earlier], BF16
            )
            arrived[c].append(swap(after, 2))
    here = project_call(channels, 0, width, mixed, mixed_pair, weight, weight_pair, [after], F32)
    out = None
    for c in range(chunks):
        out = add_call(c, here, arrived[c], out)
    return out


def solution(mesh):
    n_ctx, n_tp = mesh.shape["ctx"], mesh.shape["tp"]
    in_specs = (
        P("ctx", "tp"),
        P("ctx", "tp"),
        P("ctx", "tp"),
        P("tp", None),
        P("tp", None),
        P("tp"),
        P("tp", None),
    )

    def body(*args):
        return shards(*args, n_ctx=n_ctx, n_tp=n_tp)

    return jax.shard_map(body, mesh=mesh, in_specs=in_specs, out_specs=P("ctx", "tp"), check_vma=False)
```

time: 193 us -> 54 us (0.28)
  Pallas kernels: 158 us -> 22 us
  local copies, waits for them, and re-layouts: 11 us -> 2.09 us
  waiting for transfers between devices: 7.58 us -> 13.1 us
    pallas_call x17 -> x18, Pallas kernels: 156 us -> 20.2 us  [the longest x4 8.28 us: local_call(): pl.pallas_call(lambda *refs: local_kernel(chunk, modes, parts, started, *...]
    ppermute x10, waiting for transfers between devices: 2.71 us -> 12.5 us  [swap(): return lax.ppermute(x, 'tp', [(i, i ^ bit) for i in range(n_tp)])]
    unnamed x28 -> x8, local copies, waits for them, and re-layouts: 11 us -> 2.09 us
    ppermute x3, waiting for transfers between devices: 4.87 us -> 0.51 us  [shards(): other = lax.ppermute(total, 'ctx', pairs)]
  transfers between devices with their start and end apart: 13 -> 13, of which waited for: 3 -> 6; matrix products, arithmetic and copies ran while one was open for 0% -> 0% of each run, Pallas kernels for 81% -> 34%
where the time goes in v3:
time: 54 us; the launch traced here: 53.7 us
  Pallas kernels  22 us (41%)
  starting transfers between devices  16.3 us (30%)
  waiting for transfers between devices  13.1 us (24%)
  local copies, waits for them, and re-layouts  2.09 us (4%)
    ppermute x10, waiting for transfers between devices, swap(): return lax.ppermute(x, 'tp', [(i, i ^ bit) for i in range(n_tp)])  12.5 us
    ppermute x3, starting transfers between devices, shards(): other = lax.ppermute(total, 'ctx', pairs)  9.13 us
    pallas_call x4, Pallas kernels, local_call(): pl.pallas_call(lambda *refs: local_kernel(chunk, modes, parts, started, *...  8.28 us
    ppermute x10, starting transfers between devices, swap(): return lax.ppermute(x, 'tp', [(i, i ^ bit) for i in range(n_tp)])  7.18 us
    pallas_call x6, Pallas kernels, project_call(): pl.pallas_call(lambda *refs: project_kernel(row, first, count, *refs), in...  5.43 us
    pallas_call x4, Pallas kernels, add_call(): pl.pallas_call(add_kernel, grid=(1,), in_specs=[pl.BlockSpec((CHUNK, widt...  2.99 us
    pallas_call x1, Pallas kernels, summary_call(): pl.pallas_call(summary_kernel, in_specs=[HBM_SPEC] * 2 + [VMEM_SPEC] * 2,...  2.76 us
    unnamed x8, local copies, waits for them, and re-layouts  2.09 us
  transfers between devices with their start and end apart: 13, of which 6 were waited for; matrix products, arithmetic and copies ran while one was open for 0% of the time, Pallas kernels for 34%

profile of v3, /device:TPU:0, one launch (start us, length us, event | category | flops | bytes accessed | tf_op | source)
XLA Modules:
  0.0 53.7 jit_solution(8867837237470668530)
XLA Ops:
  0.0 0.0 copy-start.2
  0.0 0.7 %copy-done.2 = f32[64,16]{0,1:T(8,128)S(1)} copy-done((f32[64,16]{0,1:T(8,128)S(1)}, f32[64,16]{0,1:T(8,128)}, u32[]{:S(2)}) %copy-start.2) | copy-done | bytes 4120
  0.7 0.0 copy-start.3
  0.7 0.7 %copy-done.3 = f32[64,16]{0,1:T(8,128)S(1)} copy-done((f32[64,16]{0,1:T(8,128)S(1)}, f32[64,16]{0,1:T(8,128)}, u32[]{:S(2)}) %copy-start.3) | copy-done | bytes 4120
  1.4 2.8 %block_summary.1 = (f32[128,128]{1,0:T(8,128)S(1)}, f32[128,128]{1,0:T(8,128)S(1)}, f32[128,128]{1,0:T(8,128)S(1)}, f32[1,1024]{1,0:T(1,128)S(1)}, bf16[512,1024]{1,0:T(8,128)(2,1)S(1)}) custom-call(bf16[512,1024]{1,0:T(8,128)(2,1)} %k_hbm.1, bf16[512,1024]{1,0:T(8,128)(2,1)} %v_hbm.1, f32[16,64]{1,0:T(8,128)S(1)} %bitcast.7, f32[16,64]{1,0:T(8,128)S(1)} %bitcast.8), custom_call_target="tpu_custom_call" | custom-call | flops 1 | bytes 1 | tf_op jit(solution)/shard_map/block_summary/pallas_call | solution.py:119
  4.2 3.0 %collective-permute-start = (f32[128,128]{1,0:T(8,128)S(1)}, f32[128,128]{1,0:T(8,128)S(1)}, u32[]{:S(2)}, u32[]{:S(2)}) collective-permute-start(f32[128,128]{1,0:T(8,128)S(1)} %get-tuple-element.35.refs_6_.refs_3_), channel_id=1, source_target_pairs={{0,4},{4,0},{8,12},{12,8},{16,20},{20,16},{24,28},{28,24},{1,5},{5... | collective-permute-start | bytes 196616 | tf_op jit(solution)/shard_map/ppermute | solution.py:370
  7.2 0.0 copy-start
  7.2 0.7 %copy-done = f32[1024]{0:T(1024)S(1)} copy-done((f32[1024]{0:T(1024)S(1)}, f32[1024]{0:T(1024)}, u32[]{:S(2)}) %copy-start) | copy-done | bytes 4120
  7.9 2.4 %local_conv.4 = (f32[1024,128]{1,0:T(8,128)S(1)}, f32[128,128]{1,0:T(8,128)S(1)}, bf16[128,1024]{1,0:T(8,128)(2,1)S(1)}, bf16[2048,1024]{1,0:T(8,128)(2,1)S(1)}) custom-call(bf16[512,1024]{1,0:T(8,128)(2,1)S(1)} %get-tuple-element.32.refs_0_, f32[128,128]{1,0:T(8,128)S(1)} %get-tuple-element.33.refs_1_, f32[128,128]{1,0:T(8,128)S(1)} %get-tuple-element.34.refs_2_, ...), custom_call_target="tpu_custom_call" | custom-call | flops 1 | bytes 1 | tf_op jit(solution)/shard_map/local_conv/pallas_call | solution.py:193
  10.2 0.0 copy-start.1
  10.2 0.0 collective-permute-done.refs_2_
  10.3 0.1 collective-permute-start.1
  10.4 1.6 %collective-permute-start.2 = (f32[128,128]{1,0:T(8,128)S(1)}, f32[128,128]{1,0:T(8,128)S(1)}, u32[]{:S(2)}, u32[]{:S(2)}) collective-permute-start(f32[128,128]{1,0:T(8,128)S(1)} %get-tuple-element.37.refs_6_.refs_3_), channel_id=1, source_target_pairs={{0,8},{4,12},{8,0},{12,4},{16,24},{20,28},{24,16},{28,20},{1,9},{5... | collective-permute-start | bytes 196616 | tf_op jit(solution)/shard_map/ppermute | solution.py:370
  12.0 0.0 copy-done.1
  12.0 2.4 %local_conv.5 = (f32[1024,128]{1,0:T(8,128)S(1)}, f32[128,128]{1,0:T(8,128)S(1)}, bf16[128,1024]{1,0:T(8,128)(2,1)S(1)}, bf16[2048,1024]{1,0:T(8,128)(2,1)S(1)}) custom-call(bf16[512,1024]{1,0:T(8,128)(2,1)S(1)} %get-tuple-element.32.refs_0_, f32[128,128]{1,0:T(8,128)S(1)} %get-tuple-element.33.refs_1_, f32[128,128]{1,0:T(8,128)S(1)} %get-tuple-element.34.refs_2_, ...), custom_call_target="tpu_custom_call" | custom-call | flops 1 | bytes 1 | tf_op jit(solution)/shard_map/local_conv/pallas_call | solution.py:193
  14.4 0.5 collective-permute-done.2.refs_2_
  14.9 4.5 %collective-permute-start.3 = (f32[128,128]{1,0:T(8,128)S(1)}, f32[128,128]{1,0:T(8,128)S(1)}, u32[]{:S(2)}, u32[]{:S(2)}) collective-permute-start(f32[128,128]{1,0:T(8,128)S(1)} %get-tuple-element.46.refs_6_.refs_3_), channel_id=1, source_target_pairs={{0,16},{4,20},{8,24},{12,28},{1,17},{5,21},{9,25},{13,29},{2,18},{... | collective-permute-start | bytes 196616 | tf_op jit(solution)/shard_map/ppermute | solution.py:370
  19.4 1.8 %local_conv.6 = (f32[1024,128]{1,0:T(8,128)S(1)}, f32[128,128]{1,0:T(8,128)S(1)}, bf16[128,1024]{1,0:T(8,128)(2,1)S(1)}) custom-call(bf16[512,1024]{1,0:T(8,128)(2,1)S(1)} %get-tuple-element.32.refs_0_, f32[128,128]{1,0:T(8,128)S(1)} %get-tuple-element.33.refs_1_, f32[128,128]{1,0:T(8,128)S(1)} %get-tuple-element.34.refs_2_, f32[8,128]{1,0:T(8,128)S(1)} %bitcast.5, ...), custom_call_target="tpu_custom_call" | custom-call | flops 1 | bytes 1 | tf_op jit(solution)/shard_map/local_conv/pallas_call | solution.py:193
  21.2 1.8 %local_conv.7 = (f32[1024,128]{1,0:T(8,128)S(1)}, f32[128,128]{1,0:T(8,128)S(1)}, bf16[128,1024]{1,0:T(8,128)(2,1)S(1)}) custom-call(bf16[512,1024]{1,0:T(8,128)(2,1)S(1)} %get-tuple-element.32.refs_0_, f32[128,128]{1,0:T(8,128)S(1)} %get-tuple-element.33.refs_1_, f32[128,128]{1,0:T(8,128)S(1)} %get-tuple-element.34.refs_2_, f32[8,128]{1,0:T(8,128)S(1)} %bitcast.6, ...), custom_call_target="tpu_custom_call" | custom-call | flops 1 | bytes 1 | tf_op jit(solution)/shard_map/local_conv/pallas_call | solution.py:193
  23.0 0.0 collective-permute-done.3.refs_2_
  23.0 0.7 %join_blocks.5 = (f32[128,128]{1,0:T(8,128)S(1)}, f32[128,128]{1,0:T(8,128)}, f32[128,128]{1,0:T(8,128)S(1)}) custom-call(f32[128,128]{1,0:T(8,128)S(1)} %get-tuple-element.49.refs_0_, f32[128,128]{1,0:T(8,128)S(1)} %get-tuple-element.33.refs_1_, f32[128,128]{1,0:T(8,128)S(1)} %collective-permute-done.3.refs_2_, ...), custom_call_target="tpu_custom_call", output_to_operand_aliasing={{0}: (0, {})} | custom-call | flops 1 | bytes 1 | tf_op jit(solution)/shard_map/join_blocks/pallas_call | solution.py:235
  23.7 0.5 mix.4.refs_5_.refs_2_
  24.1 0.1 collective-permute-start.4
  24.2 0.5 mix.5.refs_5_.refs_2_.refs_3_
  24.7 0.6 %collective-permute-start.5 = (bf16[128,1024]{1,0:T(8,128)(2,1)S(1)}, bf16[128,1024]{1,0:T(8,128)(2,1)S(1)}, u32[]{:S(2)}, u32[]{:S(2)}) collective-permute-start(bf16[128,1024]{1,0:T(8,128)(2,1)S(1)} %mix.5.refs_5_.refs_2_.refs_3_), channel_id=1, source_target_pairs={{0,1},{1,0},{2,3},{3,2},{4,5},{5,4},{6,7},{7,6},{8,9},{9,8},{10,11... | collective-permute-start | bytes 786440 | tf_op jit(solution)/shard_map/ppermute | solution.py:346
  25.3 0.5 mix.6.refs_5_.refs_2_.refs_4_
  25.7 0.1 collective-permute-start.6
  25.8 0.4 mix.7.refs_4_.refs_2_.refs_5_
  26.2 0.6 %collective-permute-start.7 = (bf16[128,1024]{1,0:T(8,128)(2,1)S(1)}, bf16[128,1024]{1,0:T(8,128)(2,1)S(1)}, u32[]{:S(2)}, u32[]{:S(2)}) collective-permute-start(bf16[128,1024]{1,0:T(8,128)(2,1)S(1)} %mix.7.refs_4_.refs_2_.refs_5_), channel_id=1, source_target_pairs={{0,1},{1,0},{2,3},{3,2},{4,5},{5,4},{6,7},{7,6},{8,9},{9,8},{10,11... | collective-permute-start | bytes 786440 | tf_op jit(solution)/shard_map/ppermute | solution.py:346
  26.8 0.0 collective-permute-done.4.refs_3_.refs_6_
  26.8 0.0 collective-permute-done.1.refs_1_
  26.8 0.5 project.6.refs_4_
  27.3 0.5 project.7.refs_4_
  27.7 1.6 %collective-permute-start.9 = (bf16[128,512]{1,0:T(8,128)(2,1)S(1)}, bf16[128,512]{1,0:T(8,128)(2,1)S(1)}, u32[]{:S(2)}, u32[]{:S(2)}) collective-permute-start(bf16[128,512]{1,0:T(8,128)(2,1)S(1)} %project.7.refs_4_), channel_id=1, source_target_pairs={{0,2},{1,3},{2,0},{3,1},{4,6},{5,7},{6,4},{7,5},{8,10},{9,11},{10,... | collective-permute-start | bytes 393224 | tf_op jit(solution)/shard_map/ppermute | solution.py:346
  29.3 0.5 collective-permute-start.8
  29.8 0.0 collective-permute-done.5.refs_3_.refs_7_
  29.8 0.7 %project.8.refs_4_ = bf16[128,1024]{1,0:T(8,128)(2,1)S(1)} custom-call(bf16[2048,1024]{1,0:T(8,128)(2,1)S(1)} %get-tuple-element.39.refs_0_, bf16[2048,1024]{1,0:T(8,128)(2,1)S(1)} %collective-permute-done.1.refs_1_, bf16[128,1024]{1,0:T(8,128)(2,1)S(1)} %mix.5.refs_5_.refs_2_.refs_3_, bf16[128,1024]{1,0:T(8,128)(2,1)S(1)} %collective-permute-done.5.refs_3_.refs_7_, ...), custom_call_target="tpu_custom_call" | custom-call | flops 1 | bytes 1 | tf_op jit(solution)/shard_map/project/pallas_call | solution.py:300
  30.6 1.6 %collective-permute-start.12 = (bf16[128,1024]{1,0:T(8,128)(2,1)S(1)}, bf16[128,1024]{1,0:T(8,128)(2,1)S(1)}, u32[]{:S(2)}, u32[]{:S(2)}) collective-permute-start(bf16[128,1024]{1,0:T(8,128)(2,1)S(1)} %project.8.refs_4_), channel_id=1, source_target_pairs={{0,2},{1,3},{2,0},{3,1},{4,6},{5,7},{6,4},{7,5},{8,10},{9,11},{10,... | collective-permute-start | bytes 786440 | tf_op jit(solution)/shard_map/ppermute | solution.py:346
  32.2 0.0 collective-permute-done.6.refs_3_.refs_8_
  32.2 0.7 %project.9.refs_4_ = bf16[128,1024]{1,0:T(8,128)(2,1)S(1)} custom-call(bf16[2048,1024]{1,0:T(8,128)(2,1)S(1)} %get-tuple-element.39.refs_0_, bf16[2048,1024]{1,0:T(8,128)(2,1)S(1)} %collective-permute-done.1.refs_1_, bf16[128,1024]{1,0:T(8,128)(2,1)S(1)} %mix.6.refs_5_.refs_2_.refs_4_, bf16[128,1024]{1,0:T(8,128)(2,1)S(1)} %collective-permute-done.6.refs_3_.refs_8_, ...), custom_call_target="tpu_custom_call" | custom-call | flops 1 | bytes 1 | tf_op jit(solution)/shard_map/project/pallas_call | solution.py:300
  32.9 0.6 %collective-permute-start.11 = (bf16[128,1024]{1,0:T(8,128)(2,1)S(1)}, bf16[128,1024]{1,0:T(8,128)(2,1)S(1)}, u32[]{:S(2)}, u32[]{:S(2)}) collective-permute-start(bf16[128,1024]{1,0:T(8,128)(2,1)S(1)} %project.9.refs_4_), channel_id=1, source_target_pairs={{0,2},{1,3},{2,0},{3,1},{4,6},{5,7},{6,4},{7,5},{8,10},{9,11},{10,... | collective-permute-start | bytes 786440 | tf_op jit(solution)/shard_map/ppermute | solution.py:346
  33.5 0.0 collective-permute-done.7.refs_3_.refs_9_
  33.5 0.7 %collective-permute-done.9.refs_6_.refs_1_ = bf16[128,512]{1,0:T(8,128)(2,1)S(1)} collective-permute-done((bf16[128,512]{1,0:T(8,128)(2,1)S(1)}, bf16[128,512]{1,0:T(8,128)(2,1)S(1)}, u32[]{:S(2)}, u32[]{:S(2)}) %collective-permute-start.9) | collective-permute-done | bytes 131104 | tf_op jit(solution)/shard_map/ppermute | solution.py:346
  34.2 2.8 %collective-permute-done.8.refs_5_.refs_0_ = bf16[128,512]{1,0:T(8,128)(2,1)S(1)} collective-permute-done((bf16[128,512]{1,0:T(8,128)(2,1)S(1)}, bf16[128,512]{1,0:T(8,128)(2,1)S(1)}, u32[]{:S(2)}, u32[]{:S(2)}) %collective-permute-start.8) | collective-permute-done | bytes 131104 | tf_op jit(solution)/shard_map/ppermute | solution.py:346
  37.0 0.7 %project.10.refs_10_ = bf16[128,1024]{1,0:T(8,128)(2,1)S(1)} custom-call(bf16[2048,1024]{1,0:T(8,128)(2,1)S(1)} %get-tuple-element.39.refs_0_, bf16[2048,1024]{1,0:T(8,128)(2,1)S(1)} %collective-permute-done.1.refs_1_, bf16[128,1024]{1,0:T(8,128)(2,1)S(1)} %mix.7.refs_4_.refs_2_.refs_5_, bf16[128,1024]{1,0:T(8,128)(2,1)S(1)} %collective-permute-done.7.refs_3_.refs_9_, ...), custom_call_target="tpu_custom_call" | custom-call | flops 1 | bytes 1 | tf_op jit(solution)/shard_map/project/pallas_call | solution.py:300
  37.7 1.6 %collective-permute-start.10 = (bf16[128,1024]{1,0:T(8,128)(2,1)S(1)}, bf16[128,1024]{1,0:T(8,128)(2,1)S(1)}, u32[]{:S(2)}, u32[]{:S(2)}) collective-permute-start(bf16[128,1024]{1,0:T(8,128)(2,1)S(1)} %project.10.refs_10_), channel_id=1, source_target_pairs={{0,2},{1,3},{2,0},{3,1},{4,6},{5,7},{6,4},{7,5},{8,10},{9,11},{10,... | collective-permute-start | bytes 786440 | tf_op jit(solution)/shard_map/ppermute | solution.py:346
  39.3 2.3 %project.11.near_ref = f32[512,1024]{1,0:T(8,128)S(1)} custom-call(bf16[2048,1024]{1,0:T(8,128)(2,1)S(1)} %get-tuple-element.39.refs_0_, bf16[2048,1024]{1,0:T(8,128)(2,1)S(1)} %collective-permute-done.1.refs_1_, bf16[128,1024]{1,0:T(8,128)(2,1)S(1)} %mix.4.refs_5_.refs_2_, bf16[128,1024]{1,0:T(8,128)(2,1)S(1)} %mix.5.refs_5_.refs_2_.refs_3_, ...), custom_call_target="tpu_custom_call" | custom-call | flops 1 | bytes 1 | tf_op jit(solution)/shard_map/project/pallas_call | solution.py:300
  41.7 0.8 %add_arrived.4.refs_1_ = bf16[512,1024]{1,0:T(8,128)(2,1)} custom-call(f32[512,1024]{1,0:T(8,128)S(1)} %project.11.near_ref, bf16[128,512]{1,0:T(8,128)(2,1)S(1)} %collective-permute-done.8.refs_5_.refs_0_, bf16[128,512]{1,0:T(8,128)(2,1)S(1)} %collective-permute-done.9.refs_6_.refs_1_), custom_call_target="tpu_custom_call" | custom-call | flops 1 | bytes 1 | tf_op jit(solution)/shard_map/add_arrived/pallas_call | solution.py:325
  42.4 0.2 collective-permute-done.12.refs_0_
  42.6 0.7 %add_arrived.5.refs_1_ = bf16[512,1024]{1,0:T(8,128)(2,1)} custom-call(f32[512,1024]{1,0:T(8,128)S(1)} %project.11.near_ref, bf16[128,1024]{1,0:T(8,128)(2,1)S(1)} %collective-permute-done.12.refs_0_, bf16[512,1024]{1,0:T(8,128)(2,1)} %add_arrived.4.refs_1_), custom_call_target="tpu_custom_call", output_to_operand_aliasing={{}: (2, {})} | custom-call | flops 1 | bytes 1 | tf_op jit(solution)/shard_map/add_arrived/pallas_call | solution.py:325
  43.3 4.9 %collective-permute-done.11.refs_0_ = bf16[128,1024]{1,0:T(8,128)(2,1)S(1)} collective-permute-done((bf16[128,1024]{1,0:T(8,128)(2,1)S(1)}, bf16[128,1024]{1,0:T(8,128)(2,1)S(1)}, u32[]{:S(2)}, u32[]{:S(2)}) %collective-permute-start.11) | collective-permute-done | bytes 262176 | tf_op jit(solution)/shard_map/ppermute | solution.py:346
  48.2 0.7 %add_arrived.6.refs_1_ = bf16[512,1024]{1,0:T(8,128)(2,1)} custom-call(f32[512,1024]{1,0:T(8,128)S(1)} %project.11.near_ref, bf16[128,1024]{1,0:T(8,128)(2,1)S(1)} %collective-permute-done.11.refs_0_, bf16[512,1024]{1,0:T(8,128)(2,1)} %add_arrived.5.refs_1_), custom_call_target="tpu_custom_call", output_to_operand_aliasing={{}: (2, {})} | custom-call | flops 1 | bytes 1 | tf_op jit(solution)/shard_map/add_arrived/pallas_call | solution.py:325
  49.0 4.0 %collective-permute-done.10.refs_0_ = bf16[128,1024]{1,0:T(8,128)(2,1)S(1)} collective-permute-done((bf16[128,1024]{1,0:T(8,128)(2,1)S(1)}, bf16[128,1024]{1,0:T(8,128)(2,1)S(1)}, u32[]{:S(2)}, u32[]{:S(2)}) %collective-permute-start.10) | collective-permute-done | bytes 262176 | tf_op jit(solution)/shard_map/ppermute | solution.py:346
  52.9 0.7 %add_arrived.7 = bf16[512,1024]{1,0:T(8,128)(2,1)} custom-call(f32[512,1024]{1,0:T(8,128)S(1)} %project.11.near_ref, bf16[128,1024]{1,0:T(8,128)(2,1)S(1)} %collective-permute-done.10.refs_0_, bf16[512,1024]{1,0:T(8,128)(2,1)} %add_arrived.6.refs_1_), custom_call_target="tpu_custom_call", output_to_operand_aliasing={{}: (2, {})} | custom-call | flops 1 | bytes 1 | tf_op jit(solution)/shard_map/add_arrived/pallas_call | solution.py:325
  (2 shorter events, 0.1 us)
Async XLA Ops:
  0.0 0.7 %copy-start.2 = (f32[64,16]{0,1:T(8,128)S(1)}, f32[64,16]{0,1:T(8,128)}, u32[]{:S(2)}) copy-start(f32[64,16]{0,1:T(8,128)} %param.10) | copy-start | bytes 12292
  0.7 0.7 %copy-start.3 = (f32[64,16]{0,1:T(8,128)S(1)}, f32[64,16]{0,1:T(8,128)}, u32[]{:S(2)}) copy-start(f32[64,16]{0,1:T(8,128)} %param.11) | copy-start | bytes 12292
  4.2 6.1 %collective-permute-start = (f32[128,128]{1,0:T(8,128)S(1)}, f32[128,128]{1,0:T(8,128)S(1)}, u32[]{:S(2)}, u32[]{:S(2)}) collective-permute-start(f32[128,128]{1,0:T(8,128)S(1)} %get-tuple-element.35.refs_6_.refs_3_), channel_id=1, source_target_pairs={{0,4},{4,0},{8,12},{12,8},{16,20},{20,16},{24,28},{28,24},{1,5},{5... | collective-permute-start | bytes 196616 | tf_op jit(solution)/shard_map/ppermute | solution.py:370
  7.2 0.7 %copy-start = (f32[1024]{0:T(1024)S(1)}, f32[1024]{0:T(1024)}, u32[]{:S(2)}) copy-start(f32[1024]{0:T(1024)} %param.12) | copy-start | bytes 12292
  10.2 1.8 %copy-start.1 = (f32[1024]{0:T(1024)S(1)}, f32[1024]{0:T(1024)}, u32[]{:S(2)}) copy-start(f32[1024]{0:T(1024)} %param.12) | copy-start | bytes 12292
  10.3 16.5 %collective-permute-start.1 = (bf16[2048,1024]{1,0:T(8,128)(2,1)S(1)}, bf16[2048,1024]{1,0:T(8,128)(2,1)S(1)}, u32[]{:S(2)}, u32[]{:S(2)}) collective-permute-start(bf16[2048,1024]{1,0:T(8,128)(2,1)S(1)} %get-tuple-element.40), channel_id=1, source_target_pairs={{0,1},{1,0},{2,3},{3,2},{4,5},{5,4},{6,7},{7,6},{8,9},{9,8},{10,11... | collective-permute-start | bytes 12582920 | tf_op jit(solution)/shard_map/ppermute | solution.py:346
  10.4 4.5 %collective-permute-start.2 = (f32[128,128]{1,0:T(8,128)S(1)}, f32[128,128]{1,0:T(8,128)S(1)}, u32[]{:S(2)}, u32[]{:S(2)}) collective-permute-start(f32[128,128]{1,0:T(8,128)S(1)} %get-tuple-element.37.refs_6_.refs_3_), channel_id=1, source_target_pairs={{0,8},{4,12},{8,0},{12,4},{16,24},{20,28},{24,16},{28,20},{1,9},{5... | collective-permute-start | bytes 196616 | tf_op jit(solution)/shard_map/ppermute | solution.py:370
  14.9 8.1 %collective-permute-start.3 = (f32[128,128]{1,0:T(8,128)S(1)}, f32[128,128]{1,0:T(8,128)S(1)}, u32[]{:S(2)}, u32[]{:S(2)}) collective-permute-start(f32[128,128]{1,0:T(8,128)S(1)} %get-tuple-element.46.refs_6_.refs_3_), channel_id=1, source_target_pairs={{0,16},{4,20},{8,24},{12,28},{1,17},{5,21},{9,25},{13,29},{2,18},{... | collective-permute-start | bytes 196616 | tf_op jit(solution)/shard_map/ppermute | solution.py:370
  24.1 2.7 %collective-permute-start.4 = (bf16[128,1024]{1,0:T(8,128)(2,1)S(1)}, bf16[128,1024]{1,0:T(8,128)(2,1)S(1)}, u32[]{:S(2)}, u32[]{:S(2)}) collective-permute-start(bf16[128,1024]{1,0:T(8,128)(2,1)S(1)} %mix.4.refs_5_.refs_2_), channel_id=1, source_target_pairs={{0,1},{1,0},{2,3},{3,2},{4,5},{5,4},{6,7},{7,6},{8,9},{9,8},{10,11... | collective-permute-start | bytes 786440 | tf_op jit(solution)/shard_map/ppermute | solution.py:346
  24.7 5.2 %collective-permute-start.5 = (bf16[128,1024]{1,0:T(8,128)(2,1)S(1)}, bf16[128,1024]{1,0:T(8,128)(2,1)S(1)}, u32[]{:S(2)}, u32[]{:S(2)}) collective-permute-start(bf16[128,1024]{1,0:T(8,128)(2,1)S(1)} %mix.5.refs_5_.refs_2_.refs_3_), channel_id=1, source_target_pairs={{0,1},{1,0},{2,3},{3,2},{4,5},{5,4},{6,7},{7,6},{8,9},{9,8},{10,11... | collective-permute-start | bytes 786440 | tf_op jit(solution)/shard_map/ppermute | solution.py:346
  25.7 6.5 %collective-permute-start.6 = (bf16[128,1024]{1,0:T(8,128)(2,1)S(1)}, bf16[128,1024]{1,0:T(8,128)(2,1)S(1)}, u32[]{:S(2)}, u32[]{:S(2)}) collective-permute-start(bf16[128,1024]{1,0:T(8,128)(2,1)S(1)} %mix.6.refs_5_.refs_2_.refs_4_), channel_id=1, source_target_pairs={{0,1},{1,0},{2,3},{3,2},{4,5},{5,4},{6,7},{7,6},{8,9},{9,8},{10,11... | collective-permute-start | bytes 786440 | tf_op jit(solution)/shard_map/ppermute | solution.py:346
  26.2 7.2 %collective-permute-start.7 = (bf16[128,1024]{1,0:T(8,128)(2,1)S(1)}, bf16[128,1024]{1,0:T(8,128)(2,1)S(1)}, u32[]{:S(2)}, u32[]{:S(2)}) collective-permute-start(bf16[128,1024]{1,0:T(8,128)(2,1)S(1)} %mix.7.refs_4_.refs_2_.refs_5_), channel_id=1, source_target_pairs={{0,1},{1,0},{2,3},{3,2},{4,5},{5,4},{6,7},{7,6},{8,9},{9,8},{10,11... | collective-permute-start | bytes 786440 | tf_op jit(solution)/shard_map/ppermute | solution.py:346
  27.7 6.4 %collective-permute-start.9 = (bf16[128,512]{1,0:T(8,128)(2,1)S(1)}, bf16[128,512]{1,0:T(8,128)(2,1)S(1)}, u32[]{:S(2)}, u32[]{:S(2)}) collective-permute-start(bf16[128,512]{1,0:T(8,128)(2,1)S(1)} %project.7.refs_4_), channel_id=1, source_target_pairs={{0,2},{1,3},{2,0},{3,1},{4,6},{5,7},{6,4},{7,5},{8,10},{9,11},{10,... | collective-permute-start | bytes 393224 | tf_op jit(solution)/shard_map/ppermute | solution.py:346
  29.3 7.6 %collective-permute-start.8 = (bf16[128,512]{1,0:T(8,128)(2,1)S(1)}, bf16[128,512]{1,0:T(8,128)(2,1)S(1)}, u32[]{:S(2)}, u32[]{:S(2)}) collective-permute-start(bf16[128,512]{1,0:T(8,128)(2,1)S(1)} %project.6.refs_4_), channel_id=1, source_target_pairs={{0,2},{1,3},{2,0},{3,1},{4,6},{5,7},{6,4},{7,5},{8,10},{9,11},{10,... | collective-permute-start | bytes 393224 | tf_op jit(solution)/shard_map/ppermute | solution.py:346
  30.6 12.0 %collective-permute-start.12 = (bf16[128,1024]{1,0:T(8,128)(2,1)S(1)}, bf16[128,1024]{1,0:T(8,128)(2,1)S(1)}, u32[]{:S(2)}, u32[]{:S(2)}) collective-permute-start(bf16[128,1024]{1,0:T(8,128)(2,1)S(1)} %project.8.refs_4_), channel_id=1, source_target_pairs={{0,2},{1,3},{2,0},{3,1},{4,6},{5,7},{6,4},{7,5},{8,10},{9,11},{10,... | collective-permute-start | bytes 786440 | tf_op jit(solution)/shard_map/ppermute | solution.py:346
  32.9 15.3 %collective-permute-start.11 = (bf16[128,1024]{1,0:T(8,128)(2,1)S(1)}, bf16[128,1024]{1,0:T(8,128)(2,1)S(1)}, u32[]{:S(2)}, u32[]{:S(2)}) collective-permute-start(bf16[128,1024]{1,0:T(8,128)(2,1)S(1)} %project.9.refs_4_), channel_id=1, source_target_pairs={{0,2},{1,3},{2,0},{3,1},{4,6},{5,7},{6,4},{7,5},{8,10},{9,11},{10,... | collective-permute-start | bytes 786440 | tf_op jit(solution)/shard_map/ppermute | solution.py:346
  37.7 15.2 %collective-permute-start.10 = (bf16[128,1024]{1,0:T(8,128)(2,1)S(1)}, bf16[128,1024]{1,0:T(8,128)(2,1)S(1)}, u32[]{:S(2)}, u32[]{:S(2)}) collective-permute-start(bf16[128,1024]{1,0:T(8,128)(2,1)S(1)} %project.10.refs_10_), channel_id=1, source_target_pairs={{0,2},{1,3},{2,0},{3,1},{4,6},{5,7},{6,4},{7,5},{8,10},{9,11},{10,... | collective-permute-start | bytes 786440 | tf_op jit(solution)/shard_map/ppermute | solution.py:346

commit v4 on v3

v4 whole, which is shorter than its diff:
```python
import jax
import jax.numpy as jnp
from jax import lax
from jax.experimental import pallas as pl
from jax.experimental.pallas import tpu as pltpu
from jax.sharding import PartitionSpec as P

GROUP = 16
LANES = 128
BLK = 256
SEG = 256
CHUNK = 128
F32, BF16 = jnp.float32, jnp.bfloat16
VMEM_SPEC = pl.BlockSpec(memory_space=pltpu.VMEM)
HBM_SPEC = pl.BlockSpec(memory_space=pltpu.HBM)
ANY_SPEC = pl.BlockSpec(memory_space=pl.ANY)
PARAMS = pltpu.CompilerParams(vmem_limit_bytes=16 << 20)


COST = pl.CostEstimate(flops=1, bytes_accessed=1, transcendentals=0)


def in_hbm(x):
    return pltpu.with_memory_space_constraint(x, pltpu.HBM)


def shape(dims, dtype=F32):
    return jax.ShapeDtypeStruct(dims, dtype)


def split_bf16(x, parts):
    pieces = []
    for _ in range(parts):
        piece = x.astype(BF16)
        pieces.append(piece)
        x = x - piece.astype(F32)
    return pieces


def dot(a, b):
    return lax.dot_general(a, b, (((1,), (0,)), ((), ())), preferred_element_type=F32)


def group_mask(groups, modes, channels):
    dims = (groups, modes, channels)
    return lax.broadcasted_iota(jnp.int32, dims, 0) == (
        lax.broadcasted_iota(jnp.int32, dims, 2) // GROUP
    )


def column_of(table, first, groups):
    modes, width = table.shape
    rows = groups * modes
    spread = jnp.broadcast_to(table[None], (groups, modes, width)).reshape(rows, width)
    pick = lax.broadcasted_iota(jnp.int32, (rows, width), 1) == (
        lax.broadcasted_iota(jnp.int32, (rows, width), 0) // modes + first
    )
    return jnp.sum(jnp.where(pick, spread, 0.0), axis=1, keepdims=True)


def summary_kernel(
    k_hbm, v_hbm, rates_hbm, residues_hbm, skip_hbm,
    sum_ref, rate_ref, residue_ref, flat_ref, u_ref, skip_ref,
    k_ref, v_ref, rates_ref, residues_ref, decay_ref, sems,
):
    tokens, channels = u_ref.shape
    modes = rates_ref.shape[0]
    groups = BLK // GROUP
    rows = groups * modes
    blocks = channels // BLK
    tiles = BLK // LANES
    segments = tokens // SEG
    small = [
        pltpu.make_async_copy(src, dst, sems.at[i])
        for i, (src, dst) in enumerate(
            ((rates_hbm, rates_ref), (residues_hbm, residues_ref), (skip_hbm, skip_ref))
        )
    ]
    large = []
    for seg in range(segments):
        part = pl.ds(seg * SEG, SEG)
        for i, (src, dst) in enumerate(((k_hbm, k_ref), (v_hbm, v_ref))):
            sem = sems.at[len(small) + 2 * seg + i]
            large.append(pltpu.make_async_copy(src.at[part, :], dst.at[part, :], sem))
    for copy in small + large:
        copy.start()
    for copy in small:
        copy.wait()
    mask = group_mask(groups, modes, BLK)
    position = lax.broadcasted_iota(jnp.int32, (rows, SEG), 1).astype(F32)
    diagonal = lax.broadcasted_iota(jnp.int32, (rows, rows), 0) == lax.broadcasted_iota(
        jnp.int32, (rows, rows), 1
    )

    def compact(dense):
        return jnp.sum(jnp.where(mask, dense.reshape(groups, modes, BLK), 0.0), axis=0)

    def tile_rows(block, tile):
        at = (block * tiles + tile) * modes
        return slice(at, at + modes), slice(tile * LANES, (tile + 1) * LANES)

    for block in range(blocks):
        rate = column_of(rates_ref[...], block * groups, groups)
        residue = column_of(residues_ref[...], block * groups, groups)
        hi, lo = split_bf16(jnp.exp(-rate * (SEG - 1.0 - position)), 2)
        decay_ref[2 * block * rows : (2 * block + 1) * rows, :] = hi
        decay_ref[(2 * block + 1) * rows : (2 * block + 2) * rows, :] = lo
        flat_ref[:, block * rows : (block + 1) * rows] = jnp.sum(
            jnp.where(diagonal, jnp.broadcast_to(rate, (rows, rows)), 0.0), axis=0, keepdims=True
        )
        for ref, column in ((rate_ref, rate), (residue_ref, residue)):
            table = compact(jnp.broadcast_to(column, (rows, BLK)))
            for tile in range(tiles):
                at, lanes = tile_rows(block, tile)
                ref[at, :] = table[:, lanes]
    for seg in range(segments):
        part = slice(seg * SEG, (seg + 1) * SEG)
        for copy in large[2 * seg : 2 * seg + 2]:
            copy.wait()
        for block in range(blocks):
            lanes = slice(block * BLK, (block + 1) * BLK)
            u = (k_ref[part, lanes].astype(F32) * v_ref[part, lanes].astype(F32)).astype(BF16)
            u_ref[part, lanes] = u
            both = dot(decay_ref[2 * block * rows : (2 * block + 2) * rows, :], u)
            here = compact(both[:rows] + both[rows:])
            for tile in range(tiles):
                at, lanes = tile_rows(block, tile)
                part_sum = here[:, lanes]
                if seg:
                    part_sum = part_sum + jnp.exp(-rate_ref[at, :] * float(SEG)) * sum_ref[at, :]
                sum_ref[at, :] = part_sum


def summary_call(key_in, value, rates_t, residues_t, skip_tiles):
    tokens, channels = key_in.shape
    modes = rates_t.shape[0]
    table = shape((channels // LANES * modes, LANES))
    return pl.pallas_call(
        summary_kernel,
        in_specs=[HBM_SPEC] * 5,
        out_specs=[VMEM_SPEC] * 6,
        out_shape=[
            table, table, table,
            shape((1, channels // GROUP * modes)),
            shape((tokens, channels), BF16),
            shape(skip_tiles.shape),
        ],
        scratch_shapes=[
            pltpu.VMEM((tokens, channels), BF16),
            pltpu.VMEM((tokens, channels), BF16),
            pltpu.VMEM(rates_t.shape, F32),
            pltpu.VMEM(rates_t.shape, F32),
            pltpu.VMEM((2 * channels // GROUP * modes, SEG), BF16),
            pltpu.SemaphoreType.DMA((3 + 2 * tokens // SEG,)),
        ],
        compiler_params=PARAMS,
        cost_estimate=COST,
        name="block_summary",
    )(*[in_hbm(x) for x in (key_in, value, rates_t, residues_t, skip_tiles)])


def local_kernel(
    begin, count, modes, parts, started,
    u_in, rate_ref, residue_ref, skip_ref, q_hbm, weight_hbm, *rest,
):
    carry_ref = rest[1] if started else None
    out_ref, end_ref, q_ref, *rest = rest[1 + started :]
    u_ref, sems = rest[-2:]
    tiles = u_in.shape[1] // LANES
    rows = slice(begin, begin + count)
    copies = [pltpu.make_async_copy(q_hbm.at[pl.ds(begin, count), :], q_ref, sems.at[0])]
    if parts:
        me = lax.axis_index("tp")
        parts_ref = rest[0]
        depth, width = weight_hbm.shape[0], parts_ref.shape[1]
        for i, part in enumerate(parts):
            src = weight_hbm.at[:, pl.ds(pl.multiple_of((me ^ part) * width, width), width)]
            dst = parts_ref.at[pl.ds(i * depth, depth), :]
            copies.append(pltpu.make_async_copy(src, dst, sems.at[i + 1]))
    for copy in copies:
        copy.start()
    for tile in range(tiles):
        u = u_in[rows, tile * LANES : (tile + 1) * LANES]
        u_ref[tile * count : (tile + 1) * count, :] = u.astype(F32)
    decay = [jnp.exp(-rate_ref[pl.ds(m, tiles, stride=modes), :]) for m in range(modes)]
    residue = [residue_ref[pl.ds(m, tiles, stride=modes), :] for m in range(modes)]
    skip = skip_ref[...]

    def step(t, states):
        u = u_ref[pl.ds(t, tiles, stride=count), :]
        states = tuple(d * s + u for d, s in zip(decay, states))
        terms = [skip * u] + [r * s for r, s in zip(residue, states)]
        while len(terms) > 1:
            terms = [a + b for a, b in zip(terms[::2], terms[1::2])] + (
                [terms[-1]] if len(terms) % 2 else []
            )
        out_ref[pl.ds(t, tiles, stride=count), :] = terms[0]
        return states

    if started:
        first = tuple(carry_ref[m * tiles : (m + 1) * tiles, :] for m in range(modes))
    else:
        first = (jnp.zeros((tiles, LANES), F32),) * modes
    last = lax.fori_loop(0, count, step, first, unroll=4)
    for m in range(modes):
        end_ref[m * tiles : (m + 1) * tiles, :] = last[m]
    for copy in copies:
        copy.wait()


def local_call(
    begin, count, parts, u, rate_table, residue_table, skip_tiles, query, weight, after, carry, width
):
    channels = u.shape[1]
    tiles = channels // LANES
    modes = rate_table.shape[0] // tiles
    started = carry is not None
    return pl.pallas_call(
        lambda *refs: local_kernel(begin, count, modes, parts, started, *refs),
        in_specs=[VMEM_SPEC] * 4 + [HBM_SPEC] * 2 + [ANY_SPEC] + [VMEM_SPEC] * started,
        out_specs=[VMEM_SPEC] * (3 + bool(parts)),
        out_shape=[
            shape((count * tiles, LANES)),
            shape((modes * tiles, LANES)),
            shape((count, channels), BF16),
        ]
        + [shape((len(parts) * channels, width), BF16)] * bool(parts),
        scratch_shapes=[
            pltpu.VMEM((tiles * count, LANES), F32),
            pltpu.SemaphoreType.DMA((1 + len(parts),)),
        ],
        compiler_params=PARAMS,
        cost_estimate=COST,
        name="local_conv",
    )(
        u, rate_table, residue_table, skip_tiles, in_hbm(query), in_hbm(weight), after,
        *([carry] if started else []),
    )


def double(span, tokens, rate, total, state, other):
    block = lax.axis_index("ctx")
    upper = (block & span) != 0
    before = ((block & (span - 1)) * tokens).astype(F32)
    state = jnp.where(upper, state + jnp.exp(-rate * before) * other, state)
    over = jnp.exp(-rate * float(span * tokens))
    total = jnp.where(upper, total + over * other, other + over * total)
    return total, state


def join_kernel(span, tokens, started, last, passed_ref, rate_ref, other_ref, total_ref, *refs):
    state = refs[0][...] if started else jnp.zeros(rate_ref.shape, F32)
    total, state = double(span, tokens, rate_ref[...], total_ref[...], state, other_ref[...])
    refs[-1][...] = state
    if not last:
        refs[-2][...] = total


def join_call(span, tokens, last, passed, rate_table, other, total, state):
    started = state is not None
    return pl.pallas_call(
        lambda *refs: join_kernel(span, tokens, started, last, *refs),
        in_specs=[ANY_SPEC] + [VMEM_SPEC] * (3 + started),
        out_specs=[ANY_SPEC] + [VMEM_SPEC] * (1 + (not last)),
        out_shape=[shape(passed.shape, passed.dtype)] + [shape(total.shape)] * (1 + (not last)),
        input_output_aliases={0: 0},
        compiler_params=PARAMS,
        cost_estimate=COST,
        name="join_blocks",
    )(passed, rate_table, other, total, *([state] if started else []))


def mix_kernel(begin, modes, outs, residue_ref, flat_ref, state_ref, after_ref, *refs):
    pieces, out_refs = list(zip(refs[:-outs:2], refs[1:-outs:2])), refs[-outs:]
    groups = BLK // GROUP
    tiles = BLK // LANES
    rows = groups * modes
    tokens = sum(ref.shape[0] for ref in out_refs)
    mask = group_mask(groups, modes, BLK)
    since = lax.broadcasted_iota(jnp.int32, (tokens, rows), 0).astype(F32) + (begin + 1.0)
    for block in range(out_refs[0].shape[1] // BLK):
        tile0 = block * tiles
        weighted = [
            state_ref[i * modes : (i + 1) * modes, :] * residue_ref[i * modes : (i + 1) * modes, :]
            for i in range(tile0, tile0 + tiles)
        ]
        spread = jnp.broadcast_to(jnp.concatenate(weighted, axis=1)[None], (groups, modes, BLK))
        spread = jnp.where(mask, spread, 0.0).reshape(rows, BLK)
        flat = flat_ref[:, block * rows : (block + 1) * rows]
        decay_hi, decay_lo = split_bf16(jnp.exp(-flat * since), 2)
        state_hi, state_lo = split_bf16(spread, 2)
        past = dot(decay_lo, state_hi) + dot(decay_hi, state_lo) + dot(decay_hi, state_hi)
        at = 0
        for q_ref, local_ref in pieces:
            count = q_ref.shape[0]
            for tile in range(tiles):
                lanes = slice((tile0 + tile) * LANES, (tile0 + tile + 1) * LANES)
                conv = local_ref[(tile0 + tile) * count : (tile0 + tile + 1) * count, :]
                conv = conv + past[at : at + count, tile * LANES : (tile + 1) * LANES]
                mixed = (q_ref[:, lanes].astype(F32) * conv).astype(BF16)
                first = 0
                for out_ref in out_refs:
                    last = first + out_ref.shape[0]
                    lo, hi = max(first, at), min(last, at + count)
                    if lo < hi:
                        out_ref[lo - first : hi - first, lanes] = mixed[lo - at : hi - at]
                    first = last
            at += count


def mix_call(begin, sizes, query, local, residue_table, flat_rates, state, after):
    channels = query[0].shape[1]
    modes = flat_rates.shape[1] * GROUP // channels
    pieces = [x for pair in zip(query, local) for x in pair]
    return pl.pallas_call(
        lambda *refs: mix_kernel(begin, modes, len(sizes), *refs),
        in_specs=[VMEM_SPEC] * 3 + [ANY_SPEC] + [VMEM_SPEC] * len(pieces),
        out_specs=[VMEM_SPEC] * len(sizes),
        out_shape=[shape((size, channels), BF16) for size in sizes],
        compiler_params=PARAMS,
        cost_estimate=COST,
        name="mix",
    )(residue_table, flat_rates, state, after, *pieces)


def project_kernel(row, pieces, own_w_ref, pair_w_ref, *refs):
    cols = 256
    count = len(pieces)
    own_refs, pair_refs, out_ref = refs[:count], refs[count : 2 * count], refs[-1]
    rows_w = slice(row, row + own_refs[0].shape[1])
    for first in range(0, out_ref.shape[1], cols):
        lanes = slice(first, first + cols)
        at = 0
        for own, pair, (begin, tokens) in zip(own_refs, pair_refs, pieces):
            rows = slice(begin, begin + tokens)
            total = dot(own[rows, :], own_w_ref[rows_w, lanes])
            total = total + dot(pair[rows, :], pair_w_ref[rows_w, lanes])
            out_ref[at : at + tokens, lanes] = total.astype(out_ref.dtype)
            at += tokens


def project_call(row, pieces, mixed, mixed_pair, weight, weight_pair, after, out_dtype):
    return pl.pallas_call(
        lambda *refs: project_kernel(row, pieces, *refs),
        in_specs=[VMEM_SPEC] * (2 + 2 * len(mixed)) + [ANY_SPEC] * len(after),
        out_specs=VMEM_SPEC,
        out_shape=shape((sum(tokens for _, tokens in pieces), weight.shape[1]), out_dtype),
        compiler_params=PARAMS,
        cost_estimate=COST,
        name="project",
    )(weight, weight_pair, *mixed, *mixed_pair, *after)


def add_kernel(near_ref, *refs):
    out_ref = refs[-1]
    at = 0
    for ref in refs[:-1]:
        if ref.dtype == BF16 and ref.shape[0] == CHUNK:
            lanes = slice(at, at + ref.shape[1])
            out_ref[:, lanes] = (near_ref[:, lanes] + ref[...].astype(F32)).astype(BF16)
            at += ref.shape[1]


def add_call(chunk, near, arrived, out):
    tokens, width = near.shape
    args = [near, *arrived] + ([] if out is None else [out])
    row = lambda i: (chunk, 0)
    return pl.pallas_call(
        add_kernel,
        grid=(1,),
        in_specs=[pl.BlockSpec((CHUNK, width), row)]
        + [pl.BlockSpec(a.shape, lambda i: (0, 0)) for a in arrived]
        + [ANY_SPEC] * (out is not None),
        out_specs=pl.BlockSpec((CHUNK, width), row),
        out_shape=shape((tokens, width), BF16),
        input_output_aliases={} if out is None else {len(args) - 1: 0},
        compiler_params=PARAMS,
        cost_estimate=COST,
        name="add_arrived",
    )(*args)


def shards(query, key_in, value, rates, residues, skip_gain, out_weight, *, n_ctx, n_tp):
    tokens, channels = query.shape
    width = out_weight.shape[1] // n_tp
    chunks = tokens // CHUNK

    def swap(x, bit):
        return lax.ppermute(x, "tp", [(i, i ^ bit) for i in range(n_tp)])

    skip_tiles = skip_gain.reshape(channels // LANES, LANES)
    total, rate_table, residue_table, flat_rates, u, skip_tiles = summary_call(
        key_in, value, rates.T, residues.T, skip_tiles
    )
    sizes = [CHUNK] + [(tokens - CHUNK) // 2] * 2
    local, q, parts = [], [], []

    def next_local(after, carry):
        index = len(local)
        wanted = {0: (3, 1), 1: (2, 0)}.get(index, ())
        out, carry, q_rows, *got = local_call(
            sum(sizes[:index]), sizes[index], wanted, u, rate_table, residue_table, skip_tiles,
            query, out_weight, after, carry, width,
        )
        local.append(out)
        q.append(q_rows)
        parts.extend(got)
        return carry

    state = carry = weight_pair = None
    span = 1
    while span < n_ctx:
        other = lax.ppermute(total, "ctx", [(i, i ^ span) for i in range(n_ctx)])
        if len(local) < len(sizes):
            carry = next_local(total, carry)
        last = 2 * span >= n_ctx
        passed = parts[0] if span == 1 else carry
        passed, *ends, state = join_call(span, tokens, last, passed, rate_table, other, total, state)
        if span == 1:
            weight_pair = swap(passed, 1)
        else:
            carry = passed
        if not last:
            total = ends[0]
        span *= 2
    while len(local) < len(sizes):
        carry = next_local(carry, carry)
    weight = parts[1]

    mixed = mix_call(0, [CHUNK], q[:1], local[:1], residue_table, flat_rates, state, carry)
    mixed += mix_call(
        CHUNK, [CHUNK] * (chunks - 1), q[1:], local[1:], residue_table, flat_rates, state, mixed[0]
    )
    other = [swap(x, 1) for x in mixed]
    arrived = []
    after = mixed[-1]
    for c in range(chunks):
        waits = [after] + (arrived[:1] if c == chunks - 1 else [])
        after = project_call(0, [(0, CHUNK)], [mixed[c]], [other[c]], weight, weight_pair, waits, BF16)
        arrived.append(swap(after, 2))
    here = project_call(
        channels, [(0, CHUNK)] * chunks, mixed, other, weight, weight_pair, [after], F32
    )
    out = None
    for c in range(chunks):
        out = add_call(c, here, [arrived[c]], out)
    return out


def solution(mesh):
    n_ctx, n_tp = mesh.shape["ctx"], mesh.shape["tp"]
    in_specs = (
        P("ctx", "tp"),
        P("ctx", "tp"),
        P("ctx", "tp"),
        P("tp", None),
        P("tp", None),
        P("tp"),
        P("tp", None),
    )

    def body(*args):
        return shards(*args, n_ctx=n_ctx, n_tp=n_tp)

    return jax.shard_map(body, mesh=mesh, in_specs=in_specs, out_specs=P("ctx", "tp"), check_vma=False)
```

time: 54 us -> 48.6 us (0.900)
  Pallas kernels: 22 us -> 19.8 us
  local copies, waits for them, and re-layouts: 2.09 us -> 0 us
  starting transfers between devices: 16.3 us -> 14.5 us
  waiting for transfers between devices: 13.1 us -> 14 us
    pallas_call x18 -> x14, Pallas kernels: 19 us -> 16.8 us  [the longest x3 7.68 us: local_call(): pl.pallas_call(lambda *refs: local_kernel(begin, count, modes, parts, sta...]
    unnamed x8 -> x0, local copies, waits for them, and re-layouts: 2.09 us -> none
    ppermute x3, starting transfers between devices: 9.13 us -> 7.87 us  [shards(): other = lax.ppermute(total, 'ctx', [(i, i ^ span) for i in range(n_ctx)])]
    ppermute x10 -> x9, starting transfers between devices: 7.18 us -> 6.6 us  [swap(): return lax.ppermute(x, 'tp', [(i, i ^ bit) for i in range(n_tp)])]
    ppermute x10 -> x9, waiting for transfers between devices: 12.5 us -> 13 us  [swap(): return lax.ppermute(x, 'tp', [(i, i ^ bit) for i in range(n_tp)])]
  transfers between devices with their start and end apart: 13 -> 12, of which waited for: 6 -> 5; matrix products, arithmetic and copies ran while one was open for 0% -> 0% of each run, Pallas kernels for 34% -> 34%
where the time goes in v4:
time: 48.6 us; the launch traced here: 48.4 us
  Pallas kernels  19.8 us (41%)
  starting transfers between devices  14.5 us (30%)
  waiting for transfers between devices  14 us (29%)
    ppermute x9, waiting for transfers between devices, swap(): return lax.ppermute(x, 'tp', [(i, i ^ bit) for i in range(n_tp)])  13 us
    ppermute x3, starting transfers between devices, shards(): other = lax.ppermute(total, 'ctx', [(i, i ^ span) for i in range(n_ctx)])  7.87 us
    pallas_call x3, Pallas kernels, local_call(): pl.pallas_call(lambda *refs: local_kernel(begin, count, modes, parts, sta...  7.68 us
    ppermute x9, starting transfers between devices, swap(): return lax.ppermute(x, 'tp', [(i, i ^ bit) for i in range(n_tp)])  6.6 us
    pallas_call x5, Pallas kernels, project_call(): pl.pallas_call(lambda *refs: project_kernel(row, pieces, *refs), in_specs...  5.32 us
    pallas_call x4, Pallas kernels, add_call(): pl.pallas_call(add_kernel, grid=(1,), in_specs=[pl.BlockSpec((CHUNK, widt...  2.99 us
    pallas_call x1, Pallas kernels, summary_call(): pl.pallas_call(summary_kernel, in_specs=[HBM_SPEC] * 5, out_specs=[VMEM_S...  2.31 us
    pallas_call x2, Pallas kernels, mix_call(): pl.pallas_call(lambda *refs: mix_kernel(begin, modes, len(sizes), *refs),...  1.37 us
  transfers between devices with their start and end apart: 12, of which 5 were waited for; matrix products, arithmetic and copies ran while one was open for 0% of the time, Pallas kernels for 34%

profile of v4, /device:TPU:0, one launch (start us, length us, event | category | flops | bytes accessed | tf_op | source)
XLA Modules:
  0.0 48.4 jit_solution(5771549205536710548)
XLA Ops:
  0.0 2.3 %block_summary.1 = (f32[128,128]{1,0:T(8,128)S(1)}, f32[128,128]{1,0:T(8,128)S(1)}, f32[128,128]{1,0:T(8,128)S(1)}, f32[1,1024]{1,0:T(1,128)S(1)}, bf16[512,1024]{1,0:T(8,128)(2,1)S(1)}, /*index=5*/f32[8,128]{1,0:T(8,128)S(1)}) custom-call(bf16[512,1024]{1,0:T(8,128)(2,1)} %k_hbm.1, bf16[512,1024]{1,0:T(8,128)(2,1)} %v_hbm.1, f32[16,64]{1,0:T(8,128)} %bitcast.3, ...), custom_call_target="tpu_custom_call" | custom-call | flops 1 | bytes 1 | tf_op jit(solution)/shard_map/block_summary/pallas_call | solution.py:138
  2.3 3.0 %collective-permute-start = (f32[128,128]{1,0:T(8,128)S(1)}, f32[128,128]{1,0:T(8,128)S(1)}, u32[]{:S(2)}, u32[]{:S(2)}) collective-permute-start(f32[128,128]{1,0:T(8,128)S(1)} %get-tuple-element.37.refs_6_.refs_3_), channel_id=1, source_target_pairs={{0,4},{4,0},{8,12},{12,8},{16,20},{20,16},{24,28},{28,24},{1,5},{5... | collective-permute-start | bytes 196616 | tf_op jit(solution)/shard_map/ppermute | solution.py:413
  5.3 2.4 %local_conv.3 = (f32[1024,128]{1,0:T(8,128)S(1)}, f32[128,128]{1,0:T(8,128)S(1)}, bf16[128,1024]{1,0:T(8,128)(2,1)S(1)}, bf16[2048,1024]{1,0:T(8,128)(2,1)S(1)}) custom-call(bf16[512,1024]{1,0:T(8,128)(2,1)S(1)} %get-tuple-element.33.refs_0_, f32[128,128]{1,0:T(8,128)S(1)} %get-tuple-element.34.refs_1_, f32[128,128]{1,0:T(8,128)S(1)} %get-tuple-element.35.refs_2_.refs_0_, ...), custom_call_target="tpu_custom_call" | custom-call | flops 1 | bytes 1 | tf_op jit(solution)/shard_map/local_conv/pallas_call | solution.py:218
  7.7 0.0 collective-permute-done.refs_2_
  7.7 0.1 collective-permute-start.1
  7.8 2.0 %collective-permute-start.2 = (f32[128,128]{1,0:T(8,128)S(1)}, f32[128,128]{1,0:T(8,128)S(1)}, u32[]{:S(2)}, u32[]{:S(2)}) collective-permute-start(f32[128,128]{1,0:T(8,128)S(1)} %get-tuple-element.39.refs_6_.refs_3_), channel_id=1, source_target_pairs={{0,8},{4,12},{8,0},{12,4},{16,24},{20,28},{24,16},{28,20},{1,9},{5... | collective-permute-start | bytes 196616 | tf_op jit(solution)/shard_map/ppermute | solution.py:413
  9.9 2.7 %local_conv.4 = (f32[1536,128]{1,0:T(8,128)S(1)}, f32[128,128]{1,0:T(8,128)S(1)}, bf16[192,1024]{1,0:T(8,128)(2,1)S(1)}, bf16[2048,1024]{1,0:T(8,128)(2,1)S(1)}) custom-call(bf16[512,1024]{1,0:T(8,128)(2,1)S(1)} %get-tuple-element.33.refs_0_, f32[128,128]{1,0:T(8,128)S(1)} %get-tuple-element.34.refs_1_, f32[128,128]{1,0:T(8,128)S(1)} %get-tuple-element.35.refs_2_.refs_0_, ...), custom_call_target="tpu_custom_call" | custom-call | flops 1 | bytes 1 | tf_op jit(solution)/shard_map/local_conv/pallas_call | solution.py:218
  12.5 0.0 collective-permute-done.2.refs_2_
  12.6 2.8 %collective-permute-start.3 = (f32[128,128]{1,0:T(8,128)S(1)}, f32[128,128]{1,0:T(8,128)S(1)}, u32[]{:S(2)}, u32[]{:S(2)}) collective-permute-start(f32[128,128]{1,0:T(8,128)S(1)} %get-tuple-element.46.refs_6_.refs_3_), channel_id=1, source_target_pairs={{0,16},{4,20},{8,24},{12,28},{16,0},{20,4},{24,8},{28,12},{1,17},{... | collective-permute-start | bytes 196616 | tf_op jit(solution)/shard_map/ppermute | solution.py:413
  15.4 2.7 %local_conv.5 = (f32[1536,128]{1,0:T(8,128)S(1)}, f32[128,128]{1,0:T(8,128)S(1)}, bf16[192,1024]{1,0:T(8,128)(2,1)S(1)}) custom-call(bf16[512,1024]{1,0:T(8,128)(2,1)S(1)} %get-tuple-element.33.refs_0_, f32[128,128]{1,0:T(8,128)S(1)} %get-tuple-element.34.refs_1_, f32[128,128]{1,0:T(8,128)S(1)} %get-tuple-element.35.refs_2_.refs_0_, ...), custom_call_target="tpu_custom_call" | custom-call | flops 1 | bytes 1 | tf_op jit(solution)/shard_map/local_conv/pallas_call | solution.py:218
  18.1 1.0 %collective-permute-done.3.refs_2_ = f32[128,128]{1,0:T(8,128)S(1)} collective-permute-done((f32[128,128]{1,0:T(8,128)S(1)}, f32[128,128]{1,0:T(8,128)S(1)}, u32[]{:S(2)}, u32[]{:S(2)}) %collective-permute-start.3) | collective-permute-done | bytes 65568 | tf_op jit(solution)/shard_map/ppermute | solution.py:413
  19.2 0.5 mix.2.refs_3_.refs_2_
  19.6 0.1 collective-permute-start.4
  19.7 0.9 %mix.3 = (bf16[128,1024]{1,0:T(8,128)(2,1)S(1)}, bf16[128,1024]{1,0:T(8,128)(2,1)S(1)}, bf16[128,1024]{1,0:T(8,128)(2,1)S(1)}) custom-call(f32[128,128]{1,0:T(8,128)S(1)} %get-tuple-element.35.refs_2_.refs_0_, f32[1,1024]{1,0:T(1,128)S(1)} %get-tuple-element.43.refs_1_, f32[128,128]{1,0:T(8,128)S(1)} %get-tuple-element.50.refs_2_, ...), custom_call_target="tpu_custom_call" | custom-call | flops 1 | bytes 1 | tf_op jit(solution)/shard_map/mix/pallas_call | solution.py:315
  20.6 0.6 %collective-permute-start.5 = (bf16[128,1024]{1,0:T(8,128)(2,1)S(1)}, bf16[128,1024]{1,0:T(8,128)(2,1)S(1)}, u32[]{:S(2)}, u32[]{:S(2)}) collective-permute-start(bf16[128,1024]{1,0:T(8,128)(2,1)S(1)} %get-tuple-element.58.refs_2_.refs_3_), channel_id=1, source_target_pairs={{0,1},{1,0},{2,3},{3,2},{4,5},{5,4},{6,7},{7,6},{8,9},{9,8},{10,11... | collective-permute-start | bytes 786440 | tf_op jit(solution)/shard_map/ppermute | solution.py:389
  21.2 0.1 collective-permute-start.6
  21.3 0.4 collective-permute-start.7
  21.7 0.0 collective-permute-done.4.refs_3_.refs_6_
  21.7 0.0 collective-permute-done.1.refs_1_
  21.7 0.7 %project.5.refs_4_ = bf16[128,1024]{1,0:T(8,128)(2,1)S(1)} custom-call(bf16[2048,1024]{1,0:T(8,128)(2,1)S(1)} %get-tuple-element.41.refs_0_, bf16[2048,1024]{1,0:T(8,128)(2,1)S(1)} %collective-permute-done.1.refs_1_, bf16[128,1024]{1,0:T(8,128)(2,1)S(1)} %mix.2.refs_3_.refs_2_, bf16[128,1024]{1,0:T(8,128)(2,1)S(1)} %collective-permute-done.4.refs_3_.refs_6_, ...), custom_call_target="tpu_custom_call" | custom-call | flops 1 | bytes 1 | tf_op jit(solution)/shard_map/project/pallas_call | solution.py:343
  22.4 1.6 %collective-permute-start.8 = (bf16[128,1024]{1,0:T(8,128)(2,1)S(1)}, bf16[128,1024]{1,0:T(8,128)(2,1)S(1)}, u32[]{:S(2)}, u32[]{:S(2)}) collective-permute-start(bf16[128,1024]{1,0:T(8,128)(2,1)S(1)} %project.5.refs_4_), channel_id=1, source_target_pairs={{0,2},{1,3},{2,0},{3,1},{4,6},{5,7},{6,4},{7,5},{8,10},{9,11},{10,... | collective-permute-start | bytes 786440 | tf_op jit(solution)/shard_map/ppermute | solution.py:389
  24.0 0.0 collective-permute-done.5.refs_3_.refs_7_
  24.1 0.7 %project.6.refs_4_ = bf16[128,1024]{1,0:T(8,128)(2,1)S(1)} custom-call(bf16[2048,1024]{1,0:T(8,128)(2,1)S(1)} %get-tuple-element.41.refs_0_, bf16[2048,1024]{1,0:T(8,128)(2,1)S(1)} %collective-permute-done.1.refs_1_, bf16[128,1024]{1,0:T(8,128)(2,1)S(1)} %get-tuple-element.58.refs_2_.refs_3_, bf16[128,1024]{1,0:T(8,128)(2,1)S(1)} %collective-permute-done.5.refs_3_.refs_7_, ...), custom_call_target="tpu_custom_call" | custom-call | flops 1 | bytes 1 | tf_op jit(solution)/shard_map/project/pallas_call | solution.py:343
  24.8 0.5 %collective-permute-start.11 = (bf16[128,1024]{1,0:T(8,128)(2,1)S(1)}, bf16[128,1024]{1,0:T(8,128)(2,1)S(1)}, u32[]{:S(2)}, u32[]{:S(2)}) collective-permute-start(bf16[128,1024]{1,0:T(8,128)(2,1)S(1)} %project.6.refs_4_), channel_id=1, source_target_pairs={{0,2},{1,3},{2,0},{3,1},{4,6},{5,7},{6,4},{7,5},{8,10},{9,11},{10,... | collective-permute-start | bytes 786440 | tf_op jit(solution)/shard_map/ppermute | solution.py:389
  25.3 0.0 collective-permute-done.6.refs_3_.refs_8_
  25.3 0.7 %project.7.refs_4_ = bf16[128,1024]{1,0:T(8,128)(2,1)S(1)} custom-call(bf16[2048,1024]{1,0:T(8,128)(2,1)S(1)} %get-tuple-element.41.refs_0_, bf16[2048,1024]{1,0:T(8,128)(2,1)S(1)} %collective-permute-done.1.refs_1_, bf16[128,1024]{1,0:T(8,128)(2,1)S(1)} %get-tuple-element.59.refs_2_.refs_4_, bf16[128,1024]{1,0:T(8,128)(2,1)S(1)} %collective-permute-done.6.refs_3_.refs_8_, ...), custom_call_target="tpu_custom_call" | custom-call | flops 1 | bytes 1 | tf_op jit(solution)/shard_map/project/pallas_call | solution.py:343
  26.1 1.6 %collective-permute-start.10 = (bf16[128,1024]{1,0:T(8,128)(2,1)S(1)}, bf16[128,1024]{1,0:T(8,128)(2,1)S(1)}, u32[]{:S(2)}, u32[]{:S(2)}) collective-permute-start(bf16[128,1024]{1,0:T(8,128)(2,1)S(1)} %project.7.refs_4_), channel_id=1, source_target_pairs={{0,2},{1,3},{2,0},{3,1},{4,6},{5,7},{6,4},{7,5},{8,10},{9,11},{10,... | collective-permute-start | bytes 786440 | tf_op jit(solution)/shard_map/ppermute | solution.py:389
  27.7 0.0 collective-permute-done.7.refs_3_.refs_9_
  27.7 4.0 %collective-permute-done.8.refs_5_.refs_0_ = bf16[128,1024]{1,0:T(8,128)(2,1)S(1)} collective-permute-done((bf16[128,1024]{1,0:T(8,128)(2,1)S(1)}, bf16[128,1024]{1,0:T(8,128)(2,1)S(1)}, u32[]{:S(2)}, u32[]{:S(2)}) %collective-permute-start.8) | collective-permute-done | bytes 262176 | tf_op jit(solution)/shard_map/ppermute | solution.py:389
  31.7 0.7 %project.8.refs_10_ = bf16[128,1024]{1,0:T(8,128)(2,1)S(1)} custom-call(bf16[2048,1024]{1,0:T(8,128)(2,1)S(1)} %get-tuple-element.41.refs_0_, bf16[2048,1024]{1,0:T(8,128)(2,1)S(1)} %collective-permute-done.1.refs_1_, bf16[128,1024]{1,0:T(8,128)(2,1)S(1)} %get-tuple-element.60.refs_4_.refs_2_.refs_5_, ...), custom_call_target="tpu_custom_call" | custom-call | flops 1 | bytes 1 | tf_op jit(solution)/shard_map/project/pallas_call | solution.py:343
  32.4 1.6 %collective-permute-start.9 = (bf16[128,1024]{1,0:T(8,128)(2,1)S(1)}, bf16[128,1024]{1,0:T(8,128)(2,1)S(1)}, u32[]{:S(2)}, u32[]{:S(2)}) collective-permute-start(bf16[128,1024]{1,0:T(8,128)(2,1)S(1)} %project.8.refs_10_), channel_id=1, source_target_pairs={{0,2},{1,3},{2,0},{3,1},{4,6},{5,7},{6,4},{7,5},{8,10},{9,11},{10,... | collective-permute-start | bytes 786440 | tf_op jit(solution)/shard_map/ppermute | solution.py:389
  34.0 2.4 %project.9.near_ref = f32[512,1024]{1,0:T(8,128)S(1)} custom-call(bf16[2048,1024]{1,0:T(8,128)(2,1)S(1)} %get-tuple-element.41.refs_0_, bf16[2048,1024]{1,0:T(8,128)(2,1)S(1)} %collective-permute-done.1.refs_1_, bf16[128,1024]{1,0:T(8,128)(2,1)S(1)} %mix.2.refs_3_.refs_2_, bf16[128,1024]{1,0:T(8,128)(2,1)S(1)} %get-tuple-element.58.refs_2_.refs_3_, ...), custom_call_target="tpu_custom_call" | custom-call | flops 1 | bytes 1 | tf_op jit(solution)/shard_map/project/pallas_call | solution.py:343
  36.4 0.8 %add_arrived.4.refs_1_ = bf16[512,1024]{1,0:T(8,128)(2,1)} custom-call(f32[512,1024]{1,0:T(8,128)S(1)} %project.9.near_ref, bf16[128,1024]{1,0:T(8,128)(2,1)S(1)} %collective-permute-done.8.refs_5_.refs_0_), custom_call_target="tpu_custom_call" | custom-call | flops 1 | bytes 1 | tf_op jit(solution)/shard_map/add_arrived/pallas_call | solution.py:368
  37.2 0.1 collective-permute-done.11.refs_0_
  37.3 0.7 %add_arrived.5.refs_1_ = bf16[512,1024]{1,0:T(8,128)(2,1)} custom-call(f32[512,1024]{1,0:T(8,128)S(1)} %project.9.near_ref, bf16[128,1024]{1,0:T(8,128)(2,1)S(1)} %collective-permute-done.11.refs_0_, bf16[512,1024]{1,0:T(8,128)(2,1)} %add_arrived.4.refs_1_), custom_call_target="tpu_custom_call", output_to_operand_aliasing={{}: (2, {})} | custom-call | flops 1 | bytes 1 | tf_op jit(solution)/shard_map/add_arrived/pallas_call | solution.py:368
  38.0 4.9 %collective-permute-done.10.refs_0_ = bf16[128,1024]{1,0:T(8,128)(2,1)S(1)} collective-permute-done((bf16[128,1024]{1,0:T(8,128)(2,1)S(1)}, bf16[128,1024]{1,0:T(8,128)(2,1)S(1)}, u32[]{:S(2)}, u32[]{:S(2)}) %collective-permute-start.10) | collective-permute-done | bytes 262176 | tf_op jit(solution)/shard_map/ppermute | solution.py:389
  42.9 0.7 %add_arrived.6.refs_1_ = bf16[512,1024]{1,0:T(8,128)(2,1)} custom-call(f32[512,1024]{1,0:T(8,128)S(1)} %project.9.near_ref, bf16[128,1024]{1,0:T(8,128)(2,1)S(1)} %collective-permute-done.10.refs_0_, bf16[512,1024]{1,0:T(8,128)(2,1)} %add_arrived.5.refs_1_), custom_call_target="tpu_custom_call", output_to_operand_aliasing={{}: (2, {})} | custom-call | flops 1 | bytes 1 | tf_op jit(solution)/shard_map/add_arrived/pallas_call | solution.py:368
  43.7 4.0 %collective-permute-done.9.refs_0_ = bf16[128,1024]{1,0:T(8,128)(2,1)S(1)} collective-permute-done((bf16[128,1024]{1,0:T(8,128)(2,1)S(1)}, bf16[128,1024]{1,0:T(8,128)(2,1)S(1)}, u32[]{:S(2)}, u32[]{:S(2)}) %collective-permute-start.9) | collective-permute-done | bytes 262176 | tf_op jit(solution)/shard_map/ppermute | solution.py:389
  47.6 0.7 %add_arrived.7 = bf16[512,1024]{1,0:T(8,128)(2,1)} custom-call(f32[512,1024]{1,0:T(8,128)S(1)} %project.9.near_ref, bf16[128,1024]{1,0:T(8,128)(2,1)S(1)} %collective-permute-done.9.refs_0_, bf16[512,1024]{1,0:T(8,128)(2,1)} %add_arrived.6.refs_1_), custom_call_target="tpu_custom_call", output_to_operand_aliasing={{}: (2, {})} | custom-call | flops 1 | bytes 1 | tf_op jit(solution)/shard_map/add_arrived/pallas_call | solution.py:368
  (3 shorter events, 0.1 us)
Async XLA Ops:
  2.3 5.4 %collective-permute-start = (f32[128,128]{1,0:T(8,128)S(1)}, f32[128,128]{1,0:T(8,128)S(1)}, u32[]{:S(2)}, u32[]{:S(2)}) collective-permute-start(f32[128,128]{1,0:T(8,128)S(1)} %get-tuple-element.37.refs_6_.refs_3_), channel_id=1, source_target_pairs={{0,4},{4,0},{8,12},{12,8},{16,20},{20,16},{24,28},{28,24},{1,5},{5... | collective-permute-start | bytes 196616 | tf_op jit(solution)/shard_map/ppermute | solution.py:413
  7.7 13.9 %collective-permute-start.1 = (bf16[2048,1024]{1,0:T(8,128)(2,1)S(1)}, bf16[2048,1024]{1,0:T(8,128)(2,1)S(1)}, u32[]{:S(2)}, u32[]{:S(2)}) collective-permute-start(bf16[2048,1024]{1,0:T(8,128)(2,1)S(1)} %get-tuple-element.42), channel_id=1, source_target_pairs={{0,1},{1,0},{2,3},{3,2},{4,5},{5,4},{6,7},{7,6},{8,9},{9,8},{10,11... | collective-permute-start | bytes 12582920 | tf_op jit(solution)/shard_map/ppermute | solution.py:389
  7.8 4.7 %collective-permute-start.2 = (f32[128,128]{1,0:T(8,128)S(1)}, f32[128,128]{1,0:T(8,128)S(1)}, u32[]{:S(2)}, u32[]{:S(2)}) collective-permute-start(f32[128,128]{1,0:T(8,128)S(1)} %get-tuple-element.39.refs_6_.refs_3_), channel_id=1, source_target_pairs={{0,8},{4,12},{8,0},{12,4},{16,24},{20,28},{24,16},{28,20},{1,9},{5... | collective-permute-start | bytes 196616 | tf_op jit(solution)/shard_map/ppermute | solution.py:413
  12.6 6.5 %collective-permute-start.3 = (f32[128,128]{1,0:T(8,128)S(1)}, f32[128,128]{1,0:T(8,128)S(1)}, u32[]{:S(2)}, u32[]{:S(2)}) collective-permute-start(f32[128,128]{1,0:T(8,128)S(1)} %get-tuple-element.46.refs_6_.refs_3_), channel_id=1, source_target_pairs={{0,16},{4,20},{8,24},{12,28},{16,0},{20,4},{24,8},{28,12},{1,17},{... | collective-permute-start | bytes 196616 | tf_op jit(solution)/shard_map/ppermute | solution.py:413
  19.6 2.1 %collective-permute-start.4 = (bf16[128,1024]{1,0:T(8,128)(2,1)S(1)}, bf16[128,1024]{1,0:T(8,128)(2,1)S(1)}, u32[]{:S(2)}, u32[]{:S(2)}) collective-permute-start(bf16[128,1024]{1,0:T(8,128)(2,1)S(1)} %mix.2.refs_3_.refs_2_), channel_id=1, source_target_pairs={{0,1},{1,0},{2,3},{3,2},{4,5},{5,4},{6,7},{7,6},{8,9},{9,8},{10,11... | collective-permute-start | bytes 786440 | tf_op jit(solution)/shard_map/ppermute | solution.py:389
  20.6 3.4 %collective-permute-start.5 = (bf16[128,1024]{1,0:T(8,128)(2,1)S(1)}, bf16[128,1024]{1,0:T(8,128)(2,1)S(1)}, u32[]{:S(2)}, u32[]{:S(2)}) collective-permute-start(bf16[128,1024]{1,0:T(8,128)(2,1)S(1)} %get-tuple-element.58.refs_2_.refs_3_), channel_id=1, source_target_pairs={{0,1},{1,0},{2,3},{3,2},{4,5},{5,4},{6,7},{7,6},{8,9},{9,8},{10,11... | collective-permute-start | bytes 786440 | tf_op jit(solution)/shard_map/ppermute | solution.py:389
  21.2 4.2 %collective-permute-start.6 = (bf16[128,1024]{1,0:T(8,128)(2,1)S(1)}, bf16[128,1024]{1,0:T(8,128)(2,1)S(1)}, u32[]{:S(2)}, u32[]{:S(2)}) collective-permute-start(bf16[128,1024]{1,0:T(8,128)(2,1)S(1)} %get-tuple-element.59.refs_2_.refs_4_), channel_id=1, source_target_pairs={{0,1},{1,0},{2,3},{3,2},{4,5},{5,4},{6,7},{7,6},{8,9},{9,8},{10,11... | collective-permute-start | bytes 786440 | tf_op jit(solution)/shard_map/ppermute | solution.py:389
  21.3 6.5 %collective-permute-start.7 = (bf16[128,1024]{1,0:T(8,128)(2,1)S(1)}, bf16[128,1024]{1,0:T(8,128)(2,1)S(1)}, u32[]{:S(2)}, u32[]{:S(2)}) collective-permute-start(bf16[128,1024]{1,0:T(8,128)(2,1)S(1)} %get-tuple-element.60.refs_4_.refs_2_.refs_5_), channel_id=1, source_target_pairs={{0,1},{1,0},{2,3},{3,2},{4,5},{5,4},{6,7},{7,6},{8,9},{9,8},{10,11... | collective-permute-start | bytes 786440 | tf_op jit(solution)/shard_map/ppermute | solution.py:389
  22.4 9.2 %collective-permute-start.8 = (bf16[128,1024]{1,0:T(8,128)(2,1)S(1)}, bf16[128,1024]{1,0:T(8,128)(2,1)S(1)}, u32[]{:S(2)}, u32[]{:S(2)}) collective-permute-start(bf16[128,1024]{1,0:T(8,128)(2,1)S(1)} %project.5.refs_4_), channel_id=1, source_target_pairs={{0,2},{1,3},{2,0},{3,1},{4,6},{5,7},{6,4},{7,5},{8,10},{9,11},{10,... | collective-permute-start | bytes 786440 | tf_op jit(solution)/shard_map/ppermute | solution.py:389
  24.8 12.5 %collective-permute-start.11 = (bf16[128,1024]{1,0:T(8,128)(2,1)S(1)}, bf16[128,1024]{1,0:T(8,128)(2,1)S(1)}, u32[]{:S(2)}, u32[]{:S(2)}) collective-permute-start(bf16[128,1024]{1,0:T(8,128)(2,1)S(1)} %project.6.refs_4_), channel_id=1, source_target_pairs={{0,2},{1,3},{2,0},{3,1},{4,6},{5,7},{6,4},{7,5},{8,10},{9,11},{10,... | collective-permute-start | bytes 786440 | tf_op jit(solution)/shard_map/ppermute | solution.py:389
  26.1 16.8 %collective-permute-start.10 = (bf16[128,1024]{1,0:T(8,128)(2,1)S(1)}, bf16[128,1024]{1,0:T(8,128)(2,1)S(1)}, u32[]{:S(2)}, u32[]{:S(2)}) collective-permute-start(bf16[128,1024]{1,0:T(8,128)(2,1)S(1)} %project.7.refs_4_), channel_id=1, source_target_pairs={{0,2},{1,3},{2,0},{3,1},{4,6},{5,7},{6,4},{7,5},{8,10},{9,11},{10,... | collective-permute-start | bytes 786440 | tf_op jit(solution)/shard_map/ppermute | solution.py:389
  32.4 15.2 %collective-permute-start.9 = (bf16[128,1024]{1,0:T(8,128)(2,1)S(1)}, bf16[128,1024]{1,0:T(8,128)(2,1)S(1)}, u32[]{:S(2)}, u32[]{:S(2)}) collective-permute-start(bf16[128,1024]{1,0:T(8,128)(2,1)S(1)} %project.8.refs_10_), channel_id=1, source_target_pairs={{0,2},{1,3},{2,0},{3,1},{4,6},{5,7},{6,4},{7,5},{8,10},{9,11},{10,... | collective-permute-start | bytes 786440 | tf_op jit(solution)/shard_map/ppermute | solution.py:389
